TPU v7x, 32 devices: a whole 2x2x4 slice. The times are simulated.
32 devices in a mesh: dp: 4 (over z), section: 4 (over y, x), tensor: 2 (over core).
Axes of the slice: x: 2, y: 2, z: 4, core: 2. Of those that a mesh axis runs over, the one named last changes fastest.
Arguments:
- inputs: float32 [12, 256, 768], P('dp', 'tensor', 'section'), may hold values from -6 to 6
- counts: int32 [12], P('dp'), may hold values from 2 to 4, as said below
- w_query: bfloat16 [2, 768, 768], P(None, None, 'tensor'), may hold values from -0.21875 to 0.21875
- w_key: bfloat16 [2, 768, 768], P(None, None, 'tensor'), may hold values from -0.21875 to 0.21875
- w_value: bfloat16 [2, 768, 768], P(None, None, 'tensor'), may hold values from -0.21875 to 0.21875
- w_out: bfloat16 [2, 768, 768], P(None, None, 'tensor'), may hold values from -0.875 to 0.875
- w_up: bfloat16 [2, 768, 3072], P(None, None, 'tensor'), may hold values from -0.21875 to 0.21875
- w_down: bfloat16 [2, 768, 3072], P(None, None, 'tensor'), may hold values from -0.109375 to 0.109375
- gain_one: float32 [2, 768], replicated, may hold values from 0.5 to 1.5
- bias_one: float32 [2, 768], replicated, may hold values from -1.25 to 1.25
- gain_two: float32 [2, 768], replicated, may hold values from 0.5 to 1.5
- bias_two: float32 [2, 768], replicated, may hold values from -1.25 to 1.25
- pass_embed: float32 [4, 768], replicated, may hold values from -3 to 3
- cotangent: float32 [4, 12, 256, 768], P('section', 'dp', 'tensor'), may hold values from -6 to 6
Outputs:
- passes: float32 [4, 12, 256, 768], P('section', 'dp', 'tensor')
- grad_inputs: float32 [12, 256, 768], P('dp', 'tensor', 'section')
- grad_w_query: float32 [2, 768, 768], P(None, None, 'tensor')
- grad_w_key: float32 [2, 768, 768], P(None, None, 'tensor')
- grad_w_value: float32 [2, 768, 768], P(None, None, 'tensor')
- grad_w_out: float32 [2, 768, 768], P(None, None, 'tensor')
- grad_w_up: float32 [2, 768, 3072], P(None, None, 'tensor')
- grad_w_down: float32 [2, 768, 3072], P(None, None, 'tensor')
- grad_gain_one: float32 [2, 768], replicated
- grad_bias_one: float32 [2, 768], replicated
- grad_gain_two: float32 [2, 768], replicated
- grad_bias_two: float32 [2, 768], replicated
- grad_pass_embed: float32 [4, 768], replicated
Inputs may be any that keep to these rules, and one draw needn't show every extreme that they name: `counts`: each item's number of passes; among the 3 items of each index of dp at least one has 4 passes.
All inputs are finite; a program needn't handle non-finite values.
Results may differ from a plain program's by a relative error of at most 0.015.
Values may be sent and summed in bfloat16 or wider, within the bound.
No kernel may reach another device: no remote copies, remote signals or barrier semaphores. Data moves between devices by JAX's collectives and lax.ppermute only.
A program may use at most 192 MiB of HBM per device.

v0:
```python
import jax
import jax.numpy as jnp
from jax import lax
from jax.sharding import PartitionSpec as P

HEADS = 12


EPSILON = 1e-05
MASKED = -1e30


def shifted(value, axis, steps):
    count = lax.axis_size(axis)
    initial, last = (max(0, -steps), min(count, count - steps))
    return lax.ppermute(value, axis, [(source, source + steps) for source in range(initial, last)])


def layer_norm(source, gain_row, bias_row):
    average = jnp.mean(source, axis=-1, keepdims=True)
    centred = source - average
    spread = jnp.mean(centred * centred, axis=-1, keepdims=True)
    return centred * lax.rsqrt(spread + EPSILON) * gain_row + bias_row


def gelu_tanh(source):
    return jax.nn.gelu(source, approximate=True)


def dot_rows(left_side, right_side):
    return lax.dot_general(
        left_side, right_side, (((0,), (0,)), ((), ())), preferred_element_type=jnp.float32
    )


def collect_rows(local_rows):
    return lax.all_gather(local_rows, "tensor", axis=0, tiled=True)


def reduce_rows(pairings):
    summed = None
    for left_side, right_side in pairings:
        partial_sum = lax.dot_general(
            left_side, right_side, (((1,), (1,)), ((), ())), preferred_element_type=jnp.float32
        )
        summed = partial_sum if summed is None else summed + partial_sum
    return lax.psum_scatter(summed, "tensor", scatter_dimension=0, tiled=True)


def visible_mask(row_count, slot_count, pass_slot):
    key_index = jnp.arange(slot_count * row_count)
    key_slot = key_index // row_count
    key_place = key_index % row_count
    position = jnp.arange(row_count)
    return (key_place[None, :] <= position[:, None]) & (key_slot[None, :] <= pass_slot)


def split_heads(queries, cache, head_count):
    row_count, width = queries.shape
    slot_count = cache.shape[0]
    head_size = width // head_count
    key_heads = cache[:, :, :width].reshape(slot_count * row_count, head_count, head_size)
    value_heads = cache[:, :, width:].reshape(slot_count * row_count, head_count, head_size)
    query_heads = queries.reshape(row_count, head_count, head_size)
    return (query_heads, key_heads, value_heads, head_size ** (-0.5))


def masked_scores(query_heads, key_heads, scaling, pass_slot, slot_count):
    row_count = query_heads.shape[0]
    scores = (
        jnp.einsum("thd,khd->htk", query_heads, key_heads, preferred_element_type=jnp.float32)
        * scaling
    )
    allowed = visible_mask(row_count, slot_count, pass_slot)
    return jnp.where(allowed[None], scores, MASKED)


def attend_forward(queries, cache, pass_slot, head_count):
    row_count, width = queries.shape
    query_heads, key_heads, value_heads, scaling = split_heads(queries, cache, head_count)
    scores = masked_scores(query_heads, key_heads, scaling, pass_slot, cache.shape[0])
    highest = jnp.max(scores, axis=-1, keepdims=True)
    powers = jnp.exp(scores - highest)
    totals = jnp.sum(powers, axis=-1, keepdims=True)
    weights = (powers / totals).astype(jnp.bfloat16)
    logsum = highest + jnp.log(totals)
    mixed_heads = jnp.einsum(
        "htk,khd->thd", weights, value_heads, preferred_element_type=jnp.float32
    )
    return (mixed_heads.reshape(row_count, width).astype(jnp.bfloat16), logsum)


def attend_backward(queries, cache, pass_slot, logsum, grad_mixed, head_count):
    row_count, width = queries.shape
    slot_count = cache.shape[0]
    query_heads, key_heads, value_heads, scaling = split_heads(queries, cache, head_count)
    scores = masked_scores(query_heads, key_heads, scaling, pass_slot, slot_count)
    exact = jnp.exp(scores - logsum)
    rounded = exact.astype(jnp.bfloat16)
    grad_heads = grad_mixed.reshape(row_count, head_count, width // head_count)
    grad_weights = jnp.einsum(
        "thd,khd->htk", grad_heads, value_heads, preferred_element_type=jnp.float32
    )
    delta_rows = jnp.sum(grad_weights * exact, axis=-1, keepdims=True)
    grad_scores = (exact * (grad_weights - delta_rows)).astype(jnp.bfloat16)
    grad_query_heads = (
        jnp.einsum("htk,khd->thd", grad_scores, key_heads, preferred_element_type=jnp.float32)
        * scaling
    )
    grad_key_heads = (
        jnp.einsum("htk,thd->khd", grad_scores, query_heads, preferred_element_type=jnp.float32)
        * scaling
    )
    grad_value_heads = jnp.einsum(
        "htk,thd->khd", rounded, grad_heads, preferred_element_type=jnp.float32
    )
    grad_cache = jnp.concatenate(
        [
            grad_key_heads.reshape(slot_count, row_count, width),
            grad_value_heads.reshape(slot_count, row_count, width),
        ],
        axis=2,
    )
    return (grad_query_heads.reshape(row_count, width), grad_cache)


def pass_forward(resid_in, cache_in, pass_slot, weights_own, norms_own, embed_own, head_count):
    weight_query, weight_key, weight_value, weight_out, weight_up, weight_down = weights_own
    gain_first, bias_first, gain_second, bias_second = norms_own
    entered = resid_in + embed_own
    normed_all = collect_rows(layer_norm(entered, gain_first, bias_first).astype(jnp.bfloat16))
    queries = jnp.dot(normed_all, weight_query, preferred_element_type=jnp.float32).astype(
        jnp.bfloat16
    )
    key_new = jnp.dot(normed_all, weight_key, preferred_element_type=jnp.float32).astype(
        jnp.bfloat16
    )
    value_new = jnp.dot(normed_all, weight_value, preferred_element_type=jnp.float32).astype(
        jnp.bfloat16
    )
    fresh = jnp.concatenate([key_new, value_new], axis=1)
    cache_new = lax.dynamic_update_index_in_dim(cache_in, fresh, pass_slot, 0)
    mixed_heads, logsum = attend_forward(queries, cache_new, pass_slot, head_count)
    middle = entered + reduce_rows(((mixed_heads, weight_out),))
    normed_two_all = collect_rows(layer_norm(middle, gain_second, bias_second).astype(jnp.bfloat16))
    hidden = jnp.dot(normed_two_all, weight_up, preferred_element_type=jnp.float32)
    active = gelu_tanh(hidden).astype(jnp.bfloat16)
    result = middle + reduce_rows(((active, weight_down),))
    kept = (
        entered,
        normed_all,
        queries,
        cache_new,
        mixed_heads,
        logsum,
        middle,
        normed_two_all,
        hidden,
    )
    return (result, cache_new, kept)


def pass_backward(grad_out, grad_cache_in, kept, pass_slot, weights_own, norms_own, head_count):
    weight_query, weight_key, weight_value, weight_out, weight_up, weight_down = weights_own
    gain_first, bias_first, gain_second, bias_second = norms_own
    entered, normed_all, queries, cache_new, mixed_heads, logsum, middle, normed_two_all, hidden = (
        kept
    )
    width = queries.shape[1]
    grad_down_all = collect_rows(grad_out.astype(jnp.bfloat16))
    active = gelu_tanh(hidden).astype(jnp.bfloat16)
    grad_weight_down = dot_rows(grad_down_all, active)
    grad_active = jnp.dot(grad_down_all, weight_down, preferred_element_type=jnp.float32)
    unused_gelu, gelu_back = jax.vjp(gelu_tanh, hidden)
    grad_hidden = gelu_back(grad_active)[0].astype(jnp.bfloat16)
    grad_weight_up = dot_rows(normed_two_all, grad_hidden)
    grad_normed_two = reduce_rows(((grad_hidden, weight_up),))
    unused_second, norm_back_second = jax.vjp(layer_norm, middle, gain_second, bias_second)
    grad_mid_norm, grad_gain_second, grad_bias_second = norm_back_second(grad_normed_two)
    grad_middle = grad_out + grad_mid_norm
    grad_branch_all = collect_rows(grad_middle.astype(jnp.bfloat16))
    grad_weight_out = dot_rows(grad_branch_all, mixed_heads)
    grad_mixed = jnp.dot(grad_branch_all, weight_out, preferred_element_type=jnp.float32).astype(
        jnp.bfloat16
    )
    grad_queries, grad_cache_own = attend_backward(
        queries, cache_new, pass_slot, logsum, grad_mixed, head_count
    )
    grad_cache = grad_cache_in + grad_cache_own
    grad_fresh = lax.dynamic_index_in_dim(grad_cache, pass_slot, 0, keepdims=False).astype(
        jnp.bfloat16
    )
    grad_key = grad_fresh[:, :width]
    grad_value = grad_fresh[:, width:]
    grad_queries = grad_queries.astype(jnp.bfloat16)
    grad_weight_query = dot_rows(normed_all, grad_queries)
    grad_weight_key = dot_rows(normed_all, grad_key)
    grad_weight_value = dot_rows(normed_all, grad_value)
    grad_normed = reduce_rows(
        ((grad_queries, weight_query), (grad_key, weight_key), (grad_value, weight_value))
    )
    unused_first, norm_back_first = jax.vjp(layer_norm, entered, gain_first, bias_first)
    grad_ent_norm, grad_gain_first, grad_bias_first = norm_back_first(grad_normed)
    grad_entered = grad_middle + grad_ent_norm
    grad_embed = jnp.sum(grad_entered, axis=0)
    slot_ids = jnp.arange(grad_cache.shape[0])
    grad_cache = grad_cache * (slot_ids < pass_slot).astype(jnp.float32)[:, None, None]
    grads = (
        grad_weight_query,
        grad_weight_key,
        grad_weight_value,
        grad_weight_out,
        grad_weight_up,
        grad_weight_down,
        grad_gain_first,
        grad_bias_first,
        grad_gain_second,
        grad_bias_second,
        grad_embed,
    )
    return (grad_entered, grad_cache, grads)


def store_slot(buffer, fresh, batch_clip, valid):
    previous = lax.dynamic_index_in_dim(buffer, batch_clip, 0, keepdims=False)
    chosen = jnp.where(valid, fresh, previous)
    return lax.dynamic_update_index_in_dim(buffer, chosen, batch_clip, 0)


def shards(
    inputs,
    counts,
    w_query,
    w_key,
    w_value,
    w_out,
    w_up,
    w_down,
    gain_one,
    bias_one,
    gain_two,
    bias_two,
    pass_embed,
    cotangent,
):
    section_count = lax.axis_size("section")
    tensor_count = lax.axis_size("tensor")
    section_id = lax.axis_index("section")
    layer_id = jnp.minimum(section_id, 1)
    head_count = HEADS // tensor_count
    batches = counts.shape[0]
    local_rows = cotangent.shape[2]
    width_model = cotangent.shape[3]
    full_rows = local_rows * tensor_count
    width_heads = w_query.shape[2]
    width_hidden = w_up.shape[2]
    slot_total = pass_embed.shape[0]

    def own_layer(stacked):
        return lax.dynamic_index_in_dim(stacked, layer_id, 0, keepdims=False)

    weights_own = (
        own_layer(w_query),
        own_layer(w_key),
        own_layer(w_value),
        own_layer(w_out),
        own_layer(w_up),
        own_layer(w_down),
    )
    norms_own = (own_layer(gain_one), own_layer(bias_one), own_layer(gain_two), own_layer(bias_two))
    embed_own = lax.dynamic_index_in_dim(pass_embed, section_id, 0, keepdims=False)
    entries = lax.all_gather(inputs, "section", axis=2, tiled=True)
    cotangent_own = cotangent[0]
    present = (counts > section_id).astype(jnp.float32)
    steps_total = batches + section_count - 1
    shapes_kept = (
        ((local_rows, width_model), jnp.float32),
        ((full_rows, width_model), jnp.bfloat16),
        ((full_rows, width_heads), jnp.bfloat16),
        ((slot_total, full_rows, 2 * width_heads), jnp.bfloat16),
        ((full_rows, width_heads), jnp.bfloat16),
        ((head_count, full_rows, 1), jnp.float32),
        ((local_rows, width_model), jnp.float32),
        ((full_rows, width_model), jnp.bfloat16),
        ((full_rows, width_hidden), jnp.float32),
        ((local_rows, width_model), jnp.float32),
    )
    buffers_init = tuple(
        (jnp.zeros((batches,) + shape_row, kind) for shape_row, kind in shapes_kept)
    )

    def forward_step(step_id, loop_state):
        resid_recv, cache_recv, buffers = loop_state
        batch_id = step_id - section_id
        valid = (batch_id >= 0) & (batch_id < batches)
        batch_clip = jnp.clip(batch_id, 0, batches - 1)
        first_rows = lax.dynamic_index_in_dim(entries, batch_clip, 0, keepdims=False)
        resid_in = jnp.where(section_id == 0, first_rows, resid_recv)
        result, cache_new, kept = pass_forward(
            resid_in, cache_recv, section_id, weights_own, norms_own, embed_own, head_count
        )
        mask_out = lax.dynamic_index_in_dim(present, batch_clip, 0, keepdims=False)
        fresh_all = kept + (result * mask_out,)
        buffers = tuple(
            (
                store_slot(stored, update, batch_clip, valid)
                for stored, update in zip(buffers, fresh_all)
            )
        )
        resid_send = shifted(result, "section", 1)
        cache_send = shifted(cache_new, "section", 1)
        return (resid_send, cache_send, buffers)

    forward_init = (
        jnp.zeros((local_rows, width_model), jnp.float32),
        jnp.zeros((slot_total, full_rows, 2 * width_heads), jnp.bfloat16),
        buffers_init,
    )
    unused_resid, unused_cache, buffers_done = lax.fori_loop(
        0, steps_total, forward_step, forward_init
    )
    accum_init = (
        jnp.zeros((width_model, width_heads), jnp.float32),
        jnp.zeros((width_model, width_heads), jnp.float32),
        jnp.zeros((width_model, width_heads), jnp.float32),
        jnp.zeros((width_model, width_heads), jnp.float32),
        jnp.zeros((width_model, width_hidden), jnp.float32),
        jnp.zeros((width_model, width_hidden), jnp.float32),
        jnp.zeros((width_model,), jnp.float32),
        jnp.zeros((width_model,), jnp.float32),
        jnp.zeros((width_model,), jnp.float32),
        jnp.zeros((width_model,), jnp.float32),
        jnp.zeros((width_model,), jnp.float32),
    )

    def backward_step(step_id, loop_state):
        grad_recv, cache_grad_recv, accum, entry_buffer = loop_state
        batch_id = step_id - (section_count - 1 - section_id)
        valid = (batch_id >= 0) & (batch_id < batches)
        batch_clip = jnp.clip(batch_id, 0, batches - 1)
        kept = tuple(
            (
                lax.dynamic_index_in_dim(stored, batch_clip, 0, keepdims=False)
                for stored in buffers_done[:9]
            )
        )
        mask_out = lax.dynamic_index_in_dim(present, batch_clip, 0, keepdims=False)
        grad_out = (
            lax.dynamic_index_in_dim(cotangent_own, batch_clip, 0, keepdims=False) * mask_out
            + grad_recv
        )
        grad_entered, grad_cache, grads = pass_backward(
            grad_out, cache_grad_recv, kept, section_id, weights_own, norms_own, head_count
        )
        validity = valid.astype(jnp.float32)
        accum = tuple((stored + validity * update for stored, update in zip(accum, grads)))
        entry_buffer = store_slot(entry_buffer, grad_entered, batch_clip, valid)
        grad_send = shifted(grad_entered, "section", -1)
        cache_send = shifted(grad_cache, "section", -1)
        return (grad_send, cache_send, accum, entry_buffer)

    backward_init = (
        jnp.zeros((local_rows, width_model), jnp.float32),
        jnp.zeros((slot_total, full_rows, 2 * width_heads), jnp.float32),
        accum_init,
        jnp.zeros((batches, local_rows, width_model), jnp.float32),
    )
    unused_grad, unused_cache_grad, accum, entry_buffer = lax.fori_loop(
        0, steps_total, backward_step, backward_init
    )
    first_flag = (section_id == 0).astype(jnp.float32)
    grad_inputs = lax.psum_scatter(
        entry_buffer * first_flag, "section", scatter_dimension=2, tiled=True
    )
    layer_first = (layer_id == 0).astype(jnp.float32)
    layer_second = 1.0 - layer_first

    def by_slot(grad_own):
        return jnp.stack([grad_own * layer_first, grad_own * layer_second])

    finals = lax.psum(
        (
            by_slot(accum[0]),
            by_slot(accum[1]),
            by_slot(accum[2]),
            by_slot(accum[3]),
            by_slot(accum[4]),
            by_slot(accum[5]),
        ),
        ("dp", "section"),
    )
    slot_flags = (jnp.arange(slot_total) == section_id).astype(jnp.float32)[:, None]
    smalls = lax.psum(
        (
            by_slot(accum[6]),
            by_slot(accum[7]),
            by_slot(accum[8]),
            by_slot(accum[9]),
            slot_flags * accum[10][None, :],
        ),
        ("dp", "section", "tensor"),
    )
    passes_local = buffers_done[9][None]
    return (
        passes_local,
        grad_inputs,
        finals[0],
        finals[1],
        finals[2],
        finals[3],
        finals[4],
        finals[5],
        smalls[0],
        smalls[1],
        smalls[2],
        smalls[3],
        smalls[4],
    )


def solution(mesh):
    return jax.shard_map(
        shards,
        mesh=mesh,
        in_specs=(
            P("dp", "tensor", "section"),
            P("dp"),
            P(None, None, "tensor"),
            P(None, None, "tensor"),
            P(None, None, "tensor"),
            P(None, None, "tensor"),
            P(None, None, "tensor"),
            P(None, None, "tensor"),
            P(),
            P(),
            P(),
            P(),
            P(),
            P("section", "dp", "tensor", None),
        ),
        out_specs=(
            P("section", "dp", "tensor", None),
            P("dp", "tensor", "section"),
            P(None, None, "tensor"),
            P(None, None, "tensor"),
            P(None, None, "tensor"),
            P(None, None, "tensor"),
            P(None, None, "tensor"),
            P(None, None, "tensor"),
            P(),
            P(),
            P(),
            P(),
            P(),
        ),
        check_vma=False,
    )
```

profile of v0, /device:TPU:0, one launch (start us, length us, event | category | flops | bytes accessed | tf_op | source)
XLA Modules:
  0.0 2483.9 jit_solution(5707014982693657247)
XLA Ops:
  16.8 4.2 dynamic-slice_bitcast_fusion.1
  21.0 19.3 all-gather.2.cloned.1.call-done
  55.8 599.3 %while.79 = (s32[]{:T(128)}, f32[128,768]{1,0:T(8,128)}, bf16[4,256,768]{2,1,0:T(8,128)(2,1)}, f32[3,128,768]{2,1,0:T(8,128)}, bf16[3,256,768]{2,1,0:T(8,128)(2,...) while((s32[]{:T(128)}, f32[128,768]{1,0:T(8,128)}, ...), condition=%wide.region_9.10_spmd, body=%wide.region_0.9_spmd.sunk | while | flops 2243050752 | bytes 116362184 | solution.py:319
  90.5 5.0 reduce-scatter.8.cloned.1.call-done
  107.9 4.8 collective-permute-start.1
  127.5 18.7 collective-permute-done.1
  146.3 7.8 collective-permute-done
  188.6 7.0 reduce-scatter.8.cloned.1.call-done
  208.2 4.6 collective-permute-start.1
  227.7 18.7 collective-permute-done.1
  246.4 7.8 collective-permute-done
  288.8 7.0 reduce-scatter.8.cloned.1.call-done
  308.2 4.8 collective-permute-start.1
  327.8 18.9 collective-permute-done.1
  346.7 7.8 collective-permute-done
  389.0 6.9 reduce-scatter.8.cloned.1.call-done
  408.4 4.8 collective-permute-start.1
  428.0 18.7 collective-permute-done.1
  446.7 7.8 collective-permute-done
  489.1 7.1 reduce-scatter.8.cloned.1.call-done
  508.7 4.8 collective-permute-start.1
  528.3 18.7 collective-permute-done.1
  547.0 7.8 collective-permute-done
  589.3 7.1 reduce-scatter.8.cloned.1.call-done
  609.0 4.8 collective-permute-start.1
  628.5 18.8 collective-permute-done.1
  647.3 7.8 collective-permute-done
  658.2 1006.3 %while.80 = (s32[]{:T(128)}, f32[128,768]{1,0:T(8,128)S(1)}, f32[4,256,768]{2,1,0:T(8,128)}, f32[768,384]{1,0:T(8,128)}, f32[768,384]{1,0:T(8,128)}, /*index=5*/...) while((s32[]{:T(128)}, f32[128,768]{1,0:T(8,128)S(1)}, ...), condition=%wide.region_27.28_spmd.clone, body=%wide.region_10.27_spmd.clone.sunk | while | flops 4685813760 | bytes 259792576 | solution.py:368
  692.6 4.0 select_add_fusion.12
  696.6 4.7 select_add_fusion.13
  710.8 5.8 fusion.297
  731.2 4.7 broadcast_multiply_fusion.23
  767.7 54.5 %collective-permute-done.2 = f32[128,768]{1,0:T(8,128)S(1)} collective-permute-done((f32[128,768]{1,0:T(8,128)}, f32[128,768]{1,0:T(8,128)S(1)}, u32[]{:S(2)}, u32[]{:S(2)}) %collective-permute-start.2) | collective-permute-done | bytes 393248 | tf_op jit(solution)/shard_map/while/body/eval_jaxpr/ppermute | solution.py:16
  857.8 5.5 select_add_fusion.12
  863.3 6.1 select_add_fusion.13
  878.9 5.8 fusion.297
  899.3 4.7 broadcast_multiply_fusion.23
  938.8 51.5 %collective-permute-done.2 = f32[128,768]{1,0:T(8,128)S(1)} collective-permute-done((f32[128,768]{1,0:T(8,128)}, f32[128,768]{1,0:T(8,128)S(1)}, u32[]{:S(2)}, u32[]{:S(2)}) %collective-permute-start.2) | collective-permute-done | bytes 393248 | tf_op jit(solution)/shard_map/while/body/eval_jaxpr/ppermute | solution.py:16
  1025.9 5.5 select_add_fusion.12
  1031.4 6.1 select_add_fusion.13
  1047.0 5.8 fusion.297
  1067.4 4.7 broadcast_multiply_fusion.23
  1106.9 51.5 %collective-permute-done.2 = f32[128,768]{1,0:T(8,128)S(1)} collective-permute-done((f32[128,768]{1,0:T(8,128)}, f32[128,768]{1,0:T(8,128)S(1)}, u32[]{:S(2)}, u32[]{:S(2)}) %collective-permute-start.2) | collective-permute-done | bytes 393248 | tf_op jit(solution)/shard_map/while/body/eval_jaxpr/ppermute | solution.py:16
  1194.0 5.5 select_add_fusion.12
  1199.5 6.1 select_add_fusion.13
  1215.0 5.8 fusion.297
  1235.5 4.7 broadcast_multiply_fusion.23
  1275.0 51.5 %collective-permute-done.2 = f32[128,768]{1,0:T(8,128)S(1)} collective-permute-done((f32[128,768]{1,0:T(8,128)}, f32[128,768]{1,0:T(8,128)S(1)}, u32[]{:S(2)}, u32[]{:S(2)}) %collective-permute-start.2) | collective-permute-done | bytes 393248 | tf_op jit(solution)/shard_map/while/body/eval_jaxpr/ppermute | solution.py:16
  1362.1 5.5 select_add_fusion.12
  1367.6 6.1 select_add_fusion.13
  1383.1 5.8 fusion.297
  1403.6 4.7 broadcast_multiply_fusion.23
  1443.1 51.5 %collective-permute-done.2 = f32[128,768]{1,0:T(8,128)S(1)} collective-permute-done((f32[128,768]{1,0:T(8,128)}, f32[128,768]{1,0:T(8,128)S(1)}, u32[]{:S(2)}, u32[]{:S(2)}) %collective-permute-start.2) | collective-permute-done | bytes 393248 | tf_op jit(solution)/shard_map/while/body/eval_jaxpr/ppermute | solution.py:16
  1530.2 5.5 select_add_fusion.12
  1535.7 6.1 select_add_fusion.13
  1551.2 5.8 fusion.297
  1571.7 4.7 broadcast_multiply_fusion.23
  1611.2 51.5 %collective-permute-done.2 = f32[128,768]{1,0:T(8,128)S(1)} collective-permute-done((f32[128,768]{1,0:T(8,128)}, f32[128,768]{1,0:T(8,128)S(1)}, u32[]{:S(2)}, u32[]{:S(2)}) %collective-permute-start.2) | collective-permute-done | bytes 393248 | tf_op jit(solution)/shard_map/while/body/eval_jaxpr/ppermute | solution.py:16
  1664.5 7.7 multiply_bitcast_fusion.2
  1689.3 4.6 pad_maximum_fusion.1
  1695.5 4.6 pad_maximum_fusion
  1701.7 42.9 %all-reduce = (f32[2,768]{1,0:T(2,128)}, f32[2,768]{1,0:T(2,128)}, f32[2,768]{1,0:T(2,128)}, f32[2,768]{1,0:T(2,128)}, f32[4,768]{1,0:T(4,128)}) all-reduce(f32[2,768]{1,0:T(2,128)S(1)} %pad_maximum_fusion.6, f32[2,768]{1,0:T(2,128)S(1)} %pad_maximum_fusion.7, ...), channel_id=1, replica_groups=mesh['dp'=4,'section'=4,'tensor'=2] {'dp','section','tensor'}, use_global_device_ids=true, to_apply=%region_35.36 | all-reduce | flops 9216 | bytes 73728 | tf_op jit(solution)/shard_map/psum | solution.py:393
  1744.6 712.3 %all-reduce.4.cloned.1.call-done = (f32[2,768,384]{2,1,0:T(8,128)}, f32[2,768,384]{2,1,0:T(8,128)}, f32[2,768,384]{2,1,0:T(8,128)}, f32[2,768,384]{2,1,0:T(8,128...) async-done(((f32[2,768,384]{2,1,0:T(8,128)}, f32[2,768,384]{2,1,0:T(8,128)}, f32[2,768,384]{2,1,0:T(8,128)}, f32[2,768,384]{2,1,0:T(8,128)}, f32[2,768,1536]{2,1,0:T(8,128)}, ...) | async-done | bytes 28311568 | tf_op jit(solution)/shard_map/psum | solution.py:381
  2467.0 4.8 copy.199
  (1438 shorter events, 993.9 us)
Async XLA Ops:
  7.2 33.1 %all-gather.2.cloned.1.call-start = ((), (), s32[]{:S(2)}) async-start(), calls=%async_computation.5 | async-start | bytes 1474560 | tf_op jit(solution)/shard_map/all_gather | solution.py:272
  55.9 39.5 %reduce-scatter.8.cloned.1.call-start = ((), (), s32[]{:S(2)}) async-start(), calls=%async_computation.8 | async-start | bytes 1179648 | tf_op jit(solution)/shard_map/while/body/eval_jaxpr/reduce_scatter | solution.py:47
  86.7 34.5 %reduce-scatter.10.cloned.1.call-start = ((), (), s32[]{:S(2)}) async-start(), calls=%async_computation.9 | async-start | bytes 1179648 | tf_op jit(solution)/shard_map/while/body/eval_jaxpr/reduce_scatter | solution.py:47
  107.9 38.4 %collective-permute-start.1 = (bf16[4,256,768]{2,1,0:T(8,128)(2,1)S(1)}, bf16[4,256,768]{2,1,0:T(8,128)(2,1)}, u32[]{:S(2)}, u32[]{:S(2)}) collective-permute-start(bf16[4,256,768]{2,1,0:T(8,128)(2,1)S(1)} %fusion.241), channel_id=1, source_target_pairs={{0,2},{2,4},{4,6},{1,3},{3,5},{5,7},{8,10},{10,12},{12,14},{9,11},... | collective-permute-start | bytes 4718600 | tf_op jit(solution)/shard_map/while/body/eval_jaxpr/ppermute | solution.py:16
  123.8 30.3 %collective-permute-start = (f32[128,768]{1,0:T(8,128)S(1)}, f32[128,768]{1,0:T(8,128)}, u32[]{:S(2)}, u32[]{:S(2)}) collective-permute-start(f32[128,768]{1,0:T(8,128)S(1)} %get-tuple-element.2432), channel_id=1, source_target_pairs={{0,2},{2,4},{4,6},{1,3},{3,5},{5,7},{8,10},{10,12},{12,14},{9,11},... | collective-permute-start | bytes 1179656 | tf_op jit(solution)/shard_map/while/body/eval_jaxpr/ppermute | solution.py:16
  126.7 27.4 %copy-start.47 = (f32[3,6,256,1]{2,1,3,0:T(8,128)}, f32[3,6,256,1]{2,1,3,0:T(8,128)S(1)}, u32[]{:S(2)}) copy-start(f32[3,6,256,1]{2,1,3,0:T(8,128)S(1)} %fusion.250) | copy-start | bytes 55300 | tf_op jit(solution)/shard_map/while
  154.1 41.5 %reduce-scatter.8.cloned.1.call-start = ((), (), s32[]{:S(2)}) async-start(), calls=%async_computation.8 | async-start | bytes 1179648 | tf_op jit(solution)/shard_map/while/body/eval_jaxpr/reduce_scatter | solution.py:47
  184.8 36.5 %reduce-scatter.10.cloned.1.call-start = ((), (), s32[]{:S(2)}) async-start(), calls=%async_computation.9 | async-start | bytes 1179648 | tf_op jit(solution)/shard_map/while/body/eval_jaxpr/reduce_scatter | solution.py:47
  208.2 38.2 %collective-permute-start.1 = (bf16[4,256,768]{2,1,0:T(8,128)(2,1)S(1)}, bf16[4,256,768]{2,1,0:T(8,128)(2,1)}, u32[]{:S(2)}, u32[]{:S(2)}) collective-permute-start(bf16[4,256,768]{2,1,0:T(8,128)(2,1)S(1)} %fusion.241), channel_id=1, source_target_pairs={{0,2},{2,4},{4,6},{1,3},{3,5},{5,7},{8,10},{10,12},{12,14},{9,11},... | collective-permute-start | bytes 4718600 | tf_op jit(solution)/shard_map/while/body/eval_jaxpr/ppermute | solution.py:16
  223.9 30.4 %collective-permute-start = (f32[128,768]{1,0:T(8,128)S(1)}, f32[128,768]{1,0:T(8,128)}, u32[]{:S(2)}, u32[]{:S(2)}) collective-permute-start(f32[128,768]{1,0:T(8,128)S(1)} %get-tuple-element.2432), channel_id=1, source_target_pairs={{0,2},{2,4},{4,6},{1,3},{3,5},{5,7},{8,10},{10,12},{12,14},{9,11},... | collective-permute-start | bytes 1179656 | tf_op jit(solution)/shard_map/while/body/eval_jaxpr/ppermute | solution.py:16
  226.8 27.4 %copy-start.47 = (f32[3,6,256,1]{2,1,3,0:T(8,128)}, f32[3,6,256,1]{2,1,3,0:T(8,128)S(1)}, u32[]{:S(2)}) copy-start(f32[3,6,256,1]{2,1,3,0:T(8,128)S(1)} %fusion.250) | copy-start | bytes 55300 | tf_op jit(solution)/shard_map/while
  254.2 41.5 %reduce-scatter.8.cloned.1.call-start = ((), (), s32[]{:S(2)}) async-start(), calls=%async_computation.8 | async-start | bytes 1179648 | tf_op jit(solution)/shard_map/while/body/eval_jaxpr/reduce_scatter | solution.py:47
  285.0 36.5 %reduce-scatter.10.cloned.1.call-start = ((), (), s32[]{:S(2)}) async-start(), calls=%async_computation.9 | async-start | bytes 1179648 | tf_op jit(solution)/shard_map/while/body/eval_jaxpr/reduce_scatter | solution.py:47
  308.2 38.4 %collective-permute-start.1 = (bf16[4,256,768]{2,1,0:T(8,128)(2,1)S(1)}, bf16[4,256,768]{2,1,0:T(8,128)(2,1)}, u32[]{:S(2)}, u32[]{:S(2)}) collective-permute-start(bf16[4,256,768]{2,1,0:T(8,128)(2,1)S(1)} %fusion.241), channel_id=1, source_target_pairs={{0,2},{2,4},{4,6},{1,3},{3,5},{5,7},{8,10},{10,12},{12,14},{9,11},... | collective-permute-start | bytes 4718600 | tf_op jit(solution)/shard_map/while/body/eval_jaxpr/ppermute | solution.py:16
  324.1 30.4 %collective-permute-start = (f32[128,768]{1,0:T(8,128)S(1)}, f32[128,768]{1,0:T(8,128)}, u32[]{:S(2)}, u32[]{:S(2)}) collective-permute-start(f32[128,768]{1,0:T(8,128)S(1)} %get-tuple-element.2432), channel_id=1, source_target_pairs={{0,2},{2,4},{4,6},{1,3},{3,5},{5,7},{8,10},{10,12},{12,14},{9,11},... | collective-permute-start | bytes 1179656 | tf_op jit(solution)/shard_map/while/body/eval_jaxpr/ppermute | solution.py:16
  326.9 27.5 %copy-start.47 = (f32[3,6,256,1]{2,1,3,0:T(8,128)}, f32[3,6,256,1]{2,1,3,0:T(8,128)S(1)}, u32[]{:S(2)}) copy-start(f32[3,6,256,1]{2,1,3,0:T(8,128)S(1)} %fusion.250) | copy-start | bytes 55300 | tf_op jit(solution)/shard_map/while
  354.5 41.4 %reduce-scatter.8.cloned.1.call-start = ((), (), s32[]{:S(2)}) async-start(), calls=%async_computation.8 | async-start | bytes 1179648 | tf_op jit(solution)/shard_map/while/body/eval_jaxpr/reduce_scatter | solution.py:47
  385.2 36.4 %reduce-scatter.10.cloned.1.call-start = ((), (), s32[]{:S(2)}) async-start(), calls=%async_computation.9 | async-start | bytes 1179648 | tf_op jit(solution)/shard_map/while/body/eval_jaxpr/reduce_scatter | solution.py:47
  408.4 38.3 %collective-permute-start.1 = (bf16[4,256,768]{2,1,0:T(8,128)(2,1)S(1)}, bf16[4,256,768]{2,1,0:T(8,128)(2,1)}, u32[]{:S(2)}, u32[]{:S(2)}) collective-permute-start(bf16[4,256,768]{2,1,0:T(8,128)(2,1)S(1)} %fusion.241), channel_id=1, source_target_pairs={{0,2},{2,4},{4,6},{1,3},{3,5},{5,7},{8,10},{10,12},{12,14},{9,11},... | collective-permute-start | bytes 4718600 | tf_op jit(solution)/shard_map/while/body/eval_jaxpr/ppermute | solution.py:16
  424.2 30.4 %collective-permute-start = (f32[128,768]{1,0:T(8,128)S(1)}, f32[128,768]{1,0:T(8,128)}, u32[]{:S(2)}, u32[]{:S(2)}) collective-permute-start(f32[128,768]{1,0:T(8,128)S(1)} %get-tuple-element.2432), channel_id=1, source_target_pairs={{0,2},{2,4},{4,6},{1,3},{3,5},{5,7},{8,10},{10,12},{12,14},{9,11},... | collective-permute-start | bytes 1179656 | tf_op jit(solution)/shard_map/while/body/eval_jaxpr/ppermute | solution.py:16
  427.2 27.4 %copy-start.47 = (f32[3,6,256,1]{2,1,3,0:T(8,128)}, f32[3,6,256,1]{2,1,3,0:T(8,128)S(1)}, u32[]{:S(2)}) copy-start(f32[3,6,256,1]{2,1,3,0:T(8,128)S(1)} %fusion.250) | copy-start | bytes 55300 | tf_op jit(solution)/shard_map/while
  454.5 41.6 %reduce-scatter.8.cloned.1.call-start = ((), (), s32[]{:S(2)}) async-start(), calls=%async_computation.8 | async-start | bytes 1179648 | tf_op jit(solution)/shard_map/while/body/eval_jaxpr/reduce_scatter | solution.py:47
  485.3 36.6 %reduce-scatter.10.cloned.1.call-start = ((), (), s32[]{:S(2)}) async-start(), calls=%async_computation.9 | async-start | bytes 1179648 | tf_op jit(solution)/shard_map/while/body/eval_jaxpr/reduce_scatter | solution.py:47
  508.7 38.3 %collective-permute-start.1 = (bf16[4,256,768]{2,1,0:T(8,128)(2,1)S(1)}, bf16[4,256,768]{2,1,0:T(8,128)(2,1)}, u32[]{:S(2)}, u32[]{:S(2)}) collective-permute-start(bf16[4,256,768]{2,1,0:T(8,128)(2,1)S(1)} %fusion.241), channel_id=1, source_target_pairs={{0,2},{2,4},{4,6},{1,3},{3,5},{5,7},{8,10},{10,12},{12,14},{9,11},... | collective-permute-start | bytes 4718600 | tf_op jit(solution)/shard_map/while/body/eval_jaxpr/ppermute | solution.py:16
  524.5 30.4 %collective-permute-start = (f32[128,768]{1,0:T(8,128)S(1)}, f32[128,768]{1,0:T(8,128)}, u32[]{:S(2)}, u32[]{:S(2)}) collective-permute-start(f32[128,768]{1,0:T(8,128)S(1)} %get-tuple-element.2432), channel_id=1, source_target_pairs={{0,2},{2,4},{4,6},{1,3},{3,5},{5,7},{8,10},{10,12},{12,14},{9,11},... | collective-permute-start | bytes 1179656 | tf_op jit(solution)/shard_map/while/body/eval_jaxpr/ppermute | solution.py:16
  527.4 27.4 %copy-start.47 = (f32[3,6,256,1]{2,1,3,0:T(8,128)}, f32[3,6,256,1]{2,1,3,0:T(8,128)S(1)}, u32[]{:S(2)}) copy-start(f32[3,6,256,1]{2,1,3,0:T(8,128)S(1)} %fusion.250) | copy-start | bytes 55300 | tf_op jit(solution)/shard_map/while
  554.8 41.6 %reduce-scatter.8.cloned.1.call-start = ((), (), s32[]{:S(2)}) async-start(), calls=%async_computation.8 | async-start | bytes 1179648 | tf_op jit(solution)/shard_map/while/body/eval_jaxpr/reduce_scatter | solution.py:47
  585.6 36.6 %reduce-scatter.10.cloned.1.call-start = ((), (), s32[]{:S(2)}) async-start(), calls=%async_computation.9 | async-start | bytes 1179648 | tf_op jit(solution)/shard_map/while/body/eval_jaxpr/reduce_scatter | solution.py:47
  609.0 38.3 %collective-permute-start.1 = (bf16[4,256,768]{2,1,0:T(8,128)(2,1)S(1)}, bf16[4,256,768]{2,1,0:T(8,128)(2,1)}, u32[]{:S(2)}, u32[]{:S(2)}) collective-permute-start(bf16[4,256,768]{2,1,0:T(8,128)(2,1)S(1)} %fusion.241), channel_id=1, source_target_pairs={{0,2},{2,4},{4,6},{1,3},{3,5},{5,7},{8,10},{10,12},{12,14},{9,11},... | collective-permute-start | bytes 4718600 | tf_op jit(solution)/shard_map/while/body/eval_jaxpr/ppermute | solution.py:16
  624.8 30.4 %collective-permute-start = (f32[128,768]{1,0:T(8,128)S(1)}, f32[128,768]{1,0:T(8,128)}, u32[]{:S(2)}, u32[]{:S(2)}) collective-permute-start(f32[128,768]{1,0:T(8,128)S(1)} %get-tuple-element.2432), channel_id=1, source_target_pairs={{0,2},{2,4},{4,6},{1,3},{3,5},{5,7},{8,10},{10,12},{12,14},{9,11},... | collective-permute-start | bytes 1179656 | tf_op jit(solution)/shard_map/while/body/eval_jaxpr/ppermute | solution.py:16
  627.7 27.4 %copy-start.47 = (f32[3,6,256,1]{2,1,3,0:T(8,128)}, f32[3,6,256,1]{2,1,3,0:T(8,128)S(1)}, u32[]{:S(2)}) copy-start(f32[3,6,256,1]{2,1,3,0:T(8,128)S(1)} %fusion.250) | copy-start | bytes 55300 | tf_op jit(solution)/shard_map/while
  658.6 42.7 %reduce-scatter.12.cloned.1.call-start = ((), (), s32[]{:S(2)}) async-start(), calls=%async_computation.10 | async-start | bytes 1179648 | tf_op jit(solution)/shard_map/while/body/eval_jaxpr/reduce_scatter | solution.py:47
  671.6 84.4 %reduce-scatter.14.cloned.1.call-start = ((), (), s32[]{:S(2)}) async-start(), calls=%async_computation.11 | async-start | bytes 1179648 | tf_op jit(solution)/shard_map/while/body/eval_jaxpr/reduce_scatter | solution.py:47
  683.5 9.1 copy-start.13
  704.7 11.8 slice-start
  740.7 81.5 %collective-permute-start.3 = (f32[4,256,768]{2,1,0:T(8,128)}, f32[4,256,768]{2,1,0:T(8,128)S(1)}, u32[]{:S(2)}, u32[]{:S(2)}) collective-permute-start(f32[4,256,768]{2,1,0:T(8,128)} %get-tuple-element.2491), channel_id=1, source_target_pairs={{2,0},{4,2},{6,4},{3,1},{5,3},{7,5},{10,8},{12,10},{14,12},{11,9},... | collective-permute-start | bytes 9437192 | tf_op jit(solution)/shard_map/while/body/eval_jaxpr/ppermute | solution.py:16
  760.5 61.7 %collective-permute-start.2 = (f32[128,768]{1,0:T(8,128)}, f32[128,768]{1,0:T(8,128)S(1)}, u32[]{:S(2)}, u32[]{:S(2)}) collective-permute-start(f32[128,768]{1,0:T(8,128)} %get-tuple-element.2490), channel_id=1, source_target_pairs={{2,0},{4,2},{6,4},{3,1},{5,3},{7,5},{10,8},{12,10},{14,12},{11,9},... | collective-permute-start | bytes 1179656 | tf_op jit(solution)/shard_map/while/body/eval_jaxpr/ppermute | solution.py:16
  823.9 45.6 %reduce-scatter.12.cloned.1.call-start = ((), (), s32[]{:S(2)}) async-start(), calls=%async_computation.10 | async-start | bytes 1179648 | tf_op jit(solution)/shard_map/while/body/eval_jaxpr/reduce_scatter | solution.py:47
  836.8 88.9 %reduce-scatter.14.cloned.1.call-start = ((), (), s32[]{:S(2)}) async-start(), calls=%async_computation.11 | async-start | bytes 1179648 | tf_op jit(solution)/shard_map/while/body/eval_jaxpr/reduce_scatter | solution.py:47
  872.8 11.8 slice-start
  908.8 81.5 %collective-permute-start.3 = (f32[4,256,768]{2,1,0:T(8,128)}, f32[4,256,768]{2,1,0:T(8,128)S(1)}, u32[]{:S(2)}, u32[]{:S(2)}) collective-permute-start(f32[4,256,768]{2,1,0:T(8,128)} %get-tuple-element.2491), channel_id=1, source_target_pairs={{2,0},{4,2},{6,4},{3,1},{5,3},{7,5},{10,8},{12,10},{14,12},{11,9},... | collective-permute-start | bytes 9437192 | tf_op jit(solution)/shard_map/while/body/eval_jaxpr/ppermute | solution.py:16
  930.3 60.0 %collective-permute-start.2 = (f32[128,768]{1,0:T(8,128)}, f32[128,768]{1,0:T(8,128)S(1)}, u32[]{:S(2)}, u32[]{:S(2)}) collective-permute-start(f32[128,768]{1,0:T(8,128)} %get-tuple-element.2490), channel_id=1, source_target_pairs={{2,0},{4,2},{6,4},{3,1},{5,3},{7,5},{10,8},{12,10},{14,12},{11,9},... | collective-permute-start | bytes 1179656 | tf_op jit(solution)/shard_map/while/body/eval_jaxpr/ppermute | solution.py:16
  992.0 45.6 %reduce-scatter.12.cloned.1.call-start = ((), (), s32[]{:S(2)}) async-start(), calls=%async_computation.10 | async-start | bytes 1179648 | tf_op jit(solution)/shard_map/while/body/eval_jaxpr/reduce_scatter | solution.py:47
  1004.9 88.9 %reduce-scatter.14.cloned.1.call-start = ((), (), s32[]{:S(2)}) async-start(), calls=%async_computation.11 | async-start | bytes 1179648 | tf_op jit(solution)/shard_map/while/body/eval_jaxpr/reduce_scatter | solution.py:47
  1040.9 11.8 slice-start
  1076.9 81.5 %collective-permute-start.3 = (f32[4,256,768]{2,1,0:T(8,128)}, f32[4,256,768]{2,1,0:T(8,128)S(1)}, u32[]{:S(2)}, u32[]{:S(2)}) collective-permute-start(f32[4,256,768]{2,1,0:T(8,128)} %get-tuple-element.2491), channel_id=1, source_target_pairs={{2,0},{4,2},{6,4},{3,1},{5,3},{7,5},{10,8},{12,10},{14,12},{11,9},... | collective-permute-start | bytes 9437192 | tf_op jit(solution)/shard_map/while/body/eval_jaxpr/ppermute | solution.py:16
  1098.4 60.1 %collective-permute-start.2 = (f32[128,768]{1,0:T(8,128)}, f32[128,768]{1,0:T(8,128)S(1)}, u32[]{:S(2)}, u32[]{:S(2)}) collective-permute-start(f32[128,768]{1,0:T(8,128)} %get-tuple-element.2490), channel_id=1, source_target_pairs={{2,0},{4,2},{6,4},{3,1},{5,3},{7,5},{10,8},{12,10},{14,12},{11,9},... | collective-permute-start | bytes 1179656 | tf_op jit(solution)/shard_map/while/body/eval_jaxpr/ppermute | solution.py:16
  1160.1 45.6 %reduce-scatter.12.cloned.1.call-start = ((), (), s32[]{:S(2)}) async-start(), calls=%async_computation.10 | async-start | bytes 1179648 | tf_op jit(solution)/shard_map/while/body/eval_jaxpr/reduce_scatter | solution.py:47
  1173.0 88.9 %reduce-scatter.14.cloned.1.call-start = ((), (), s32[]{:S(2)}) async-start(), calls=%async_computation.11 | async-start | bytes 1179648 | tf_op jit(solution)/shard_map/while/body/eval_jaxpr/reduce_scatter | solution.py:47
  1209.0 11.8 slice-start
  1245.0 81.5 %collective-permute-start.3 = (f32[4,256,768]{2,1,0:T(8,128)}, f32[4,256,768]{2,1,0:T(8,128)S(1)}, u32[]{:S(2)}, u32[]{:S(2)}) collective-permute-start(f32[4,256,768]{2,1,0:T(8,128)} %get-tuple-element.2491), channel_id=1, source_target_pairs={{2,0},{4,2},{6,4},{3,1},{5,3},{7,5},{10,8},{12,10},{14,12},{11,9},... | collective-permute-start | bytes 9437192 | tf_op jit(solution)/shard_map/while/body/eval_jaxpr/ppermute | solution.py:16
  1266.5 60.1 %collective-permute-start.2 = (f32[128,768]{1,0:T(8,128)}, f32[128,768]{1,0:T(8,128)S(1)}, u32[]{:S(2)}, u32[]{:S(2)}) collective-permute-start(f32[128,768]{1,0:T(8,128)} %get-tuple-element.2490), channel_id=1, source_target_pairs={{2,0},{4,2},{6,4},{3,1},{5,3},{7,5},{10,8},{12,10},{14,12},{11,9},... | collective-permute-start | bytes 1179656 | tf_op jit(solution)/shard_map/while/body/eval_jaxpr/ppermute | solution.py:16
  1328.1 45.6 %reduce-scatter.12.cloned.1.call-start = ((), (), s32[]{:S(2)}) async-start(), calls=%async_computation.10 | async-start | bytes 1179648 | tf_op jit(solution)/shard_map/while/body/eval_jaxpr/reduce_scatter | solution.py:47
  1341.1 88.9 %reduce-scatter.14.cloned.1.call-start = ((), (), s32[]{:S(2)}) async-start(), calls=%async_computation.11 | async-start | bytes 1179648 | tf_op jit(solution)/shard_map/while/body/eval_jaxpr/reduce_scatter | solution.py:47
  1377.1 11.8 slice-start
  1413.1 81.5 %collective-permute-start.3 = (f32[4,256,768]{2,1,0:T(8,128)}, f32[4,256,768]{2,1,0:T(8,128)S(1)}, u32[]{:S(2)}, u32[]{:S(2)}) collective-permute-start(f32[4,256,768]{2,1,0:T(8,128)} %get-tuple-element.2491), channel_id=1, source_target_pairs={{2,0},{4,2},{6,4},{3,1},{5,3},{7,5},{10,8},{12,10},{14,12},{11,9},... | collective-permute-start | bytes 9437192 | tf_op jit(solution)/shard_map/while/body/eval_jaxpr/ppermute | solution.py:16
  1434.5 60.1 %collective-permute-start.2 = (f32[128,768]{1,0:T(8,128)}, f32[128,768]{1,0:T(8,128)S(1)}, u32[]{:S(2)}, u32[]{:S(2)}) collective-permute-start(f32[128,768]{1,0:T(8,128)} %get-tuple-element.2490), channel_id=1, source_target_pairs={{2,0},{4,2},{6,4},{3,1},{5,3},{7,5},{10,8},{12,10},{14,12},{11,9},... | collective-permute-start | bytes 1179656 | tf_op jit(solution)/shard_map/while/body/eval_jaxpr/ppermute | solution.py:16
  1496.2 45.6 %reduce-scatter.12.cloned.1.call-start = ((), (), s32[]{:S(2)}) async-start(), calls=%async_computation.10 | async-start | bytes 1179648 | tf_op jit(solution)/shard_map/while/body/eval_jaxpr/reduce_scatter | solution.py:47
  1509.2 88.9 %reduce-scatter.14.cloned.1.call-start = ((), (), s32[]{:S(2)}) async-start(), calls=%async_computation.11 | async-start | bytes 1179648 | tf_op jit(solution)/shard_map/while/body/eval_jaxpr/reduce_scatter | solution.py:47
  1545.2 11.8 slice-start
  1581.2 81.5 %collective-permute-start.3 = (f32[4,256,768]{2,1,0:T(8,128)}, f32[4,256,768]{2,1,0:T(8,128)S(1)}, u32[]{:S(2)}, u32[]{:S(2)}) collective-permute-start(f32[4,256,768]{2,1,0:T(8,128)} %get-tuple-element.2491), channel_id=1, source_target_pairs={{2,0},{4,2},{6,4},{3,1},{5,3},{7,5},{10,8},{12,10},{14,12},{11,9},... | collective-permute-start | bytes 9437192 | tf_op jit(solution)/shard_map/while/body/eval_jaxpr/ppermute | solution.py:16
  1602.6 60.1 %collective-permute-start.2 = (f32[128,768]{1,0:T(8,128)}, f32[128,768]{1,0:T(8,128)S(1)}, u32[]{:S(2)}, u32[]{:S(2)}) collective-permute-start(f32[128,768]{1,0:T(8,128)} %get-tuple-element.2490), channel_id=1, source_target_pairs={{2,0},{4,2},{6,4},{3,1},{5,3},{7,5},{10,8},{12,10},{14,12},{11,9},... | collective-permute-start | bytes 1179656 | tf_op jit(solution)/shard_map/while/body/eval_jaxpr/ppermute | solution.py:16
  1664.5 80.2 %reduce-scatter.6.cloned.1.call-start = ((), (), s32[]{:S(2)}) async-start(), calls=%async_computation.6 | async-start | bytes 1474560 | tf_op jit(solution)/shard_map/reduce_scatter | solution.py:372
  1680.2 776.8 %all-reduce.4.cloned.1.call-start = ((), (), s32[]{:S(2)}) async-start(), calls=%async_computation.7 | async-start | bytes 56623104 | tf_op jit(solution)/shard_map/psum | solution.py:381
  (281 other events, 1014.0 us)
Sparse Core Ops, SparseCore 0:
  9.9 30.4 all-gather.1
  86.9 8.5 reduce-scatter.7
  108.1 9.4 reduce-scatter.9
  185.0 10.6 reduce-scatter.7
  208.3 9.2 reduce-scatter.9
  285.1 10.5 reduce-scatter.7
  308.4 9.3 reduce-scatter.9
  385.4 10.4 reduce-scatter.7
  408.5 9.3 reduce-scatter.9
  485.4 10.6 reduce-scatter.7
  508.8 9.4 reduce-scatter.9
  585.7 10.6 reduce-scatter.7
  609.1 9.3 reduce-scatter.9
  671.7 10.2 reduce-scatter.11
  740.3 10.2 reduce-scatter.13
  837.0 9.3 reduce-scatter.11
  908.4 9.4 reduce-scatter.13
  1005.0 9.3 reduce-scatter.11
  1076.5 9.3 reduce-scatter.13
  1173.1 9.3 reduce-scatter.11
  1244.6 9.3 reduce-scatter.13
  1341.2 9.3 reduce-scatter.11
  1412.7 9.3 reduce-scatter.13
  1509.3 9.3 reduce-scatter.11
  1580.7 9.3 reduce-scatter.13
  1680.3 29.7 reduce-scatter.5
  1716.9 739.9 all-reduce.3
where the time goes:
time: 2510 us; the launch traced here: 2480 us
  waiting for transfers between devices  1240 us (49%)
  matrix products  395 us (16%)
  local copies, waits for them, and re-layouts  366 us (15%)
  other arithmetic  304 us (12%)
  blocking collectives  92.9 us (4%)
  starting transfers between devices  62.2 us (2%)
    psum x1, waiting for transfers between devices, shards(): lax.psum((by_slot(accum[0]), by_slot(accum[1]), by_slot(accum[2]), by_slo...  712 us
    ppermute x24, waiting for transfers between devices, shifted(): lax.ppermute(value, axis, [(source, source + steps) for source in range(i...  471 us
    dot_general x36, matrix products, dot_rows(): lax.dot_general(left_side, right_side, (((0,), (0,)), ((), ())), preferre...  123 us
    dynamic_slice x54, local copies, waits for them, and re-layouts, store_slot(): previous = lax.dynamic_index_in_dim(buffer, batch_clip, 0, keepdims=False)  79.3 us
    dot_general x36, matrix products, reduce_rows(): lax.dot_general(left_side, right_side, (((1,), (1,)), ((), ())), preferre...  74.8 us
    ppermute x24, starting transfers between devices, shifted(): lax.ppermute(value, axis, [(source, source + steps) for source in range(i...  61.5 us
    dynamic_update_slice x48, other arithmetic, store_slot(): return lax.dynamic_update_index_in_dim(buffer, chosen, batch_clip, 0)  56 us
  transfers between devices with their start and end apart: 51, of which 26 were waited for; matrix products, arithmetic and copies ran while one was open for 19% of the time, Pallas kernels for 0%

commit v1 on v0

v1 whole, which is shorter than its diff:
```python
import functools

import jax
import jax.numpy as jnp
from jax import lax
from jax.experimental import pallas as pl
from jax.experimental.pallas import tpu as pltpu
from jax.sharding import PartitionSpec as P

HEADS = 12
EPSILON = 1e-05
MASKED = -1e30
F32 = jnp.float32
BF16 = jnp.bfloat16
ROOT = 0.7978845608028654
CUBIC = 0.044715
NN = (((1,), (0,)), ((), ()))
NT = (((1,), (1,)), ((), ()))
TN = (((0,), (0,)), ((), ()))
VMEM_LIMIT = 40 * 1024 * 1024


def dot(left, right, dims=NN):
    return lax.dot_general(left, right, dims, preferred_element_type=F32)


def norm_parts(rows):
    centred = rows - jnp.mean(rows, axis=-1, keepdims=True)
    spread = jnp.mean(centred * centred, axis=-1, keepdims=True)
    inverse = lax.rsqrt(spread + EPSILON)
    return centred * inverse, inverse


def norm_back(rows, gain, grad):
    normal, inverse = norm_parts(rows)
    scaled = gain * grad
    middle = jnp.mean(scaled, axis=-1, keepdims=True)
    along = jnp.mean(scaled * normal, axis=-1, keepdims=True)
    back = inverse * (scaled - middle - normal * along)
    gain_sum = jnp.sum(grad * normal, axis=0, keepdims=True)
    bias_sum = jnp.sum(grad, axis=0, keepdims=True)
    return back, gain_sum, bias_sum


def both(own, other):
    return own[...].astype(F32) + other[...].astype(F32)


def fetch(sources, layer, places, sems):
    copies = []
    for index, (source, place) in enumerate(zip(sources, places)):
        copy = pltpu.make_async_copy(source.at[layer], place, sems.at[index])
        copy.start()
        copies.append(copy)
    return copies


def causal_mask(length):
    key_place = lax.broadcasted_iota(jnp.int32, (length, length), 0)
    query_place = lax.broadcasted_iota(jnp.int32, (length, length), 1)
    return key_place <= query_place


def lane_half(rows, half, pair):
    lane = lax.broadcasted_iota(jnp.int32, pair.shape, 1)
    keep = (lane < 64) if half == 0 else (lane >= 64)
    return jnp.where(keep, pair, jnp.zeros_like(pair))


def attention_forward(step, layer, *refs):
    refs = list(refs)
    take = lambda count: [refs.pop(0) for _ in range(count)]
    if step == 0:
        (x_ref,) = take(1)
    else:
        r_ref, own_ref, other_ref = take(3)
    embed_ref, gain_ref, bias_ref = take(3)
    wq, wk, wv, wo = take(4)
    past_k = take(step)
    past_vt = take(step)
    if step > 0:
        (h_ref,) = take(1)
    u_ref, a_ref, q_ref, k_ref, kt_ref, v_ref, vt_ref, lse_ref, o_ref, part_ref = take(10)
    wq_v, wk_v, wv_v, wo_v, ot_v, sems = take(6)
    copies = fetch((wq, wk, wv, wo), layer, (wq_v, wk_v, wv_v, wo_v), sems)
    if step == 0:
        entered = x_ref[...] + embed_ref[0:1, :]
    else:
        result = r_ref[...] + both(own_ref, other_ref)
        h_ref[...] = result
        entered = result + embed_ref[step : step + 1, :]
    u_ref[...] = entered
    normal, _ = norm_parts(entered)
    a = (normal * gain_ref[layer : layer + 1, :] + bias_ref[layer : layer + 1, :]).astype(BF16)
    a_ref[...] = a
    copies[0].wait()
    q_ref[...] = (dot(a, wq_v[...]).astype(BF16).astype(F32) * 0.125).astype(BF16)
    copies[1].wait()
    k_full = dot(a, wk_v[...])
    k_ref[...] = k_full.astype(BF16)
    kt_ref[...] = k_full.T.astype(BF16)
    copies[2].wait()
    v_full = dot(a, wv_v[...])
    v_ref[...] = v_full.astype(BF16)
    vt_ref[...] = v_full.T.astype(BF16)
    length = entered.shape[0]
    seen = causal_mask(length)
    all_k = past_k + [k_ref]
    all_vt = past_vt + [vt_ref]
    head_count = q_ref.shape[1] // 64
    for head in range(head_count):
        pair, half = divmod(head, 2)
        lanes = slice(128 * pair, 128 * pair + 128)
        query = lane_half(length, half, q_ref[:, lanes])
        scores = [jnp.where(seen, dot(key[:, lanes], query, NT), MASKED) for key in all_k]
        highest = functools.reduce(
            jnp.maximum, [jnp.max(one, axis=0, keepdims=True) for one in scores]
        )
        powers = [jnp.exp(one - highest) for one in scores]
        total = functools.reduce(jnp.add, [jnp.sum(one, axis=0, keepdims=True) for one in powers])
        inverse = 1.0 / total
        lse_ref[head : head + 1, :] = highest + jnp.log(total)
        rows = slice(64 * head, 64 * head + 64)
        mixed = None
        for power, value in zip(powers, all_vt):
            term = dot(value[rows, :], (power * inverse).astype(BF16))
            mixed = term if mixed is None else mixed + term
        ot_v[rows, :] = mixed
    o = ot_v[...].T.astype(BF16)
    o_ref[...] = o
    copies[3].wait()
    part_ref[...] = dot(o, wo_v[...], NT).astype(BF16)


def gelu_parts(hidden):
    square = hidden * hidden
    bent = jnp.tanh(ROOT * hidden * (1.0 + CUBIC * square))
    return square, bent


def feed_forward(layer, u_ref, own_ref, other_ref, gain_ref, bias_ref, wu, wd, *refs):
    r_ref, b_ref, g_ref, m_ref, part_ref, wu_v, wd_v, sems = refs
    copies = fetch((wu, wd), layer, (wu_v, wd_v), sems)
    middle = u_ref[...] + both(own_ref, other_ref)
    r_ref[...] = middle
    normal, _ = norm_parts(middle)
    b = (normal * gain_ref[layer : layer + 1, :] + bias_ref[layer : layer + 1, :]).astype(BF16)
    b_ref[...] = b
    copies[0].wait()
    hidden = dot(b, wu_v[...])
    g_ref[...] = hidden
    _, bent = gelu_parts(hidden)
    m = (0.5 * hidden * (1.0 + bent)).astype(BF16)
    m_ref[...] = m
    copies[1].wait()
    part_ref[...] = dot(m, wd_v[...], NT).astype(BF16)


def feed_backward(step, layer, last, *refs):
    refs = list(refs)
    take = lambda count: [refs.pop(0) for _ in range(count)]
    (cot_ref,) = take(1)
    if not last:
        dr_ref, own_ref, other_ref, u_ref, gain_ref = take(5)
    g_ref, wu, wd = take(3)
    dh_ref, e_ref, dg_ref, part_ref = take(4)
    if not last:
        (small_ref,) = take(1)
    wu_v, wd_v, sems = take(3)
    copies = fetch((wd, wu), layer, (wd_v, wu_v), sems)
    grad = cot_ref[...]
    if not last:
        back, gain_sum, bias_sum = norm_back(
            u_ref[...], gain_ref[1:2, :], both(own_ref, other_ref)
        )
        entered = dr_ref[...] + back
        small_ref[0:1, :] = gain_sum
        small_ref[1:2, :] = bias_sum
        small_ref[2:3, :] = jnp.sum(entered, axis=0, keepdims=True)
        grad = grad + entered
    dh_ref[...] = grad
    e = grad.astype(BF16)
    e_ref[...] = e
    hidden = g_ref[...]
    square, bent = gelu_parts(hidden)
    slope = 0.5 * (1.0 + bent) + 0.5 * hidden * (1.0 - bent * bent) * ROOT * (
        1.0 + 3.0 * CUBIC * square
    )
    copies[0].wait()
    dg = (dot(e, wd_v[...]) * slope).astype(BF16)
    dg_ref[...] = dg
    copies[1].wait()
    part_ref[...] = dot(dg, wu_v[...], NT).astype(BF16)


def attention_backward(step, layer, last, *refs):
    refs = list(refs)
    take = lambda count: [refs.pop(0) for _ in range(count)]
    dh_ref, own_ref, other_ref, r_ref, gain_ref = take(5)
    wq, wk, wv, wo = take(4)
    q_ref, lse_ref = take(2)
    keys = take(step + 1)
    keys_t = take(step + 1)
    values = take(step + 1)
    if not last:
        dk_in, dv_in = take(2)
    dr_ref, f_ref, dq_ref, dk_ref, dv_ref, part_ref, small_ref = take(7)
    if step > 0:
        dk_out, dv_out = take(2)
    wq_v, wk_v, wv_v, wo_v, do_v, dqt_v, sems = take(7)
    copies = fetch((wo, wq, wk, wv), layer, (wo_v, wq_v, wk_v, wv_v), sems)
    back, gain_sum, bias_sum = norm_back(
        r_ref[...], gain_ref[layer : layer + 1, :], both(own_ref, other_ref)
    )
    small_ref[0:1, :] = gain_sum
    small_ref[1:2, :] = bias_sum
    grad = dh_ref[...] + back
    dr_ref[...] = grad
    f = grad.astype(BF16)
    f_ref[...] = f
    copies[0].wait()
    do_v[...] = dot(f, wo_v[...]).astype(BF16)
    length = f.shape[0]
    seen = causal_mask(length)
    head_count = q_ref.shape[1] // 64
    for pair in range(head_count // 2):
        lanes = slice(128 * pair, 128 * pair + 128)
        key_sums = [None] * (step + 1)
        value_sums = [None] * (step + 1)
        for half in range(2):
            head = 2 * pair + half
            rows = slice(64 * head, 64 * head + 64)
            query = lane_half(length, half, q_ref[:, lanes])
            grad_mix = lane_half(length, half, do_v[:, lanes])
            logsum = lse_ref[head : head + 1, :]
            exact = [
                jnp.exp(jnp.where(seen, dot(key[:, lanes], query, NT), MASKED) - logsum)
                for key in keys
            ]
            grad_weights = [dot(value[:, lanes], grad_mix, NT) for value in values]
            delta = functools.reduce(
                jnp.add,
                [jnp.sum(p * dp, axis=0, keepdims=True) for p, dp in zip(exact, grad_weights)],
            )
            query_grad = None
            for slot in range(step + 1):
                grad_scores = (exact[slot] * (grad_weights[slot] - delta)).astype(BF16)
                term = dot(keys_t[slot][rows, :], grad_scores)
                query_grad = term if query_grad is None else query_grad + term
                key_term = dot(grad_scores, query)
                value_term = dot(exact[slot].astype(BF16), grad_mix)
                if half == 0:
                    key_sums[slot] = key_term
                    value_sums[slot] = value_term
                else:
                    key_sums[slot] = key_sums[slot] + key_term
                    value_sums[slot] = value_sums[slot] + value_term
            dqt_v[rows, :] = query_grad
        for slot in range(step + 1):
            key_sum, value_sum = key_sums[slot], value_sums[slot]
            if not last:
                key_sum = key_sum + dk_in[slot, :, lanes]
                value_sum = value_sum + dv_in[slot, :, lanes]
            if slot == step:
                dk_ref[:, lanes] = key_sum.astype(BF16)
                dv_ref[:, lanes] = value_sum.astype(BF16)
            else:
                dk_out[slot, :, lanes] = key_sum
                dv_out[slot, :, lanes] = value_sum
    dq = (dqt_v[...].T * 0.125).astype(BF16)
    dq_ref[...] = dq
    for copy in copies[1:]:
        copy.wait()
    part = dot(dq, wq_v[...], NT) + dot(dk_ref[...], wk_v[...], NT) + dot(dv_ref[...], wv_v[...], NT)
    part_ref[...] = part.astype(BF16)


def entry_backward(dr_ref, own_ref, other_ref, u_ref, gain_ref, out_ref, small_ref):
    back, gain_sum, bias_sum = norm_back(u_ref[...], gain_ref[0:1, :], both(own_ref, other_ref))
    entered = dr_ref[...] + back
    out_ref[...] = entered
    small_ref[0:1, :] = gain_sum
    small_ref[1:2, :] = bias_sum
    small_ref[2:3, :] = jnp.sum(entered, axis=0, keepdims=True)


def call(body, operands, hbm, outs, scratch, flops=0, bytes_accessed=0):
    inside = pl.BlockSpec(memory_space=pltpu.VMEM)
    outside = pl.BlockSpec(memory_space=pl.ANY)
    return pl.pallas_call(
        body,
        out_shape=tuple(jax.ShapeDtypeStruct(shape, kind) for shape, kind in outs),
        in_specs=[outside if index in hbm else inside for index in range(len(operands))],
        out_specs=tuple(inside for _ in outs),
        scratch_shapes=scratch,
        compiler_params=pltpu.CompilerParams(vmem_limit_bytes=VMEM_LIMIT),
        cost_estimate=pl.CostEstimate(
            flops=flops, bytes_accessed=bytes_accessed, transcendentals=0
        ),
    )(*operands)


def swap(value):
    return lax.ppermute(value, "tensor", [(0, 1), (1, 0)])


def xor_pairs(axis, bits):
    return [(place, place ^ bits) for place in range(lax.axis_size(axis))]


def pick(stacked, index):
    return lax.dynamic_index_in_dim(stacked, index, 0, keepdims=False)


def add_low(left, right):
    return (left.astype(F32) + right.astype(F32)).astype(BF16)


def halve(buffer, axis, bits, bit):
    rows = buffer.shape[0] // 2
    kept = lax.dynamic_slice_in_dim(buffer, bit * rows, rows, 0)
    sent = lax.dynamic_slice_in_dim(buffer, (1 - bit) * rows, rows, 0)
    return add_low(kept, lax.ppermute(sent, axis, xor_pairs(axis, bits)))


def widen(buffer, axis, bits, bit):
    other = lax.ppermute(buffer, axis, xor_pairs(axis, bits))
    ring = jnp.concatenate([other, buffer, other], axis=0)
    rows = buffer.shape[0]
    return lax.dynamic_slice_in_dim(ring, (1 - bit) * rows, 2 * rows, 0)


def line_reduce(buffer, axis):
    count = lax.axis_size(axis)
    place = lax.axis_index(axis)
    rows = buffer.shape[0] // count

    def chunk(index):
        return lax.dynamic_slice_in_dim(buffer, jnp.clip(index, 0, count - 1) * rows, rows, 0)

    up = down = None
    for step in range(1, count):
        send_up = chunk(count - step + place)
        send_down = chunk(step - count + place)
        if up is not None:
            send_up = add_low(send_up, up)
            send_down = add_low(send_down, down)
        up = lax.ppermute(send_up, axis, [(i, i + 1) for i in range(step)])
        down = lax.ppermute(
            send_down, axis, [(count - 1 - i, count - 2 - i) for i in range(step)]
        )
    total = chunk(place).astype(F32) + up.astype(F32) + down.astype(F32)
    return total.astype(BF16)


def line_gather(buffer, axis):
    count = lax.axis_size(axis)
    place = lax.axis_index(axis)
    rows = buffer.shape[0]
    below, above = [], []
    up = down = buffer
    for step in range(1, count):
        up = lax.ppermute(up, axis, [(i, i + 1) for i in range(step - 1, count - 1)])
        down = lax.ppermute(
            down, axis, [(count - 1 - i, count - 2 - i) for i in range(step - 1, count - 1)]
        )
        below.insert(0, up)
        above.append(down)
    ring = jnp.concatenate(below + [buffer] + above, axis=0)
    return lax.dynamic_slice_in_dim(ring, (count - 1 - place) * rows, count * rows, 0)


def shards(
    inputs,
    counts,
    w_query,
    w_key,
    w_value,
    w_out,
    w_up,
    w_down,
    gain_one,
    bias_one,
    gain_two,
    bias_two,
    pass_embed,
    cotangent,
):
    section_count = lax.axis_size("section")
    section = lax.axis_index("section")
    tensor = lax.axis_index("tensor")
    batches, half_rows, slice_width = inputs.shape
    length = 2 * half_rows
    width = cotangent.shape[3]
    head_width = w_query.shape[2]
    hidden_width = w_up.shape[2]
    passes = pass_embed.shape[0]
    heads = HEADS // lax.axis_size("tensor")
    bit_x, bit_y = section % 2, section // 2

    def by_item(stacked, index):
        valid = index < batches
        return jnp.where(valid, pick(stacked, jnp.minimum(index, batches - 1)), 0)

    def full_rows(own):
        other = swap(own)
        axis = own.ndim - 2
        return jnp.where(
            tensor == 0,
            jnp.concatenate([own, other], axis=axis),
            jnp.concatenate([other, own], axis=axis),
        )

    def exchange(pieces):
        got = [pieces[0]]
        for bits in range(1, section_count):
            got.append(lax.ppermute(pieces[bits], "section", xor_pairs("section", bits)))
        return jnp.stack(got)

    got = exchange([by_item(inputs, section ^ bits) for bits in range(section_count)])
    entries = full_rows(
        jnp.concatenate([pick(got, section ^ place) for place in range(section_count)], axis=1)
    )
    got = exchange([by_item(cotangent[0], section ^ bits) for bits in range(section_count)])
    own_count = by_item(counts, section)
    cot = full_rows(
        jnp.stack(
            [
                jnp.where(place < own_count, pick(got, section ^ place), 0.0)
                for place in range(passes)
            ]
        )
    )

    wide = ((length, width), F32)
    wide_low = ((length, width), BF16)
    heads_low = ((length, head_width), BF16)
    heads_turned = ((head_width, length), BF16)
    hidden_low = ((length, hidden_width), BF16)
    small = ((8, width), F32)
    square_v = pltpu.VMEM((width, head_width), BF16)
    hidden_v = pltpu.VMEM((width, hidden_width), BF16)

    kept = []
    keys, keys_t, values, values_t = [], [], [], []
    results = []
    resid = None
    for step in range(passes):
        layer = min(step, 1)
        first = [entries] if step == 0 else list(resid)
        operands = first + [pass_embed, gain_one, bias_one]
        at = len(operands)
        operands += [w_query, w_key, w_value, w_out] + keys + values_t
        outs = ([] if step == 0 else [wide]) + [
            wide,
            wide_low,
            heads_low,
            heads_low,
            heads_turned,
            heads_low,
            heads_turned,
            ((8, length), F32),
            heads_low,
            wide_low,
        ]
        done = call(
            functools.partial(attention_forward, step, layer),
            operands,
            range(at, at + 4),
            outs,
            [square_v] * 4
            + [pltpu.VMEM((head_width, length), F32), pltpu.SemaphoreType.DMA((4,))],
            flops=2 * length * width * head_width * 4
            + 4 * length * length * 64 * heads * (step + 1) * 2,
            bytes_accessed=width * head_width * 8,
        )
        if step > 0:
            results.append(done[0])
            done = done[1:]
        u, a, q, k, kt, v, vt, lse, o, part = done
        keys.append(k)
        keys_t.append(kt)
        values.append(v)
        values_t.append(vt)
        r, b, g, m, part_two = call(
            functools.partial(feed_forward, layer),
            [u, part, swap(part), gain_two, bias_two, w_up, w_down],
            (5, 6),
            [wide, wide_low, ((length, hidden_width), F32), hidden_low, wide_low],
            [hidden_v] * 2 + [pltpu.SemaphoreType.DMA((2,))],
            flops=4 * length * width * hidden_width,
            bytes_accessed=width * hidden_width * 4,
        )
        resid = (r, part_two, swap(part_two))
        kept.append((u, a, q, lse, o, r, b, g, m))
    results.append(resid[0] + (resid[1].astype(F32) + resid[2].astype(F32)))

    half_start = tensor * half_rows
    sent = jnp.stack(
        [lax.dynamic_slice_in_dim(one, half_start, half_rows, 0) for one in results]
    )
    got = exchange([pick(sent, section ^ bits) for bits in range(section_count)])
    passes_out = jnp.stack(
        [
            jnp.where(section < counts[item], pick(got, section ^ item), 0.0)
            for item in range(batches)
        ]
    )[None]

    factors = [None] * passes
    rows_small = {}
    state = None
    carried = None
    for step in reversed(range(passes)):
        layer = min(step, 1)
        last = step == passes - 1
        u, a, q, lse, o, r, b, g, m = kept[step]
        operands = [cot[step]]
        if not last:
            operands += list(state) + [gain_one]
        at = len(operands) + 1
        operands += [g, w_up, w_down]
        done = call(
            functools.partial(feed_backward, step, layer, last),
            operands,
            (at, at + 1),
            [wide, wide_low, hidden_low, wide_low] + ([] if last else [small]),
            [hidden_v] * 2 + [pltpu.SemaphoreType.DMA((2,))],
            flops=4 * length * width * hidden_width,
            bytes_accessed=width * hidden_width * 4,
        )
        dh, e, dg, part = done[:4]
        if not last:
            rows_small["entry", step + 1] = done[4]
        operands = [dh, part, swap(part), r, gain_two]
        at = len(operands)
        operands += [w_query, w_key, w_value, w_out, q, lse]
        operands += keys[: step + 1] + keys_t[: step + 1] + values[: step + 1]
        if not last:
            operands += list(carried)
        outs = [wide, wide_low, heads_low, heads_low, heads_low, wide_low, small]
        if step > 0:
            outs += [((step, length, head_width), F32)] * 2
        done = call(
            functools.partial(attention_backward, step, layer, last),
            operands,
            range(at, at + 4),
            outs,
            [square_v] * 4
            + [
                pltpu.VMEM((length, head_width), BF16),
                pltpu.VMEM((head_width, length), F32),
                pltpu.SemaphoreType.DMA((4,)),
            ],
            flops=2 * length * width * head_width * 4
            + 10 * length * length * 64 * heads * (step + 1) * 2,
            bytes_accessed=width * head_width * 8,
        )
        dr, f, dq, dk, dv, part, rows_small["middle", step] = done[:7]
        carried = done[7:]
        state = (dr, part, swap(part), u)
        factors[step] = (a, dq, dk, dv, f, o, b, dg, e, m)

    entered, rows_small["entry", 0] = call(
        entry_backward, list(state) + [gain_one], (), [wide, small], []
    )

    own_half = lax.dynamic_slice_in_dim(entered, half_start, half_rows, 0)
    pieces = jnp.stack(
        [
            own_half[:, place * slice_width : (place + 1) * slice_width]
            for place in range(section_count)
        ]
    )
    got = exchange([pick(pieces, section ^ bits) for bits in range(section_count)])
    grad_inputs = jnp.stack([pick(got, section ^ item) for item in range(batches)])

    def weight_grads(steps):
        sums = []
        for left, right in ((6, 7), (0, 1), (8, 9), (4, 5), (0, 2), (0, 3)):
            lefts = jnp.concatenate([factors[step][left] for step in steps], axis=0)
            rights = jnp.concatenate([factors[step][right] for step in steps], axis=0)
            sums.append(dot(lefts, rights, TN).astype(BF16))
        return [jnp.concatenate(sums[at : at + 2], axis=1) for at in (0, 2, 4)]

    def sum_all(parts):
        first, second, third = parts
        first = halve(first, "section", 1, bit_x)
        second = halve(second, "section", 2, bit_y)
        third = line_reduce(third, "dp")
        first = halve(first, "section", 2, bit_y)
        second = halve(second, "section", 1, bit_x)
        third = halve(third, "section", 1, bit_x)
        third = halve(third, "section", 2, bit_y)
        first = line_reduce(first, "dp")
        second = line_reduce(second, "dp")
        first = line_gather(first, "dp")
        second = line_gather(second, "dp")
        third = widen(third, "section", 2, bit_y)
        third = widen(third, "section", 1, bit_x)
        first = widen(first, "section", 2, bit_y)
        second = widen(second, "section", 1, bit_x)
        first = widen(first, "section", 1, bit_x)
        second = widen(second, "section", 2, bit_y)
        third = line_gather(third, "dp")
        return first, second, third

    later = sum_all(weight_grads(range(1, passes)))
    early = sum_all(weight_grads(range(1)))
    layers = [early, later]

    def spread(group, start, size):
        return jnp.stack([one[group][:, start : start + size] for one in layers]).astype(F32)

    def small_rows(kind, row):
        early_rows = rows_small[kind, 0][row]
        later_rows = functools.reduce(
            jnp.add, [rows_small[kind, step][row] for step in range(1, passes)]
        )
        return [early_rows, later_rows]

    packed = jnp.stack(
        small_rows("entry", 0)
        + small_rows("entry", 1)
        + small_rows("middle", 0)
        + small_rows("middle", 1)
        + [rows_small["entry", step][2] for step in range(passes)]
    )
    for axis in ("section", "dp"):
        bits = 1
        while bits < lax.axis_size(axis):
            packed = packed + lax.ppermute(packed, axis, xor_pairs(axis, bits))
            bits *= 2
    return (
        passes_out,
        grad_inputs,
        spread(0, hidden_width, head_width),
        spread(2, 0, head_width),
        spread(2, head_width, head_width),
        spread(1, hidden_width, head_width),
        spread(0, 0, hidden_width),
        spread(1, 0, hidden_width),
        packed[0:2],
        packed[2:4],
        packed[4:6],
        packed[6:8],
        packed[8:],
    )


def solution(mesh):
    weight = P(None, None, "tensor")
    return jax.shard_map(
        shards,
        mesh=mesh,
        in_specs=(
            P("dp", "tensor", "section"),
            P("dp"),
            weight,
            weight,
            weight,
            weight,
            weight,
            weight,
            P(),
            P(),
            P(),
            P(),
            P(),
            P("section", "dp", "tensor", None),
        ),
        out_specs=(
            P("section", "dp", "tensor", None),
            P("dp", "tensor", "section"),
            weight,
            weight,
            weight,
            weight,
            weight,
            weight,
            P(),
            P(),
            P(),
            P(),
            P(),
        ),
        check_vma=False,
    )
```

time: 2510 us -> 677 us (0.27)
  waiting for transfers between devices: 1240 us -> 160 us
  matrix products: 395 us -> 13 us
  local copies, waits for them, and re-layouts: 366 us -> 101 us
  other arithmetic: 304 us -> 82.6 us
  starting transfers between devices: 62.2 us -> 217 us
  blocking collectives: 92.9 us -> 0 us
  Pallas kernels: 0 us -> 83.9 us
    psum x1 -> x0, waiting for transfers between devices: 712 us -> none  [shards(): lax.psum((by_slot(accum[0]), by_slot(accum[1]), by_slot(accum[2]), by_slo...]
    dot_general x150 -> x12, matrix products: 395 us -> 13 us  [dot(): return lax.dot_general(left, right, dims, preferred_element_type=F32)]
    ppermute x24 -> x130, waiting for transfers between devices: 471 us -> 160 us  [the longest x12 57.8 us: widen(): other = lax.ppermute(buffer, axis, xor_pairs(axis, bits))]
    ppermute x24 -> x130, starting transfers between devices: 61.5 us -> 217 us  [the longest x18 90.8 us: line_reduce(): up = lax.ppermute(send_up, axis, [(i, i + 1) for i in range(step)])]
    dynamic_slice x105 -> x25, local copies, waits for them, and re-layouts: 126 us -> 12 us  [the longest x9 6.49 us: pick(): return lax.dynamic_index_in_dim(stacked, index, 0, keepdims=False)]
    reduce_sum x84 -> x0, other arithmetic: 90.7 us -> none  [the longest x24 23.1 us: layer_norm(): spread = jnp.mean(centred * centred, axis=-1, keepdims=True)]
    pallas_call x0 -> x17, Pallas kernels: none -> 83.9 us  [call(): pl.pallas_call(body, out_shape=tuple((jax.ShapeDtypeStruct(shape, kind) f...]
    reshape x48 -> x0, local copies, waits for them, and re-layouts: 76.8 us -> none  [the longest x12 22.3 us: attend_backward(): grad_value_heads.reshape(slot_count, row_count, width)]
  transfers between devices with their start and end apart: 51 -> 130, of which waited for: 26 -> 40; matrix products, arithmetic and copies ran while one was open for 19% -> 17% of each run, Pallas kernels for 0% -> 8%
where the time goes in v1:
time: 677 us; the launch traced here: 664 us
  starting transfers between devices  217 us (32%)
  waiting for transfers between devices  160 us (24%)
  local copies, waits for them, and re-layouts  101 us (15%)
  Pallas kernels  83.9 us (12%)
  other arithmetic  82.6 us (12%)
  matrix products  13 us (2%)
  between operations  7.14 us (1%)
    ppermute x18, starting transfers between devices, line_reduce(): up = lax.ppermute(send_up, axis, [(i, i + 1) for i in range(step)])  90.8 us
    pallas_call x17, Pallas kernels, call(): pl.pallas_call(body, out_shape=tuple((jax.ShapeDtypeStruct(shape, kind) f...  83.9 us
    unnamed x415, local copies, waits for them, and re-layouts  66.2 us
    ppermute x12, waiting for transfers between devices, widen(): other = lax.ppermute(buffer, axis, xor_pairs(axis, bits))  57.8 us
    ppermute x18, starting transfers between devices, line_gather(): lax.ppermute(up, axis, [(i, i + 1) for i in range(step - 1, count - 1)])  34.8 us
    concatenate x12, other arithmetic, widen(): ring = jnp.concatenate([other, buffer, other], axis=0)  31.6 us
    ppermute x18, waiting for transfers between devices, line_reduce(): lax.ppermute(send_down, axis, [(count - 1 - i, count - 2 - i) for i in ra...  28.4 us
    ppermute x18, starting transfers between devices, line_gather(): lax.ppermute(down, axis, [(count - 1 - i, count - 2 - i) for i in range(s...  23.4 us
  transfers between devices with their start and end apart: 130, of which 40 were waited for; matrix products, arithmetic and copies ran while one was open for 17% of the time, Pallas kernels for 8%

profile of v1, /device:TPU:0, one launch (start us, length us, event | category | flops | bytes accessed | tf_op | source)
XLA Modules:
  0.0 664.1 jit_solution(15845573530840567211)
XLA Ops:
  1.8 3.0 collective-permute-start
  7.9 3.2 collective-permute-done.2
  25.7 4.4 shard_map.237
  37.3 3.8 shard_map.238
  54.5 6.0 shard_map.239
  67.8 3.1 shard_map.240
  75.4 5.7 shard_map.241
  95.3 6.1 shard_map.243
  104.2 3.1 shard_map.244
  109.8 4.9 shard_map.245
  137.5 9.5 %shard_map.246 = (f32[256,768]{1,0:T(8,128)S(1)}, bf16[256,768]{1,0:T(8,128)(2,1)S(1)}, bf16[256,384]{1,0:T(8,128)(2,1)S(1)}, bf16[256,384]{1,0:T(8,128)(2,1)S(1...) custom-call(f32[256,768]{1,0:T(8,128)S(1)} %copy-done.116, ...), custom_call_target="tpu_custom_call" | custom-call | flops 2617245696 | bytes 2359296 | tf_op jit(solution)/shard_map/pallas_call | solution.py:290
  151.0 4.6 shard_map.247
  160.1 8.8 %shard_map.248 = (f32[256,768]{1,0:T(8,128)S(1)}, bf16[256,768]{1,0:T(8,128)(2,1)S(1)}, bf16[256,384]{1,0:T(8,128)(2,1)S(1)}, bf16[256,384]{1,0:T(8,128)(2,1)S(1...) custom-call(f32[256,768]{1,0:T(8,128)S(1)} %get-tuple-element.172.re, ...), custom_call_target="tpu_custom_call" | custom-call | flops 2113929216 | bytes 2359296 | tf_op jit(solution)/shard_map/pallas_call | solution.py:290
  169.3 7.7 %collective-permute-done.13 = f32[128,768]{1,0:T(8,128)S(1)} collective-permute-done((f32[128,768]{1,0:T(8,128)S(1)}, f32[128,768]{1,0:T(8,128)S(1)}, u32[]{:S(2)}, u32[]{:S(2)}) %collective-permute-start.13) | collective-permute-done | bytes 393248 | tf_op jit(solution)/shard_map/ppermute | solution.py:417
  179.6 4.6 shard_map.249
  184.3 3.4 convolution_convert_fusion
  187.8 3.4 convolution_convert_fusion.2
  191.3 6.4 shard_map.250
  200.7 3.6 collective-permute-start.78
  213.8 4.3 collective-permute-start.79
  218.9 4.8 shard_map.251
  227.1 8.0 %collective-permute-start.80 = (bf16[192,768]{0,1:T(8,128)(2,1)S(1)}, bf16[192,768]{0,1:T(8,128)(2,1)S(1)}, u32[]{:S(2)}, u32[]{:S(2)}) collective-permute-start(bf16[192,768]{0,1:T(8,128)(2,1)S(1)} %get-tuple-element.285), channel_id=1, source_target_pairs={{0,8},{8,16},{16,24},{1,9},{9,17},{17,25},{2,10},{10,18},{18,26},{... | collective-permute-start | bytes 884744 | tf_op jit(solution)/shard_map/ppermute | solution.py:348
  236.5 4.6 shard_map.252
  242.8 5.0 collective-permute-start.62
  254.6 5.0 collective-permute-done.84
  262.2 3.9 collective-permute-done.85
  287.8 4.3 collective-permute-done.128
  293.1 3.3 collective-permute-start.129
  299.9 17.2 %collective-permute-done.87 = bf16[96,768]{0,1:T(8,128)(2,1)S(1)} collective-permute-done((bf16[96,768]{0,1:T(8,128)(2,1)S(1)}, bf16[96,768]{0,1:T(8,128)(2,1)S(1)}, u32[]{:S(2)}, u32[]{:S(2)}) %collective-permute-start.87) | collective-permute-done | bytes 147488 | tf_op jit(solution)/shard_map/ppermute | solution.py:327
  322.4 8.6 %collective-permute-done.67 = bf16[192,768]{0,1:T(8,128)(2,1)S(1)} collective-permute-done((bf16[192,768]{0,1:T(8,128)(2,1)S(1)}, bf16[192,768]{0,1:T(8,128)(2,1)S(1)}, u32[]{:S(2)}, u32[]{:S(2)}) %collective-permute-start.67) | collective-permute-done | bytes 294944 | tf_op jit(solution)/shard_map/ppermute | solution.py:349
  331.0 3.3 collective-permute-start.88
  337.8 5.0 collective-permute-done.68
  346.4 8.5 %collective-permute-done.69 = bf16[48,768]{0,1:T(8,128)(2,1)S(1)} collective-permute-done((bf16[48,768]{0,1:T(8,128)(2,1)S(1)}, bf16[48,768]{0,1:T(8,128)(2,1)S(1)}, u32[]{:S(2)}, u32[]{:S(2)}) %collective-permute-start.69) | collective-permute-done | bytes 73760 | tf_op jit(solution)/shard_map/ppermute | solution.py:323
  363.8 5.9 collective-permute-done.71
  375.3 5.1 concatenate.145
  380.4 2.9 dynamic-slice_bitcast_fusion
  383.3 7.3 %collective-permute-start.72 = (bf16[192,768]{0,1:T(8,128)(2,1)}, bf16[192,768]{0,1:T(8,128)(2,1)S(1)}, u32[]{:S(2)}, u32[]{:S(2)}) collective-permute-start(bf16[192,768]{0,1:T(8,128)(2,1)} %fusion.72), channel_id=1, source_target_pairs={{0,8},{8,16},{16,24},{1,9},{9,17},{17,25},{2,10},{10,18},{18,26},{... | collective-permute-start | bytes 884744 | tf_op jit(solution)/shard_map/ppermute | solution.py:363
  392.0 5.9 collective-permute-start.112
  402.8 3.5 collective-permute-start.48
  411.3 4.4 collective-permute-start.113
  420.3 6.8 %collective-permute-start.114 = (bf16[48,1920]{1,0:T(8,128)(2,1)S(1)}, bf16[48,1920]{1,0:T(8,128)(2,1)S(1)}, u32[]{:S(2)}, u32[]{:S(2)}) collective-permute-start(bf16[48,1920]{1,0:T(8,128)(2,1)S(1)} %get-tuple-element.303), channel_id=1, source_target_pairs={{0,8},{8,16},{16,24},{1,9},{9,17},{17,25},{2,10},{10,18},{18,26},{... | collective-permute-start | bytes 552968 | tf_op jit(solution)/shard_map/ppermute | solution.py:348
  430.1 15.8 %collective-permute-start.50 = (bf16[48,1920]{1,0:T(8,128)(2,1)S(1)}, bf16[48,1920]{1,0:T(8,128)(2,1)S(1)}, u32[]{:S(2)}, u32[]{:S(2)}) collective-permute-start(bf16[48,1920]{1,0:T(8,128)(2,1)S(1)} %get-tuple-element.311), channel_id=1, source_target_pairs={{0,8},{8,16},{16,24},{1,9},{9,17},{17,25},{2,10},{10,18},{18,26},{... | collective-permute-start | bytes 552968 | tf_op jit(solution)/shard_map/ppermute | solution.py:348
  445.8 3.5 collective-permute-done.117
  452.9 4.8 collective-permute-done.53
  459.0 4.0 collective-permute-done.77
  467.2 5.1 concatenate.139
  474.2 4.6 collective-permute-start.54
  485.7 4.4 collective-permute-start.32
  493.1 4.4 collective-permute-start.97
  501.6 9.7 %collective-permute-start.33 = (bf16[48,1920]{1,0:T(8,128)(2,1)S(1)}, bf16[48,1920]{1,0:T(8,128)(2,1)S(1)}, u32[]{:S(2)}, u32[]{:S(2)}) collective-permute-start(bf16[48,1920]{1,0:T(8,128)(2,1)S(1)} %add_convert_fusion.41), channel_id=1, source_target_pairs={{0,8},{8,16},{1,9},{9,17},{2,10},{10,18},{3,11},{11,19},{4,12},{12... | collective-permute-start | bytes 552968 | tf_op jit(solution)/shard_map/ppermute | solution.py:348
  515.4 4.6 collective-permute-start.98
  531.2 11.4 %collective-permute-done.101 = bf16[48,1920]{1,0:T(8,128)(2,1)S(1)} collective-permute-done((bf16[48,1920]{1,0:T(8,128)(2,1)S(1)}, bf16[48,1920]{1,0:T(8,128)(2,1)S(1)}, u32[]{:S(2)}, u32[]{:S(2)}) %collective-permute-start.101) | collective-permute-done | bytes 184352 | tf_op jit(solution)/shard_map/ppermute | solution.py:349
  543.9 4.9 collective-permute-start.102
  550.2 4.6 collective-permute-start.38
  558.9 3.4 collective-permute-done.106
  564.4 3.7 collective-permute-done.42
  588.4 3.0 copy.36
  597.5 28.0 %collective-permute-done.44 = bf16[192,1920]{1,0:T(8,128)(2,1)} collective-permute-done((bf16[192,1920]{1,0:T(8,128)(2,1)}, bf16[192,1920]{1,0:T(8,128)(2,1)}, u32[]{:S(2)}, u32[]{:S(2)}) %collective-permute-start.44) | collective-permute-done | bytes 737312 | tf_op jit(solution)/shard_map/ppermute | solution.py:327
  630.4 4.6 fusion.1
  635.1 4.6 fusion.5
  641.3 4.1 fusion.3
  647.7 3.8 fusion.7
  654.9 4.4 maximum_convert_fusion
  659.3 4.4 maximum_convert_fusion.1
  (775 shorter events, 288.6 us)
Async XLA Ops:
  44.1 17.5 %collective-permute-start.15 = (f32[128,768]{1,0:T(8,128)}, f32[128,768]{1,0:T(8,128)}, u32[]{:S(2)}, u32[]{:S(2)}) collective-permute-start(f32[128,768]{1,0:T(8,128)} %get-tuple-element.292), channel_id=1, source_target_pairs={{0,2},{2,0},{4,6},{6,4},{1,3},{3,1},{5,7},{7,5},{8,10},{10,8},{12,... | collective-permute-start | bytes 1179656 | tf_op jit(solution)/shard_map/ppermute | solution.py:417
  45.5 18.5 %collective-permute-start.17 = (f32[128,768]{1,0:T(8,128)}, f32[128,768]{1,0:T(8,128)}, u32[]{:S(2)}, u32[]{:S(2)}) collective-permute-start(f32[128,768]{1,0:T(8,128)} %get-tuple-element.293), channel_id=1, source_target_pairs={{0,6},{2,4},{4,2},{6,0},{1,7},{3,5},{5,3},{7,1},{8,14},{10,12},{12... | collective-permute-start | bytes 1179656 | tf_op jit(solution)/shard_map/ppermute | solution.py:417
  46.1 19.3 %collective-permute-start.16 = (f32[128,768]{1,0:T(8,128)}, f32[128,768]{1,0:T(8,128)}, u32[]{:S(2)}, u32[]{:S(2)}) collective-permute-start(f32[128,768]{1,0:T(8,128)} %get-tuple-element.294), channel_id=1, source_target_pairs={{0,4},{2,6},{4,0},{6,2},{1,5},{3,7},{5,1},{7,3},{8,12},{10,14},{12... | collective-permute-start | bytes 1179656 | tf_op jit(solution)/shard_map/ppermute | solution.py:417
  67.2 34.5 %collective-permute-start.18 = (f32[4,128,768]{2,1,0:T(8,128)S(1)}, f32[4,128,768]{2,1,0:T(8,128)S(1)}, u32[]{:S(2)}, u32[]{:S(2)}) collective-permute-start(f32[4,128,768]{2,1,0:T(8,128)S(1)} %pad_maximum_fusion.3), channel_id=1, source_target_pairs={{0,1},{1,0},{2,3},{3,2},{4,5},{5,4},{6,7},{7,6},{8,9},{9,8},{10,11... | collective-permute-start | bytes 4718600 | tf_op jit(solution)/shard_map/ppermute | solution.py:304
  120.5 28.8 %collective-permute-start.11 = (bf16[256,768]{1,0:T(8,128)(2,1)}, bf16[256,768]{1,0:T(8,128)(2,1)S(1)}, u32[]{:S(2)}, u32[]{:S(2)}) collective-permute-start(bf16[256,768]{1,0:T(8,128)(2,1)} %copy-done.96), channel_id=1, source_target_pairs={{0,1},{1,0},{2,3},{3,2},{4,5},{5,4},{6,7},{7,6},{8,9},{9,8},{10,11... | collective-permute-start | bytes 1179656 | tf_op jit(solution)/shard_map/ppermute | solution.py:304
  156.3 13.0 %collective-permute-start.14 = (f32[128,768]{1,0:T(8,128)S(1)}, f32[128,768]{1,0:T(8,128)S(1)}, u32[]{:S(2)}, u32[]{:S(2)}) collective-permute-start(f32[128,768]{1,0:T(8,128)S(1)} %get-tuple-element.276), channel_id=1, source_target_pairs={{0,6},{2,4},{4,2},{6,0},{1,7},{3,5},{5,3},{7,1},{8,14},{10,12},{12... | collective-permute-start | bytes 1179656 | tf_op jit(solution)/shard_map/ppermute | solution.py:417
  158.8 18.2 %collective-permute-start.13 = (f32[128,768]{1,0:T(8,128)S(1)}, f32[128,768]{1,0:T(8,128)S(1)}, u32[]{:S(2)}, u32[]{:S(2)}) collective-permute-start(f32[128,768]{1,0:T(8,128)S(1)} %get-tuple-element.277), channel_id=1, source_target_pairs={{0,4},{2,6},{4,0},{6,2},{1,5},{3,7},{5,1},{7,3},{8,12},{10,14},{12... | collective-permute-start | bytes 1179656 | tf_op jit(solution)/shard_map/ppermute | solution.py:417
  159.4 17.7 %collective-permute-start.12 = (f32[128,768]{1,0:T(8,128)S(1)}, f32[128,768]{1,0:T(8,128)S(1)}, u32[]{:S(2)}, u32[]{:S(2)}) collective-permute-start(f32[128,768]{1,0:T(8,128)S(1)} %get-tuple-element.278), channel_id=1, source_target_pairs={{0,2},{2,0},{4,6},{6,4},{1,3},{3,1},{5,7},{7,5},{8,10},{10,8},{12,... | collective-permute-start | bytes 1179656 | tf_op jit(solution)/shard_map/ppermute | solution.py:417
  197.7 21.1 %collective-permute-start.24 = (bf16[256,768]{1,0:T(8,128)(2,1)S(1)}, bf16[256,768]{1,0:T(8,128)(2,1)S(1)}, u32[]{:S(2)}, u32[]{:S(2)}) collective-permute-start(bf16[256,768]{1,0:T(8,128)(2,1)S(1)} %get-tuple-element.188.refs_2_), channel_id=1, source_target_pairs={{0,1},{1,0},{2,3},{3,2},{4,5},{5,4},{6,7},{7,6},{8,9},{9,8},{10,11... | collective-permute-start | bytes 1179656 | tf_op jit(solution)/shard_map/ppermute | solution.py:304
  208.0 126.9 %collective-permute-start.110 = (bf16[384,1920]{1,0:T(8,128)(2,1)}, bf16[384,1920]{1,0:T(8,128)(2,1)}, u32[]{:S(2)}, u32[]{:S(2)}) collective-permute-start(bf16[384,1920]{1,0:T(8,128)(2,1)} %fusion.26), channel_id=1, source_target_pairs={{0,4},{2,6},{4,0},{6,2},{1,5},{3,7},{5,1},{7,3},{8,12},{10,14},{12... | collective-permute-start | bytes 4423688 | tf_op jit(solution)/shard_map/ppermute | solution.py:323
  213.8 12.4 %collective-permute-start.79 = (bf16[192,768]{0,1:T(8,128)(2,1)S(1)}, bf16[192,768]{0,1:T(8,128)(2,1)S(1)}, u32[]{:S(2)}, u32[]{:S(2)}) collective-permute-start(bf16[192,768]{0,1:T(8,128)(2,1)S(1)} %get-tuple-element.287), channel_id=1, source_target_pairs={{0,8},{8,16},{1,9},{9,17},{2,10},{10,18},{3,11},{11,19},{4,12},{12... | collective-permute-start | bytes 884744 | tf_op jit(solution)/shard_map/ppermute | solution.py:348
  223.7 12.7 %collective-permute-start.25 = (bf16[256,768]{1,0:T(8,128)(2,1)S(1)}, bf16[256,768]{1,0:T(8,128)(2,1)S(1)}, u32[]{:S(2)}, u32[]{:S(2)}) collective-permute-start(bf16[256,768]{1,0:T(8,128)(2,1)S(1)} %get-tuple-element.191.refs_1_), channel_id=1, source_target_pairs={{0,1},{1,0},{2,3},{3,2},{4,5},{5,4},{6,7},{7,6},{8,9},{9,8},{10,11... | collective-permute-start | bytes 1179656 | tf_op jit(solution)/shard_map/ppermute | solution.py:304
  227.1 24.1 %collective-permute-start.80 = (bf16[192,768]{0,1:T(8,128)(2,1)S(1)}, bf16[192,768]{0,1:T(8,128)(2,1)S(1)}, u32[]{:S(2)}, u32[]{:S(2)}) collective-permute-start(bf16[192,768]{0,1:T(8,128)(2,1)S(1)} %get-tuple-element.285), channel_id=1, source_target_pairs={{0,8},{8,16},{16,24},{1,9},{9,17},{17,25},{2,10},{10,18},{18,26},{... | collective-permute-start | bytes 884744 | tf_op jit(solution)/shard_map/ppermute | solution.py:348
  235.1 16.8 %collective-permute-start.83 = (bf16[192,768]{0,1:T(8,128)(2,1)S(1)}, bf16[192,768]{0,1:T(8,128)(2,1)S(1)}, u32[]{:S(2)}, u32[]{:S(2)}) collective-permute-start(bf16[192,768]{0,1:T(8,128)(2,1)S(1)} %get-tuple-element.286), channel_id=1, source_target_pairs={{24,16},{16,8},{8,0},{25,17},{17,9},{9,1},{26,18},{18,10},{10,2},{... | collective-permute-start | bytes 884744 | tf_op jit(solution)/shard_map/ppermute | solution.py:349
  241.1 26.6 %collective-permute-start.26 = (bf16[256,768]{1,0:T(8,128)(2,1)S(1)}, bf16[256,768]{1,0:T(8,128)(2,1)S(1)}, u32[]{:S(2)}, u32[]{:S(2)}) collective-permute-start(bf16[256,768]{1,0:T(8,128)(2,1)S(1)} %get-tuple-element.197.own_ref), channel_id=1, source_target_pairs={{0,1},{1,0},{2,3},{3,2},{4,5},{5,4},{6,7},{7,6},{8,9},{9,8},{10,11... | collective-permute-start | bytes 1179656 | tf_op jit(solution)/shard_map/ppermute | solution.py:304
  242.8 18.5 %collective-permute-start.62 = (bf16[192,768]{0,1:T(8,128)(2,1)S(1)}, bf16[192,768]{0,1:T(8,128)(2,1)S(1)}, u32[]{:S(2)}, u32[]{:S(2)}) collective-permute-start(bf16[192,768]{0,1:T(8,128)(2,1)S(1)} %get-tuple-element.283), channel_id=1, source_target_pairs={{0,8},{1,9},{2,10},{3,11},{4,12},{5,13},{6,14},{7,15}} | collective-permute-start | bytes 884744 | tf_op jit(solution)/shard_map/ppermute | solution.py:348
  281.5 74.3 %collective-permute-start.46 = (bf16[384,1920]{1,0:T(8,128)(2,1)}, bf16[384,1920]{1,0:T(8,128)(2,1)}, u32[]{:S(2)}, u32[]{:S(2)}) collective-permute-start(bf16[384,1920]{1,0:T(8,128)(2,1)} %fusion.30), channel_id=1, source_target_pairs={{0,2},{2,0},{4,6},{6,4},{1,3},{3,1},{5,7},{7,5},{8,10},{10,8},{12,... | collective-permute-start | bytes 4423688 | tf_op jit(solution)/shard_map/ppermute | solution.py:323
  292.1 25.0 %collective-permute-start.87 = (bf16[96,768]{0,1:T(8,128)(2,1)S(1)}, bf16[96,768]{0,1:T(8,128)(2,1)S(1)}, u32[]{:S(2)}, u32[]{:S(2)}) collective-permute-start(bf16[96,768]{0,1:T(8,128)(2,1)S(1)} %fusion.89), channel_id=1, source_target_pairs={{0,2},{2,0},{4,6},{6,4},{1,3},{3,1},{5,7},{7,5},{8,10},{10,8},{12,... | collective-permute-start | bytes 442376 | tf_op jit(solution)/shard_map/ppermute | solution.py:327
  293.1 25.8 %collective-permute-start.129 = (f32[12,768]{1,0:T(8,128)S(1)}, f32[12,768]{1,0:T(8,128)S(1)}, u32[]{:S(2)}, u32[]{:S(2)}) collective-permute-start(f32[12,768]{1,0:T(8,128)S(1)} %add.568), channel_id=1, source_target_pairs={{0,16},{8,24},{16,0},{24,8},{1,17},{9,25},{17,1},{25,9},{2,18},{10... | collective-permute-start | bytes 110600 | tf_op jit(solution)/shard_map/ppermute | solution.py:632
  298.4 22.7 %collective-permute-start.64 = (bf16[192,768]{0,1:T(8,128)(2,1)S(1)}, bf16[192,768]{0,1:T(8,128)(2,1)S(1)}, u32[]{:S(2)}, u32[]{:S(2)}) collective-permute-start(bf16[192,768]{0,1:T(8,128)(2,1)S(1)} %get-tuple-element.279), channel_id=1, source_target_pairs={{0,8},{8,16},{16,24},{1,9},{9,17},{17,25},{2,10},{10,18},{18,26},{... | collective-permute-start | bytes 884744 | tf_op jit(solution)/shard_map/ppermute | solution.py:348
  317.1 13.9 %collective-permute-start.67 = (bf16[192,768]{0,1:T(8,128)(2,1)S(1)}, bf16[192,768]{0,1:T(8,128)(2,1)S(1)}, u32[]{:S(2)}, u32[]{:S(2)}) collective-permute-start(bf16[192,768]{0,1:T(8,128)(2,1)S(1)} %get-tuple-element.280), channel_id=1, source_target_pairs={{24,16},{16,8},{8,0},{25,17},{17,9},{9,1},{26,18},{18,10},{10,2},{... | collective-permute-start | bytes 884744 | tf_op jit(solution)/shard_map/ppermute | solution.py:349
  319.0 80.3 %collective-permute-start.94 = (bf16[384,1920]{1,0:T(8,128)(2,1)}, bf16[384,1920]{1,0:T(8,128)(2,1)}, u32[]{:S(2)}, u32[]{:S(2)}) collective-permute-start(bf16[384,1920]{1,0:T(8,128)(2,1)} %fusion.28), channel_id=1, source_target_pairs={{0,4},{2,6},{4,0},{6,2},{1,5},{3,7},{5,1},{7,3},{8,12},{10,14},{12... | collective-permute-start | bytes 4423688 | tf_op jit(solution)/shard_map/ppermute | solution.py:323
  321.1 23.6 %collective-permute-start.91 = (bf16[192,768]{0,1:T(8,128)(2,1)S(1)}, bf16[192,768]{0,1:T(8,128)(2,1)S(1)}, u32[]{:S(2)}, u32[]{:S(2)}) collective-permute-start(bf16[192,768]{0,1:T(8,128)(2,1)S(1)} %fusion.70), channel_id=1, source_target_pairs={{24,16},{16,8},{8,0},{25,17},{17,9},{9,1},{26,18},{18,10},{10,2},{... | collective-permute-start | bytes 884744 | tf_op jit(solution)/shard_map/ppermute | solution.py:364
  331.0 14.1 %collective-permute-start.88 = (bf16[192,768]{0,1:T(8,128)(2,1)S(1)}, bf16[192,768]{0,1:T(8,128)(2,1)S(1)}, u32[]{:S(2)}, u32[]{:S(2)}) collective-permute-start(bf16[192,768]{0,1:T(8,128)(2,1)S(1)} %fusion.70), channel_id=1, source_target_pairs={{0,8},{8,16},{16,24},{1,9},{9,17},{17,25},{2,10},{10,18},{18,26},{... | collective-permute-start | bytes 884744 | tf_op jit(solution)/shard_map/ppermute | solution.py:363
  344.7 38.6 %collective-permute-start.111 = (bf16[192,1920]{1,0:T(8,128)(2,1)}, bf16[192,1920]{1,0:T(8,128)(2,1)}, u32[]{:S(2)}, u32[]{:S(2)}) collective-permute-start(bf16[192,1920]{1,0:T(8,128)(2,1)} %constant_dynamic-slice_fusion.3), channel_id=1, source_target_pairs={{0,2},{2,0},{4,6},{6,4},{1,3},{3,1},{5,7},{7,5},{8,10},{10,8},{12,... | collective-permute-start | bytes 2211848 | tf_op jit(solution)/shard_map/ppermute | solution.py:323
  345.1 13.3 %collective-permute-start.92 = (bf16[192,768]{0,1:T(8,128)(2,1)S(1)}, bf16[192,768]{0,1:T(8,128)(2,1)S(1)}, u32[]{:S(2)}, u32[]{:S(2)}) collective-permute-start(bf16[192,768]{0,1:T(8,128)(2,1)S(1)} %collective-permute-done.91), channel_id=1, source_target_pairs={{16,8},{8,0},{17,9},{9,1},{18,10},{10,2},{19,11},{11,3},{20,12},{1... | collective-permute-start | bytes 884744 | tf_op jit(solution)/shard_map/ppermute | solution.py:364
  358.5 13.5 %collective-permute-start.93 = (bf16[192,768]{0,1:T(8,128)(2,1)S(1)}, bf16[192,768]{0,1:T(8,128)(2,1)S(1)}, u32[]{:S(2)}, u32[]{:S(2)}) collective-permute-start(bf16[192,768]{0,1:T(8,128)(2,1)S(1)} %collective-permute-done.92), channel_id=1, source_target_pairs={{8,0},{9,1},{10,2},{11,3},{12,4},{13,5},{14,6},{15,7}} | collective-permute-start | bytes 884744 | tf_op jit(solution)/shard_map/ppermute | solution.py:364
  359.8 13.3 %collective-permute-start.90 = (bf16[192,768]{0,1:T(8,128)(2,1)S(1)}, bf16[192,768]{0,1:T(8,128)(2,1)S(1)}, u32[]{:S(2)}, u32[]{:S(2)}) collective-permute-start(bf16[192,768]{0,1:T(8,128)(2,1)S(1)} %collective-permute-done.89), channel_id=1, source_target_pairs={{16,24},{17,25},{18,26},{19,27},{20,28},{21,29},{22,30},{23,31}} | collective-permute-start | bytes 884744 | tf_op jit(solution)/shard_map/ppermute | solution.py:363
  369.7 33.1 %collective-permute-start.30 = (bf16[384,1920]{1,0:T(8,128)(2,1)}, bf16[384,1920]{1,0:T(8,128)(2,1)}, u32[]{:S(2)}, u32[]{:S(2)}) collective-permute-start(bf16[384,1920]{1,0:T(8,128)(2,1)} %fusion.32), channel_id=1, source_target_pairs={{0,2},{2,0},{4,6},{6,4},{1,3},{3,1},{5,7},{7,5},{8,10},{10,8},{12,... | collective-permute-start | bytes 4423688 | tf_op jit(solution)/shard_map/ppermute | solution.py:323
  372.0 20.0 %collective-permute-start.47 = (bf16[192,1920]{1,0:T(8,128)(2,1)}, bf16[192,1920]{1,0:T(8,128)(2,1)}, u32[]{:S(2)}, u32[]{:S(2)}) collective-permute-start(bf16[192,1920]{1,0:T(8,128)(2,1)} %constant_dynamic-slice_fusion.15), channel_id=1, source_target_pairs={{0,4},{2,6},{4,0},{6,2},{1,5},{3,7},{5,1},{7,3},{8,12},{10,14},{12... | collective-permute-start | bytes 2211848 | tf_op jit(solution)/shard_map/ppermute | solution.py:323
  373.8 42.0 %collective-permute-start.75 = (bf16[192,768]{0,1:T(8,128)(2,1)}, bf16[192,768]{0,1:T(8,128)(2,1)}, u32[]{:S(2)}, u32[]{:S(2)}) collective-permute-start(bf16[192,768]{0,1:T(8,128)(2,1)} %fusion.72), channel_id=1, source_target_pairs={{24,16},{16,8},{8,0},{25,17},{17,9},{9,1},{26,18},{18,10},{10,2},{... | collective-permute-start | bytes 884744 | tf_op jit(solution)/shard_map/ppermute | solution.py:364
  383.3 34.4 %collective-permute-start.72 = (bf16[192,768]{0,1:T(8,128)(2,1)}, bf16[192,768]{0,1:T(8,128)(2,1)S(1)}, u32[]{:S(2)}, u32[]{:S(2)}) collective-permute-start(bf16[192,768]{0,1:T(8,128)(2,1)} %fusion.72), channel_id=1, source_target_pairs={{0,8},{8,16},{16,24},{1,9},{9,17},{17,25},{2,10},{10,18},{18,26},{... | collective-permute-start | bytes 884744 | tf_op jit(solution)/shard_map/ppermute | solution.py:363
  392.0 17.0 %collective-permute-start.112 = (bf16[48,1920]{1,0:T(8,128)(2,1)S(1)}, bf16[48,1920]{1,0:T(8,128)(2,1)S(1)}, u32[]{:S(2)}, u32[]{:S(2)}) collective-permute-start(bf16[48,1920]{1,0:T(8,128)(2,1)S(1)} %get-tuple-element.305), channel_id=1, source_target_pairs={{0,8},{1,9},{2,10},{3,11},{4,12},{5,13},{6,14},{7,15}} | collective-permute-start | bytes 552968 | tf_op jit(solution)/shard_map/ppermute | solution.py:348
  399.2 16.5 %collective-permute-start.115 = (bf16[48,1920]{1,0:T(8,128)(2,1)S(1)}, bf16[48,1920]{1,0:T(8,128)(2,1)S(1)}, u32[]{:S(2)}, u32[]{:S(2)}) collective-permute-start(bf16[48,1920]{1,0:T(8,128)(2,1)S(1)} %get-tuple-element.306), channel_id=1, source_target_pairs={{24,16},{25,17},{26,18},{27,19},{28,20},{29,21},{30,22},{31,23}} | collective-permute-start | bytes 552968 | tf_op jit(solution)/shard_map/ppermute | solution.py:349
  415.7 58.4 %collective-permute-start.95 = (bf16[192,1920]{1,0:T(8,128)(2,1)}, bf16[192,1920]{1,0:T(8,128)(2,1)}, u32[]{:S(2)}, u32[]{:S(2)}) collective-permute-start(bf16[192,1920]{1,0:T(8,128)(2,1)} %constant_dynamic-slice_fusion.7), channel_id=1, source_target_pairs={{0,2},{2,0},{4,6},{6,4},{1,3},{3,1},{5,7},{7,5},{8,10},{10,8},{12,... | collective-permute-start | bytes 2211848 | tf_op jit(solution)/shard_map/ppermute | solution.py:323
  417.8 33.0 %collective-permute-start.76 = (bf16[192,768]{0,1:T(8,128)(2,1)}, bf16[192,768]{0,1:T(8,128)(2,1)S(1)}, u32[]{:S(2)}, u32[]{:S(2)}) collective-permute-start(bf16[192,768]{0,1:T(8,128)(2,1)} %collective-permute-done.75), channel_id=1, source_target_pairs={{16,8},{8,0},{17,9},{9,1},{18,10},{10,2},{19,11},{11,3},{20,12},{1... | collective-permute-start | bytes 884744 | tf_op jit(solution)/shard_map/ppermute | solution.py:364
  419.5 31.3 %collective-permute-start.73 = (bf16[192,768]{0,1:T(8,128)(2,1)S(1)}, bf16[192,768]{0,1:T(8,128)(2,1)S(1)}, u32[]{:S(2)}, u32[]{:S(2)}) collective-permute-start(bf16[192,768]{0,1:T(8,128)(2,1)S(1)} %collective-permute-done.72), channel_id=1, source_target_pairs={{8,16},{16,24},{9,17},{17,25},{10,18},{18,26},{11,19},{19,27},{12,... | collective-permute-start | bytes 884744 | tf_op jit(solution)/shard_map/ppermute | solution.py:363
  428.6 20.8 %collective-permute-start.117 = (bf16[48,1920]{1,0:T(8,128)(2,1)S(1)}, bf16[48,1920]{1,0:T(8,128)(2,1)S(1)}, u32[]{:S(2)}, u32[]{:S(2)}) collective-permute-start(bf16[48,1920]{1,0:T(8,128)(2,1)S(1)} %add_convert_fusion.23), channel_id=1, source_target_pairs={{24,16},{16,8},{8,0},{25,17},{17,9},{9,1},{26,18},{18,10},{10,2},{... | collective-permute-start | bytes 552968 | tf_op jit(solution)/shard_map/ppermute | solution.py:349
  430.1 22.1 %collective-permute-start.50 = (bf16[48,1920]{1,0:T(8,128)(2,1)S(1)}, bf16[48,1920]{1,0:T(8,128)(2,1)S(1)}, u32[]{:S(2)}, u32[]{:S(2)}) collective-permute-start(bf16[48,1920]{1,0:T(8,128)(2,1)S(1)} %get-tuple-element.311), channel_id=1, source_target_pairs={{0,8},{8,16},{16,24},{1,9},{9,17},{17,25},{2,10},{10,18},{18,26},{... | collective-permute-start | bytes 552968 | tf_op jit(solution)/shard_map/ppermute | solution.py:348
  450.8 29.3 %collective-permute-start.31 = (bf16[192,1920]{1,0:T(8,128)(2,1)}, bf16[192,1920]{1,0:T(8,128)(2,1)}, u32[]{:S(2)}, u32[]{:S(2)}) collective-permute-start(bf16[192,1920]{1,0:T(8,128)(2,1)} %constant_dynamic-slice_fusion.19), channel_id=1, source_target_pairs={{0,4},{2,6},{4,0},{6,2},{1,5},{3,7},{5,1},{7,3},{8,12},{10,14},{12... | collective-permute-start | bytes 2211848 | tf_op jit(solution)/shard_map/ppermute | solution.py:323
  452.2 12.9 %collective-permute-start.74 = (bf16[192,768]{0,1:T(8,128)(2,1)S(1)}, bf16[192,768]{0,1:T(8,128)(2,1)S(1)}, u32[]{:S(2)}, u32[]{:S(2)}) collective-permute-start(bf16[192,768]{0,1:T(8,128)(2,1)S(1)} %collective-permute-done.73), channel_id=1, source_target_pairs={{16,24},{17,25},{18,26},{19,27},{20,28},{21,29},{22,30},{23,31}} | collective-permute-start | bytes 884744 | tf_op jit(solution)/shard_map/ppermute | solution.py:363
  457.6 32.5 %collective-permute-start.121 = (bf16[48,1920]{1,0:T(8,128)(2,1)S(1)}, bf16[48,1920]{1,0:T(8,128)(2,1)}, u32[]{:S(2)}, u32[]{:S(2)}) collective-permute-start(bf16[48,1920]{1,0:T(8,128)(2,1)S(1)} %add_convert_fusion.22), channel_id=1, source_target_pairs={{24,16},{16,8},{8,0},{25,17},{17,9},{9,1},{26,18},{18,10},{10,2},{... | collective-permute-start | bytes 552968 | tf_op jit(solution)/shard_map/ppermute | solution.py:364
  463.0 27.9 %collective-permute-start.118 = (bf16[48,1920]{1,0:T(8,128)(2,1)S(1)}, bf16[48,1920]{1,0:T(8,128)(2,1)}, u32[]{:S(2)}, u32[]{:S(2)}) collective-permute-start(bf16[48,1920]{1,0:T(8,128)(2,1)S(1)} %add_convert_fusion.22), channel_id=1, source_target_pairs={{0,8},{8,16},{16,24},{1,9},{9,17},{17,25},{2,10},{10,18},{18,26},{... | collective-permute-start | bytes 552968 | tf_op jit(solution)/shard_map/ppermute | solution.py:363
  465.9 31.7 %collective-permute-start.57 = (bf16[48,1920]{1,0:T(8,128)(2,1)S(1)}, bf16[48,1920]{1,0:T(8,128)(2,1)S(1)}, u32[]{:S(2)}, u32[]{:S(2)}) collective-permute-start(bf16[48,1920]{1,0:T(8,128)(2,1)S(1)} %add_convert_fusion.32), channel_id=1, source_target_pairs={{24,16},{16,8},{8,0},{25,17},{17,9},{9,1},{26,18},{18,10},{10,2},{... | collective-permute-start | bytes 552968 | tf_op jit(solution)/shard_map/ppermute | solution.py:364
  474.2 24.7 %collective-permute-start.54 = (bf16[48,1920]{1,0:T(8,128)(2,1)S(1)}, bf16[48,1920]{1,0:T(8,128)(2,1)S(1)}, u32[]{:S(2)}, u32[]{:S(2)}) collective-permute-start(bf16[48,1920]{1,0:T(8,128)(2,1)S(1)} %add_convert_fusion.32), channel_id=1, source_target_pairs={{0,8},{8,16},{16,24},{1,9},{9,17},{17,25},{2,10},{10,18},{18,26},{... | collective-permute-start | bytes 552968 | tf_op jit(solution)/shard_map/ppermute | solution.py:363
  497.6 13.8 %collective-permute-start.122 = (bf16[48,1920]{1,0:T(8,128)(2,1)}, bf16[48,1920]{1,0:T(8,128)(2,1)S(1)}, u32[]{:S(2)}, u32[]{:S(2)}) collective-permute-start(bf16[48,1920]{1,0:T(8,128)(2,1)} %collective-permute-done.121), channel_id=1, source_target_pairs={{16,8},{8,0},{17,9},{9,1},{18,10},{10,2},{19,11},{11,3},{20,12},{1... | collective-permute-start | bytes 552968 | tf_op jit(solution)/shard_map/ppermute | solution.py:364
  498.9 13.8 %collective-permute-start.119 = (bf16[48,1920]{1,0:T(8,128)(2,1)}, bf16[48,1920]{1,0:T(8,128)(2,1)S(1)}, u32[]{:S(2)}, u32[]{:S(2)}) collective-permute-start(bf16[48,1920]{1,0:T(8,128)(2,1)} %collective-permute-done.118), channel_id=1, source_target_pairs={{8,16},{16,24},{9,17},{17,25},{10,18},{18,26},{11,19},{19,27},{12,... | collective-permute-start | bytes 552968 | tf_op jit(solution)/shard_map/ppermute | solution.py:363
  499.6 13.8 %collective-permute-start.58 = (bf16[48,1920]{1,0:T(8,128)(2,1)S(1)}, bf16[48,1920]{1,0:T(8,128)(2,1)S(1)}, u32[]{:S(2)}, u32[]{:S(2)}) collective-permute-start(bf16[48,1920]{1,0:T(8,128)(2,1)S(1)} %collective-permute-done.57), channel_id=1, source_target_pairs={{16,8},{8,0},{17,9},{9,1},{18,10},{10,2},{19,11},{11,3},{20,12},{1... | collective-permute-start | bytes 552968 | tf_op jit(solution)/shard_map/ppermute | solution.py:364
  500.9 13.8 %collective-permute-start.55 = (bf16[48,1920]{1,0:T(8,128)(2,1)S(1)}, bf16[48,1920]{1,0:T(8,128)(2,1)S(1)}, u32[]{:S(2)}, u32[]{:S(2)}) collective-permute-start(bf16[48,1920]{1,0:T(8,128)(2,1)S(1)} %collective-permute-done.54), channel_id=1, source_target_pairs={{8,16},{16,24},{9,17},{17,25},{10,18},{18,26},{11,19},{19,27},{12,... | collective-permute-start | bytes 552968 | tf_op jit(solution)/shard_map/ppermute | solution.py:363
  501.6 13.8 %collective-permute-start.33 = (bf16[48,1920]{1,0:T(8,128)(2,1)S(1)}, bf16[48,1920]{1,0:T(8,128)(2,1)S(1)}, u32[]{:S(2)}, u32[]{:S(2)}) collective-permute-start(bf16[48,1920]{1,0:T(8,128)(2,1)S(1)} %add_convert_fusion.41), channel_id=1, source_target_pairs={{0,8},{8,16},{1,9},{9,17},{2,10},{10,18},{3,11},{11,19},{4,12},{12... | collective-permute-start | bytes 552968 | tf_op jit(solution)/shard_map/ppermute | solution.py:348
  511.4 14.0 %collective-permute-start.123 = (bf16[48,1920]{1,0:T(8,128)(2,1)S(1)}, bf16[48,1920]{1,0:T(8,128)(2,1)S(1)}, u32[]{:S(2)}, u32[]{:S(2)}) collective-permute-start(bf16[48,1920]{1,0:T(8,128)(2,1)S(1)} %collective-permute-done.122), channel_id=1, source_target_pairs={{8,0},{9,1},{10,2},{11,3},{12,4},{13,5},{14,6},{15,7}} | collective-permute-start | bytes 552968 | tf_op jit(solution)/shard_map/ppermute | solution.py:364
  513.4 36.8 %collective-permute-start.59 = (bf16[48,1920]{1,0:T(8,128)(2,1)S(1)}, bf16[48,1920]{1,0:T(8,128)(2,1)S(1)}, u32[]{:S(2)}, u32[]{:S(2)}) collective-permute-start(bf16[48,1920]{1,0:T(8,128)(2,1)S(1)} %collective-permute-done.58), channel_id=1, source_target_pairs={{8,0},{9,1},{10,2},{11,3},{12,4},{13,5},{14,6},{15,7}} | collective-permute-start | bytes 552968 | tf_op jit(solution)/shard_map/ppermute | solution.py:364
  515.4 14.4 %collective-permute-start.98 = (bf16[48,1920]{1,0:T(8,128)(2,1)S(1)}, bf16[48,1920]{1,0:T(8,128)(2,1)S(1)}, u32[]{:S(2)}, u32[]{:S(2)}) collective-permute-start(bf16[48,1920]{1,0:T(8,128)(2,1)S(1)} %get-tuple-element.299), channel_id=1, source_target_pairs={{0,8},{8,16},{16,24},{1,9},{9,17},{17,25},{2,10},{10,18},{18,26},{... | collective-permute-start | bytes 552968 | tf_op jit(solution)/shard_map/ppermute | solution.py:348
  521.8 22.1 %collective-permute-start.34 = (bf16[48,1920]{1,0:T(8,128)(2,1)S(1)}, bf16[48,1920]{1,0:T(8,128)(2,1)S(1)}, u32[]{:S(2)}, u32[]{:S(2)}) collective-permute-start(bf16[48,1920]{1,0:T(8,128)(2,1)S(1)} %get-tuple-element.307), channel_id=1, source_target_pairs={{0,8},{8,16},{16,24},{1,9},{9,17},{17,25},{2,10},{10,18},{18,26},{... | collective-permute-start | bytes 552968 | tf_op jit(solution)/shard_map/ppermute | solution.py:348
  526.3 43.8 %collective-permute-start.124 = (bf16[192,1920]{1,0:T(8,128)(2,1)S(1)}, bf16[192,1920]{1,0:T(8,128)(2,1)S(1)}, u32[]{:S(2)}, u32[]{:S(2)}) collective-permute-start(bf16[192,1920]{1,0:T(8,128)(2,1)S(1)} %constant_dynamic-slice_fusion), channel_id=1, source_target_pairs={{0,2},{2,0},{4,6},{6,4},{1,3},{3,1},{5,7},{7,5},{8,10},{10,8},{12,... | collective-permute-start | bytes 2211848 | tf_op jit(solution)/shard_map/ppermute | solution.py:327
  528.5 14.1 %collective-permute-start.101 = (bf16[48,1920]{1,0:T(8,128)(2,1)S(1)}, bf16[48,1920]{1,0:T(8,128)(2,1)S(1)}, u32[]{:S(2)}, u32[]{:S(2)}) collective-permute-start(bf16[48,1920]{1,0:T(8,128)(2,1)S(1)} %add_convert_fusion.28), channel_id=1, source_target_pairs={{24,16},{16,8},{8,0},{25,17},{17,9},{9,1},{26,18},{18,10},{10,2},{... | collective-permute-start | bytes 552968 | tf_op jit(solution)/shard_map/ppermute | solution.py:349
  529.9 19.0 %collective-permute-start.37 = (bf16[48,1920]{1,0:T(8,128)(2,1)S(1)}, bf16[48,1920]{1,0:T(8,128)(2,1)S(1)}, u32[]{:S(2)}, u32[]{:S(2)}) collective-permute-start(bf16[48,1920]{1,0:T(8,128)(2,1)S(1)} %add_convert_fusion.38), channel_id=1, source_target_pairs={{24,16},{16,8},{8,0},{25,17},{17,9},{9,1},{26,18},{18,10},{10,2},{... | collective-permute-start | bytes 552968 | tf_op jit(solution)/shard_map/ppermute | solution.py:349
  562.3 19.4 %collective-permute-start.60 = (bf16[192,1920]{1,0:T(8,128)(2,1)S(1)}, bf16[192,1920]{1,0:T(8,128)(2,1)S(1)}, u32[]{:S(2)}, u32[]{:S(2)}) collective-permute-start(bf16[192,1920]{1,0:T(8,128)(2,1)S(1)} %constant_dynamic-slice_fusion.12), channel_id=1, source_target_pairs={{0,4},{2,6},{4,0},{6,2},{1,5},{3,7},{5,1},{7,3},{8,12},{10,14},{12... | collective-permute-start | bytes 2211848 | tf_op jit(solution)/shard_map/ppermute | solution.py:327
  573.7 56.6 %collective-permute-start.125 = (bf16[384,1920]{1,0:T(8,128)(2,1)}, bf16[384,1920]{1,0:T(8,128)(2,1)}, u32[]{:S(2)}, u32[]{:S(2)}) collective-permute-start(bf16[384,1920]{1,0:T(8,128)(2,1)} %fusion.19), channel_id=1, source_target_pairs={{0,4},{2,6},{4,0},{6,2},{1,5},{3,7},{5,1},{7,3},{8,12},{10,14},{12... | collective-permute-start | bytes 4423688 | tf_op jit(solution)/shard_map/ppermute | solution.py:327
  574.8 18.8 %collective-permute-start.108 = (bf16[192,1920]{1,0:T(8,128)(2,1)S(1)}, bf16[192,1920]{1,0:T(8,128)(2,1)}, u32[]{:S(2)}, u32[]{:S(2)}) collective-permute-start(bf16[192,1920]{1,0:T(8,128)(2,1)S(1)} %constant_dynamic-slice_fusion.4), channel_id=1, source_target_pairs={{0,2},{2,0},{4,6},{6,4},{1,3},{3,1},{5,7},{7,5},{8,10},{10,8},{12,... | collective-permute-start | bytes 2211848 | tf_op jit(solution)/shard_map/ppermute | solution.py:327
  578.6 46.9 %collective-permute-start.44 = (bf16[192,1920]{1,0:T(8,128)(2,1)}, bf16[192,1920]{1,0:T(8,128)(2,1)}, u32[]{:S(2)}, u32[]{:S(2)}) collective-permute-start(bf16[192,1920]{1,0:T(8,128)(2,1)} %constant_dynamic-slice_fusion.16), channel_id=1, source_target_pairs={{0,4},{2,6},{4,0},{6,2},{1,5},{3,7},{5,1},{7,3},{8,12},{10,14},{12... | collective-permute-start | bytes 2211848 | tf_op jit(solution)/shard_map/ppermute | solution.py:327
  584.6 50.5 %collective-permute-start.61 = (bf16[384,1920]{1,0:T(8,128)(2,1)}, bf16[384,1920]{1,0:T(8,128)(2,1)}, u32[]{:S(2)}, u32[]{:S(2)}) collective-permute-start(bf16[384,1920]{1,0:T(8,128)(2,1)} %fusion.23), channel_id=1, source_target_pairs={{0,2},{2,0},{4,6},{6,4},{1,3},{3,1},{5,7},{7,5},{8,10},{10,8},{12,... | collective-permute-start | bytes 4423688 | tf_op jit(solution)/shard_map/ppermute | solution.py:327
  596.1 45.1 %collective-permute-start.109 = (bf16[384,1920]{1,0:T(8,128)(2,1)S(1)}, bf16[384,1920]{1,0:T(8,128)(2,1)S(1)}, u32[]{:S(2)}, u32[]{:S(2)}) collective-permute-start(bf16[384,1920]{1,0:T(8,128)(2,1)S(1)} %fusion.21), channel_id=1, source_target_pairs={{0,4},{2,6},{4,0},{6,2},{1,5},{3,7},{5,1},{7,3},{8,12},{10,14},{12... | collective-permute-start | bytes 4423688 | tf_op jit(solution)/shard_map/ppermute | solution.py:327
  628.2 19.5 %collective-permute-start.45 = (bf16[384,1920]{1,0:T(8,128)(2,1)S(1)}, bf16[384,1920]{1,0:T(8,128)(2,1)S(1)}, u32[]{:S(2)}, u32[]{:S(2)}) collective-permute-start(bf16[384,1920]{1,0:T(8,128)(2,1)S(1)} %fusion.25), channel_id=1, source_target_pairs={{0,2},{2,0},{4,6},{6,4},{1,3},{3,1},{5,7},{7,5},{8,10},{10,8},{12,... | collective-permute-start | bytes 4423688 | tf_op jit(solution)/shard_map/ppermute | solution.py:327
  (259 other events, 1458.5 us)

commit v2 on v1

v2 whole, which is shorter than its diff:
```python
import functools

import jax
import jax.numpy as jnp
from jax import lax
from jax.experimental import pallas as pl
from jax.experimental.pallas import tpu as pltpu
from jax.sharding import PartitionSpec as P

HEADS = 12
EPSILON = 1e-05
MASKED = -1e30
F32 = jnp.float32
BF16 = jnp.bfloat16
ROOT = 0.7978845608028654
CUBIC = 0.044715
NN = (((1,), (0,)), ((), ()))
NT = (((1,), (1,)), ((), ()))
TN = (((0,), (0,)), ((), ()))


def dot(left, right, dims=NN):
    return lax.dot_general(left, right, dims, preferred_element_type=F32)


def norm_parts(rows):
    centred = rows - jnp.mean(rows, axis=-1, keepdims=True)
    spread = jnp.mean(centred * centred, axis=-1, keepdims=True)
    inverse = lax.rsqrt(spread + EPSILON)
    return centred * inverse, inverse


def norm_back(rows, gain, grad):
    normal, inverse = norm_parts(rows)
    scaled = gain * grad
    middle = jnp.mean(scaled, axis=-1, keepdims=True)
    along = jnp.mean(scaled * normal, axis=-1, keepdims=True)
    back = inverse * (scaled - middle - normal * along)
    gain_sum = jnp.sum(grad * normal, axis=0, keepdims=True)
    bias_sum = jnp.sum(grad, axis=0, keepdims=True)
    return back, gain_sum, bias_sum


def both(own, other):
    return own[...].astype(F32) + other[...].astype(F32)


class Incoming:
    def __init__(self, source, place, sem):
        self.copy = pltpu.make_async_copy(source, place, sem)
        self.copy.start()
        self.place = place
        self.waiting = True

    def ref(self):
        if self.waiting:
            self.copy.wait()
            self.waiting = False
        return self.place

    def __getitem__(self, index):
        return self.ref()[index]


class Outgoing:
    def __init__(self, place, target, sem):
        self.place = place
        self.copy = pltpu.make_async_copy(place, target, sem)

    def put(self, value):
        self.place[...] = value
        self.copy.start()

    def __getitem__(self, index):
        return self.place[index]

    def __setitem__(self, index, value):
        self.place[index] = value


class Chosen:
    def __init__(self, array, index):
        self.array, self.index = array, index


class Near:
    def __init__(self, array):
        self.array = array


class Held:
    def __init__(self, name, *index):
        self.name, self.index = name, index


class Raw:
    def __init__(self, array):
        self.array = array


class Scalars:
    def __init__(self, array):
        self.array = array


class Mover:
    def __init__(self, sems):
        self.sems, self.used = sems, 0

    def start(self, source, target):
        copy = pltpu.make_async_copy(source, target, self.sems.at[self.used])
        self.used += 1
        copy.start()
        return copy


class Order:
    def __init__(self, shapes):
        self.shapes = shapes
        self.stores = {}

    def call(self, body, operands, outs, scratch=(), limit=26, moves=0, update=None):
        kind = lambda one: one[2] if isinstance(one, tuple) and len(one) > 2 else "staged"
        plain = lambda one: not isinstance(one, (Near, Raw, Scalars))
        names = ["order"] + [one.name for one in operands + outs if isinstance(one, Held)]
        names = list(dict.fromkeys(names))
        old = [name for name in names if name in self.stores]
        new = [name for name in names if name not in self.stores]
        given = [one for one in operands if not isinstance(one, Held)]
        made = [one for one in outs if not isinstance(one, Held)]
        arrays = [one.array if isinstance(one, (Chosen, Near, Raw, Scalars)) else one for one in given]

        def shape_of(one):
            if isinstance(one, Held):
                shape, dtype = self.shapes[one.name]
                for index in one.index:
                    if isinstance(index, int):
                        shape = shape[1:]
                    else:
                        sizes = [
                            cut.stop - cut.start if isinstance(cut, slice) else cut for cut in index
                        ]
                        shape = tuple(sizes) + tuple(shape[len(sizes) :])
                return shape, dtype
            if isinstance(one, Chosen):
                return one.array.shape[1:], one.array.dtype
            if isinstance(one, tuple):
                return one[0], one[1]
            return one.shape, one.dtype

        places = [pltpu.VMEM(*shape_of(one)) for one in operands if plain(one)]
        places += [pltpu.VMEM(*shape_of(one)) for one in outs if kind(one) == "staged"]
        first_out = len(old) + len(given)
        total = first_out + len(names) + len(made)
        count = len(places)

        def part(stores, one):
            ref = stores[one.name]
            for index in one.index:
                ref = ref.at[index]
            return ref

        def kernel(*refs):
            in_refs = list(refs[len(old) : first_out])
            stores = dict(zip(old + new, refs[first_out : first_out + len(names)]))
            out_refs = list(refs[first_out + len(names) : total])
            rooms = refs[total : total + count]
            sems, more = refs[total + count], refs[total + count + 1]
            rest = refs[total + count + 2 :]
            ins, results = [], []
            at = 0
            for one in operands:
                ref = part(stores, one) if isinstance(one, Held) else in_refs.pop(0)
                if plain(one):
                    source = ref.at[one.index] if isinstance(one, Chosen) else ref
                    ins.append(Incoming(source, rooms[at], sems.at[at]))
                    at += 1
                else:
                    ins.append(ref)
            for one in outs:
                ref = part(stores, one) if isinstance(one, Held) else out_refs.pop(0)
                if kind(one) == "staged":
                    results.append(Outgoing(rooms[at], ref, sems.at[at]))
                    at += 1
                else:
                    results.append(ref)
            extra = (Mover(more),) if moves else ()
            body(ins, results, *extra, *rest)
            for one in ins:
                if isinstance(one, Incoming):
                    one.ref()
            for one in results:
                if isinstance(one, Outgoing):
                    one.copy.wait()

        anywhere = pl.BlockSpec(memory_space=pl.ANY)
        inside = pl.BlockSpec(memory_space=pltpu.VMEM)
        scalar = pl.BlockSpec(memory_space=pltpu.SMEM)
        spec = lambda one: inside if isinstance(one, Near) else scalar if isinstance(one, Scalars) else anywhere
        aliases = {at: at for at in range(len(old))}
        for out_at, in_at in (update or {}).items():
            shift_in = sum(isinstance(one, Held) for one in operands[:in_at])
            shift_out = sum(isinstance(one, Held) for one in outs[:out_at])
            aliases[len(old) + in_at - shift_in] = len(names) + out_at - shift_out
        shapes = [pltpu.HBM(*self.shapes[name]) for name in old + new]
        for one in made:
            form = pltpu.VMEM if kind(one) == "near" else jax.ShapeDtypeStruct
            shapes.append(form(one[0], one[1]))
        arrays = [
            pltpu.with_memory_space_constraint(array, pltpu.VMEM)
            if isinstance(one, Near)
            else pltpu.with_memory_space_constraint(array, pltpu.HBM)
            if isinstance(one, Chosen)
            else array
            for one, array in zip(given, arrays)
        ]
        done = pl.pallas_call(
            kernel,
            out_shape=tuple(shapes),
            in_specs=[anywhere] * len(old) + [spec(one) for one in given],
            out_specs=(anywhere,) * len(names)
            + tuple(inside if kind(one) == "near" else anywhere for one in made),
            scratch_shapes=places
            + [pltpu.SemaphoreType.DMA((max(count, 1),)), pltpu.SemaphoreType.DMA((max(moves, 1),))]
            + list(scratch),
            input_output_aliases=aliases,
            compiler_params=pltpu.CompilerParams(vmem_limit_bytes=int(limit * 1024 * 1024)),
            cost_estimate=pl.CostEstimate(flops=1000, bytes_accessed=1000, transcendentals=0),
        )(
            *[pltpu.with_memory_space_constraint(self.stores[name], pltpu.HBM) for name in old],
            *arrays,
        )
        self.stores.update(zip(old + new, done[: len(names)]))
        return done[len(names) :]


class Place:
    def __getitem__(self, slot):
        name, bits = slot
        return (lax.axis_index(name) // bits) % 2 if bits else lax.axis_index(name)


HERE = Place()


def causal_mask(length):
    key_place = lax.broadcasted_iota(jnp.int32, (length, length), 0)
    query_place = lax.broadcasted_iota(jnp.int32, (length, length), 1)
    return key_place <= query_place


def lane_half(half, pair):
    lane = lax.broadcasted_iota(jnp.int32, pair.shape, 1)
    keep = (lane < 64) if half == 0 else (lane >= 64)
    return jnp.where(keep, pair, jnp.zeros_like(pair))


def attention_forward(step, layer, ins, outs, mover, turned, *rest):
    count = 2 if step == 0 else 3
    first, (embed, gain, bias, wq, wk, wv, wo) = ins[:count], ins[count : count + 7]
    past_k, past_vt = ins[count + 7 : count + 7 + step], ins[count + 7 + step : count + 7 + 2 * step]
    sent = None
    if step == 0:
        own_t, other_t = first
        (entry_v,) = rest
        half = own_t.shape[1]
        place = pl.multiple_of(lax.axis_index("tensor") * half, half)
        entry_v[pl.ds(place, half), :] = own_t[...].T
        entry_v[pl.ds(pl.multiple_of(half - place, half), half), :] = other_t[...].T
        entered = entry_v[...] + embed[0:1, :]
    else:
        near_r, own, other = first
        (entry_v,) = rest
        result = near_r[...] + both(own, other)
        entry_v[...] = result
        half = entry_v.shape[0] // 2
        place = pl.multiple_of(lax.axis_index("tensor") * half, half)
        sent = mover.start(entry_v.at[pl.ds(place, half)], outs[0].at[step - 1])
        outs = outs[1:]
        entered = result + embed[step : step + 1, :]
    near_out = outs[0]
    near_out[...] = entered
    outs = outs[1:]
    u_out, a_out, q_out, k_out, kt_out, v_out, vt_out, lse_out, o_out, part_out = outs
    u_out.put(entered)
    normal, _ = norm_parts(entered)
    a = (normal * gain[layer : layer + 1, :] + bias[layer : layer + 1, :]).astype(BF16)
    a_out.put(a)
    q_out.put((dot(a, wq[...]).astype(BF16).astype(F32) * 0.125).astype(BF16))
    k_full = dot(a, wk[...])
    k_out.put(k_full.astype(BF16))
    v_full = dot(a, wv[...])
    vt_out.put(v_full.T.astype(BF16))
    v_out.put(v_full.astype(BF16))
    kt_out.put(k_full.T.astype(BF16))
    length = entered.shape[0]
    seen = causal_mask(length)
    all_k = past_k + [k_out]
    all_vt = past_vt + [vt_out]
    head_count = wq.place.shape[1] // 64
    sums = []
    for head in range(head_count):
        pair, half = divmod(head, 2)
        lanes = slice(128 * pair, 128 * pair + 128)
        query = lane_half(half, q_out[:, lanes])
        scores = [jnp.where(seen, dot(key[:, lanes], query, NT), MASKED) for key in all_k]
        highest = functools.reduce(
            jnp.maximum, [jnp.max(one, axis=0, keepdims=True) for one in scores]
        )
        powers = [jnp.exp(one - highest) for one in scores]
        total = functools.reduce(jnp.add, [jnp.sum(one, axis=0, keepdims=True) for one in powers])
        inverse = 1.0 / total
        sums.append(highest + jnp.log(total))
        rows = slice(64 * head, 64 * head + 64)
        mixed = None
        for power, value in zip(powers, all_vt):
            term = dot(value[rows, :], (power * inverse).astype(BF16))
            mixed = term if mixed is None else mixed + term
        turned[rows, :] = mixed
    o = turned[...].T.astype(BF16)
    part_out[...] = dot(o, wo[...], NT).astype(BF16)
    o_out.put(o)
    if sent is not None:
        sent.wait()
    sums += [jnp.zeros_like(sums[0])] * (8 - len(sums))
    lse_out.put(jnp.concatenate(sums, axis=0))


def gelu_parts(hidden):
    square = hidden * hidden
    bent = jnp.tanh(ROOT * hidden * (1.0 + CUBIC * square))
    return square, bent


def feed_forward(layer, ins, outs):
    own, other, u, gain, bias, wu, wd = ins
    near_out, r_out, b_out, g_out, m_out, part_out = outs
    middle = u[...] + both(own, other)
    near_out[...] = middle
    r_out.put(middle)
    normal, _ = norm_parts(middle)
    b = (normal * gain[layer : layer + 1, :] + bias[layer : layer + 1, :]).astype(BF16)
    b_out.put(b)
    hidden = dot(b, wu[...])
    g_out.put(hidden)
    _, bent = gelu_parts(hidden)
    m = (0.5 * hidden * (1.0 + bent)).astype(BF16)
    m_out.put(m)
    part_out[...] = dot(m, wd[...], NT).astype(BF16)


def small_put(out, rows):
    rows = rows + [jnp.zeros_like(rows[0])] * (8 - len(rows))
    out.put(jnp.concatenate(rows, axis=0))


def feed_backward(step, last, ins, outs, mover, cot_v):
    counts, cot_own, cot_other, wd, g, wu = ins[:6]
    near_out, e_out, dg_out, part_out = outs[:4]
    half = cot_v.shape[0] // 2
    place = pl.multiple_of(lax.axis_index("tensor") * half, half)
    copies = [
        mover.start(cot_own.at[step], cot_v.at[pl.ds(place, half)]),
        mover.start(cot_other.at[step], cot_v.at[pl.ds(pl.multiple_of(half - place, half), half)]),
    ]
    item = lax.axis_index("section")
    own_count = jnp.where(
        item < counts.shape[0], counts[jnp.minimum(item, counts.shape[0] - 1)], 0
    )
    present = jnp.where(own_count > step, 1.0, 0.0).astype(F32)
    if last:
        near_r, own, other, end_v = *ins[6:], outs[5]
        end_v[...] = near_r[...] + both(own, other)
        sent = mover.start(end_v.at[pl.ds(place, half)], outs[4].at[step])
    else:
        own, other, dr, u, gain = ins[6:]
        back, gain_sum, bias_sum = norm_back(u[...], gain[1:2, :], both(own, other))
        entered = dr[...] + back
        small_put(outs[4], [gain_sum, bias_sum, jnp.sum(entered, axis=0, keepdims=True)])
    for copy in copies:
        copy.wait()
    grad = cot_v[...] * present
    if not last:
        grad = grad + entered
    near_out[...] = grad
    e = grad.astype(BF16)
    e_out.put(e)
    raw = dot(e, wd[...])
    hidden = g[...]
    square, bent = gelu_parts(hidden)
    slope = 0.5 * (1.0 + bent) + 0.5 * hidden * (1.0 - bent * bent) * ROOT * (
        1.0 + 3.0 * CUBIC * square
    )
    dg = (raw * slope).astype(BF16)
    dg_out.put(dg)
    part_out[...] = dot(dg, wu[...], NT).astype(BF16)
    if last:
        sent.wait()


def attention_backward(step, layer, last, ins, outs, do_v, dqt_v):
    own, other, dh, r, gain, wo, q, lse = ins[:8]
    count = step + 1
    keys, values, keys_t = ins[8 : 8 + count], ins[8 + count : 8 + 2 * count], ins[8 + 2 * count : 8 + 3 * count]
    rest = ins[8 + 3 * count :]
    if not last:
        dk_in, dv_in = rest[:2]
    wq, wk, wv = rest[-3:]
    near_out, f_out, dq_out, dk_out, dv_out, part_out, small_out = outs[:7]
    if step > 0:
        dk_all, dv_all = outs[7:]
    back, gain_sum, bias_sum = norm_back(r[...], gain[layer : layer + 1, :], both(own, other))
    small_put(small_out, [gain_sum, bias_sum])
    grad = dh[...] + back
    near_out[...] = grad
    f = grad.astype(BF16)
    f_out.put(f)
    do_v[...] = dot(f, wo[...]).astype(BF16)
    length = f.shape[0]
    seen = causal_mask(length)
    head_count = q.place.shape[1] // 64
    for pair in range(head_count // 2):
        lanes = slice(128 * pair, 128 * pair + 128)
        key_sums = [None] * count
        value_sums = [None] * count
        for half in range(2):
            head = 2 * pair + half
            rows = slice(64 * head, 64 * head + 64)
            query = lane_half(half, q[:, lanes])
            grad_mix = lane_half(half, do_v[:, lanes])
            logsum = lse[head : head + 1, :]
            exact = [
                jnp.exp(jnp.where(seen, dot(key[:, lanes], query, NT), MASKED) - logsum)
                for key in keys
            ]
            grad_weights = [dot(value[:, lanes], grad_mix, NT) for value in values]
            delta = functools.reduce(
                jnp.add,
                [jnp.sum(p * dp, axis=0, keepdims=True) for p, dp in zip(exact, grad_weights)],
            )
            query_grad = None
            for slot in range(count):
                grad_scores = (exact[slot] * (grad_weights[slot] - delta)).astype(BF16)
                term = dot(keys_t[slot][rows, :], grad_scores)
                query_grad = term if query_grad is None else query_grad + term
                key_term = dot(grad_scores, query)
                value_term = dot(exact[slot].astype(BF16), grad_mix)
                if half == 0:
                    key_sums[slot] = key_term
                    value_sums[slot] = value_term
                else:
                    key_sums[slot] = key_sums[slot] + key_term
                    value_sums[slot] = value_sums[slot] + value_term
            dqt_v[rows, :] = query_grad
        for slot in range(count):
            key_sum, value_sum = key_sums[slot], value_sums[slot]
            if not last:
                key_sum = key_sum + dk_in[slot, :, lanes]
                value_sum = value_sum + dv_in[slot, :, lanes]
            if slot == step:
                dk_out[:, lanes] = key_sum.astype(BF16)
                dv_out[:, lanes] = value_sum.astype(BF16)
            else:
                dk_all[slot, :, lanes] = key_sum
                dv_all[slot, :, lanes] = value_sum
    dq = (dqt_v[...].T * 0.125).astype(BF16)
    part = dot(dq, wq[...], NT) + dot(dk_out[...], wk[...], NT) + dot(dv_out[...], wv[...], NT)
    part_out[...] = part.astype(BF16)
    dq_out.put(dq)
    for one in (dk_out, dv_out) + ((dk_all, dv_all) if step > 0 else ()):
        one.copy.start()


def entry_backward(ins, outs, entry_v):
    own, other, dr, u, gain = ins
    back, gain_sum, bias_sum = norm_back(u[...], gain[0:1, :], both(own, other))
    entered = dr[...] + back
    entry_v[...] = entered
    half = entry_v.shape[0] // 2
    place = pl.multiple_of(lax.axis_index("tensor") * half, half)
    outs[0].put(entry_v[pl.ds(place, half), :].T)
    small_put(outs[1], [gain_sum, bias_sum, jnp.sum(entered, axis=0, keepdims=True)])


def place_pieces(ins, outs, mover):
    pieces = ins
    rows = pieces[0].shape[0]
    copies = []
    for bits, piece in enumerate(pieces):
        at = pl.multiple_of((lax.axis_index("section") ^ bits) * rows, rows)
        copies.append(mover.start(piece, outs[0].at[pl.ds(at, rows)]))
    for copy in copies:
        copy.wait()


def place_passes(ins, outs, mover, room):
    counts, pieces = ins[0], ins[1:]
    copies = [mover.start(piece, room.at[lax.axis_index("section") ^ bits]) for bits, piece in enumerate(pieces)]
    for copy in copies:
        copy.wait()
    for item in range(outs[0].place.shape[0]):
        outs[0][item] = room[item] * jnp.where(counts[item] > lax.axis_index("section"), 1.0, 0.0).astype(F32)
    outs[0].copy.start()


def place_items(ins, outs, mover, room):
    pieces = ins
    copies = [mover.start(piece, room.at[lax.axis_index("section") ^ bits]) for bits, piece in enumerate(pieces)]
    for copy in copies:
        copy.wait()
    out = mover.start(room.at[pl.ds(0, outs[0].shape[0])], outs[0])
    out.wait()


def pack_small(ins, outs):
    passes = (len(ins)) // 2
    entry, middle = ins[:passes], ins[passes:]
    rows = []
    for kind in (entry, middle):
        for row in range(2):
            rows.append(kind[0][row : row + 1, :])
            later = kind[1][row : row + 1, :]
            for step in range(2, passes):
                later = later + kind[step][row : row + 1, :]
            rows.append(later)
    rows += [entry[step][2:3, :] for step in range(passes)]
    rows += [jnp.zeros_like(rows[0])] * (-len(rows) % 8)
    outs[0].put(jnp.concatenate(rows, axis=0))


def add_small(ins, outs):
    outs[0].put(ins[0][...] + ins[1][...])


def part_small(ins, outs):
    total = ins[0][...] + ins[1][...]
    at = 0
    for out in outs:
        count = out.place.shape[0]
        out.put(total[at : at + count])
        at += count


def halves(slot, room, axis):
    size = room.shape[axis] // 2
    kept = pl.multiple_of(HERE[slot] * size, size)
    sent = pl.multiple_of(size - kept, size)
    if axis == 0:
        return room.at[pl.ds(kept, size)], room.at[pl.ds(sent, size)]
    return room.at[:, pl.ds(kept, size)], room.at[:, pl.ds(sent, size)]


def weight_first(products, splits, ins, outs, mover, *rooms):
    factors = ins
    copies = []
    for at, (room, slot) in enumerate(zip(rooms, splits)):
        column = 0
        for lefts, rights in products[at]:
            total = None
            for left, right in zip(lefts, rights):
                term = dot(factors[left][...], factors[right][...], TN)
                total = term if total is None else total + term
            room[:, column : column + total.shape[1]] = total.astype(BF16)
            column += total.shape[1]
        kept, sent = halves(slot, room, 0)
        copies.append(mover.start(sent, outs[2 * at + 1]))
        copies.append(mover.start(kept, outs[2 * at]))
    for copy in copies:
        copy.wait()


def add_split(slots, axis, ins, outs, mover, *rooms):
    copies = []
    for at, (room, slot) in enumerate(zip(rooms, slots)):
        room[...] = (ins[2 * at][...].astype(F32) + ins[2 * at + 1][...].astype(F32)).astype(BF16)
        kept, sent = halves(slot, room, axis)
        copies.append(mover.start(sent, outs[2 * at + 1]))
        copies.append(mover.start(kept, outs[2 * at]))
    for copy in copies:
        copy.wait()


def add_merge(slot, axis, ins, outs, mover, room):
    columns = room.shape[1] // 2
    for at in range(2):
        total = ins[2 * at][...].astype(F32) + ins[2 * at + 1][...].astype(F32)
        room[:, at * columns : (at + 1) * columns] = total.astype(BF16)
    kept, sent = halves(slot, room, axis)
    copies = [mover.start(sent, outs[1]), mover.start(kept, outs[0])]
    for copy in copies:
        copy.wait()


def add_last(ins, outs):
    outs[0].put((ins[0][...].astype(F32) + ins[1][...].astype(F32)).astype(BF16))


def join(slots, axis, ins, outs, mover):
    copies = []
    for at, slot in enumerate(slots):
        own, other = halves(slot, outs[at], axis)
        copies.append(mover.start(ins[2 * at], own))
        copies.append(mover.start(ins[2 * at + 1], other))
    for copy in copies:
        copy.wait()


def join_part(slot, axis, ins, outs, mover, room):
    own, other = halves(slot, room, axis)
    copies = [mover.start(ins[0], own), mover.start(ins[1], other)]
    for copy in copies:
        copy.wait()
    columns = room.shape[1] // 2
    copies = [mover.start(room.at[:, pl.ds(at * columns, columns)], outs[at]) for at in range(2)]
    for copy in copies:
        copy.wait()


def finish(layer, parts, slots, count, ins, outs, mover, *rooms):
    halves_in = ins[:4]
    copies = []
    out_at = 0
    for at, slot in enumerate(slots):
        rows = halves_in[2 * at].place.shape[0]
        for which in range(2):
            place = HERE[slot] * rows
            place = pl.multiple_of(place if which == 0 else rows - place, rows)
            column = 0
            for part in range(parts):
                room = rooms[2 * (out_at + part) + which]
                columns = room.shape[1]
                room[...] = halves_in[2 * at + which][:, column : column + columns].astype(F32)
                copies.append(
                    mover.start(room, outs[out_at + part].at[layer].at[pl.ds(place, rows)])
                )
                column += columns
        out_at += parts
    for copy in copies:
        copy.wait()


def swap(value):
    return lax.ppermute(value, "tensor", [(0, 1), (1, 0)])


def xor_pairs(axis, bits):
    return [(place, place ^ bits) for place in range(lax.axis_size(axis))]


def pick(stacked, index):
    return lax.dynamic_index_in_dim(stacked, index, 0, keepdims=False)


def schedule(levels):
    sizes = [2.0, 1.0, 2.0, 1.0]
    unit = 13.0
    plan = []
    for size in sizes:
        hop = size * unit
        plan.append(
            [("xy", hop), ("xy", hop / 2)]
            + [("z", hop * 2 * (1 << level) / (4 << level)) for level in range(levels)]
            + [("z", hop * 2 * (1 << level) / (4 << level)) for level in reversed(range(levels))]
            + [("xy", hop / 2), ("xy", hop)]
        )
    order = []
    free = {"xy": plan[0][0][1], "z": 0.0}
    place = [1, 0, 0, 0]
    ready = [plan[0][0][1], 0.0, 0.0, 0.0]
    now = 20.0
    sides = {"small": [levels + 3, 20.0, 6.0], "inputs": [2, 20.0, 12.0]}
    while True:
        options = []
        for group in range(4):
            if place[group] > len(plan[group]):
                continue
            if place[group] == 0 and place[group - 1] < 2:
                continue
            options.append((max(ready[group], now), place[group] == 0, -place[group], group))
        for name, (left, time, gap) in sides.items():
            if left:
                options.append((max(time, now), False, -1, name))
        if not options:
            return order
        start, _, _, name = min(options, key=lambda one: one[:3])
        order.append(name)
        if name in sides:
            now = start + 1.5
            sides[name][0] -= 1
            sides[name][1] = now + sides[name][2]
            continue
        now = start + (5.0 if place[name] == 0 else 2.5)
        if place[name] < len(plan[name]):
            link, cost = plan[name][place[name]]
            free[link] = max(free[link], now) + cost
            ready[name] = free[link] + 2.5
        place[name] += 1


def shards(
    inputs,
    counts,
    w_query,
    w_key,
    w_value,
    w_out,
    w_up,
    w_down,
    gain_one,
    bias_one,
    gain_two,
    bias_two,
    pass_embed,
    cotangent,
):
    section_count = lax.axis_size("section")
    section = lax.axis_index("section")
    tensor = lax.axis_index("tensor")
    batches, half_rows, slice_width = inputs.shape
    length = 2 * half_rows
    width = cotangent.shape[3]
    head_width = w_query.shape[2]
    hidden_width = w_up.shape[2]
    passes = pass_embed.shape[0]
    dp_count = lax.axis_size("dp")
    dp_place = lax.axis_index("dp")
    dp_bits = [1 << level for level in range(dp_count.bit_length() - 1)]
    order = Order(
        {
            "order": ((2, passes, length, head_width), F32),
            "low": ((passes, 4, length, width), BF16),
            "hidden": ((passes, 2, length, hidden_width), BF16),
            "heads": ((passes, 7, length, head_width), BF16),
            "turned": ((passes, 4, head_width, length), BF16),
            "wide": ((passes, 2 * length + 24, width), F32),
            "before": ((passes, length, hidden_width), F32),
        }
    )

    def by_item(stacked, index):
        valid = index < batches
        return jnp.where(valid, pick(stacked, jnp.minimum(index, batches - 1)), 0)

    def exchange(pieces):
        return [pieces[0]] + [
            lax.ppermute(pieces[bits], "section", xor_pairs("section", bits))
            for bits in range(1, section_count)
        ]

    slot_x, slot_y = ("section", 1), ("section", 2)
    slots_dp = [("dp", bits) for bits in dp_bits]

    inputs_t = jnp.swapaxes(inputs, 1, 2)
    got = exchange([by_item(inputs_t, section ^ bits) for bits in range(section_count)])
    (entry_t,) = order.call(
        place_pieces,
        [Raw(one) for one in got],
        [((width, half_rows), F32, "near")],
        moves=section_count,
        limit=8,
    )
    entry_other = swap(entry_t)
    cot_got = exchange([by_item(cotangent[0], section ^ bits) for bits in range(section_count)])

    wide_near = ((length, width), F32, "near")
    part_near = ((length, width), BF16, "near")
    stacked = ((2 * passes, half_rows, width), F32, "raw")
    turned = pltpu.VMEM((head_width, length), F32)
    entry_v = pltpu.VMEM((length, width), F32)
    whole = slice(None)

    def low(step, name):
        return Held("low", step, "abef".index(name))

    def hidden(step, name):
        return Held("hidden", step, ("m", "dg").index(name))

    def heads(step, name):
        return Held("heads", step, ("q", "k", "v", "o", "dq", "dk", "dv").index(name))

    def turn(step, name):
        return Held("turned", step, ("kt", "vt").index(name))

    def rows(step, start, count, columns=None):
        cut = (slice(start, start + count), slice(0, columns or width))
        return Held("wide", step, cut)

    def entered(step):
        return rows(step, 0, length)

    def middle(step):
        return rows(step, length, length)

    def logsum(step):
        return rows(step, 2 * length, 8, length)

    def small_entry(step):
        return rows(step, 2 * length + 8, 8)

    def small_middle(step):
        return rows(step, 2 * length + 16, 8)

    results = None
    resid = None
    cot_own = cot_other = None
    for step in range(passes):
        layer = min(step, 1)
        first = [Near(entry_t), Near(entry_other)] if step == 0 else [Near(one) for one in resid]
        weights = [Chosen(one, layer) for one in (w_query, w_key, w_value, w_out)]
        operands = first + [pass_embed, gain_one, bias_one] + weights
        operands += [heads(past, "k") for past in range(step)]
        operands += [turn(past, "vt") for past in range(step)]
        update = None
        if step > 1:
            operands.append(Raw(results))
            update = {0: len(operands) - 1}
        done = order.call(
            functools.partial(attention_forward, step, layer),
            operands,
            ([] if step == 0 else [stacked])
            + [wide_near, entered(step), low(step, "a"), heads(step, "q"), heads(step, "k")]
            + [turn(step, "kt"), heads(step, "v"), turn(step, "vt"), logsum(step)]
            + [heads(step, "o"), part_near],
            [turned, entry_v],
            moves=1,
            update=update,
        )
        if step > 0:
            results = done[0]
            done = done[1:]
        near_u, part = done
        if step == min(2, passes - 1):
            (cot_flat,) = order.call(
                place_pieces,
                [Raw(one) for one in cot_got],
                [((section_count * half_rows, width), F32, "raw")],
                moves=section_count,
                limit=8,
            )
            cot_own = cot_flat.reshape(section_count, half_rows, width)
            cot_other = swap(cot_own)
        near_r, part_two = order.call(
            functools.partial(feed_forward, layer),
            [Near(part), Near(swap(part)), Near(near_u), gain_two, bias_two]
            + [Chosen(w_up, layer), Chosen(w_down, layer)],
            [wide_near, middle(step), low(step, "b"), Held("before", step), hidden(step, "m"), part_near],
        )
        resid = (near_r, part_two, swap(part_two))

    factors = [
        {name: low(step, name) for name in "abef"}
        | {name: hidden(step, name) for name in ("m", "dg")}
        | {name: heads(step, name) for name in ("o", "dq", "dk", "dv")}
        for step in range(passes)
    ]
    state = None

    def feed_step(step):
        nonlocal results
        layer = min(step, 1)
        last = step == passes - 1
        operands = [Scalars(counts), Raw(cot_own), Raw(cot_other)]
        operands += [Chosen(w_down, layer), Held("before", step), Chosen(w_up, layer)]
        outs = [wide_near, low(step, "e"), hidden(step, "dg"), part_near]
        update = None
        if last:
            operands += [Near(one) for one in resid]
            outs += [stacked, wide_near]
            operands.append(Raw(results))
            update = {4: len(operands) - 1}
        else:
            dr, part, other = state
            operands += [Near(part), Near(other), Near(dr), entered(step + 1), gain_one]
            outs += [small_entry(step + 1)]

        def body(ins, outs, mover, cot_v):
            feed_backward(step, last, ins[:9] if last else ins, outs, mover, cot_v)

        done = order.call(body, operands, outs, [entry_v], moves=3, update=update)
        near_dh, part = done[:2]
        if last:
            results = done[2]
        return near_dh, part, swap(part)

    def attention_step(step, fed):
        layer = min(step, 1)
        last = step == passes - 1
        near_dh, part, other = fed
        operands = [Near(part), Near(other), Near(near_dh), middle(step), gain_two]
        operands += [Chosen(w_out, layer), heads(step, "q"), logsum(step)]
        operands += [heads(past, "k") for past in range(step + 1)]
        operands += [heads(past, "v") for past in range(step + 1)]
        operands += [turn(past, "kt") for past in range(step + 1)]
        cut = (slice(0, step + 1),)
        if not last:
            operands += [Held("order", at, cut) for at in range(2)]
        operands += [Chosen(one, layer) for one in (w_query, w_key, w_value)]
        outs = [wide_near, low(step, "f"), heads(step, "dq"), heads(step, "dk"), heads(step, "dv")]
        outs += [part_near, small_middle(step)]
        if step > 0:
            outs += [Held("order", at, (slice(0, step),)) for at in range(2)]
        near_dr, part = order.call(
            functools.partial(attention_backward, step, layer, last),
            operands,
            outs,
            [pltpu.VMEM((length, head_width), BF16), turned],
        )
        return near_dr, part, swap(part)

    later, early = list(range(1, passes)), [0]
    feed_products = ([("b", "dg")], [("e", "m")])
    heads_products = ([("a", "dq"), ("a", "dk")], [("f", "o"), ("a", "dv")])
    kinds = [(later, feed_products), (later, heads_products), (early, feed_products), (early, heads_products)]
    outputs = {}

    def stages(group):
        steps, products = kinds[group]
        names = sorted({name for pair in products for product in pair for name in product})
        operands, place = [], {}
        for name in names:
            for step in steps:
                place[name, step] = len(operands)
                operands.append(factors[step][name])
        columns = sum(order.shapes[factors[steps[0]][right].name][0][-1] for _, right in products[0])
        numbered = [
            [
                ([place[left, step] for step in steps], [place[right, step] for step in steps])
                for left, right in pair
            ]
            for pair in products
        ]
        room = lambda rows, cols: pltpu.VMEM((rows, cols), BF16)
        raw = lambda rows, cols: ((rows, cols), BF16, "raw")
        send = lambda value, axis, bits: lax.ppermute(value, axis, xor_pairs(axis, bits))
        kept_a, sent_a, kept_b, sent_b = order.call(
            functools.partial(weight_first, numbered, (slot_x, slot_y)),
            operands,
            [raw(width // 2, columns)] * 4,
            [room(width, columns)] * 2,
            moves=4,
            limit=40,
        )
        got_a, got_b = send(sent_a, "section", 1), send(sent_b, "section", 2)
        yield
        kept_a, sent_a, kept_b, sent_b = order.call(
            functools.partial(add_split, (slot_y, slot_x), 0),
            [kept_a, got_a, kept_b, got_b],
            [raw(width // 4, columns)] * 4,
            [room(width // 2, columns)] * 2,
            moves=4,
            limit=30,
        )
        got_a, got_b = send(sent_a, "section", 2), send(sent_b, "section", 1)
        yield
        shape = [width // 4, 2 * columns]
        axes = []
        for level, bits in enumerate(dp_bits):
            axis = 0 if shape[0] % 32 == 0 else 1
            axes.append(axis)
            before = tuple(shape)
            shape[axis] //= 2
            if level == 0:
                own, sent = order.call(
                    functools.partial(add_merge, slots_dp[level], axis),
                    [kept_a, got_a, kept_b, got_b],
                    [raw(*shape)] * 2,
                    [room(*before)],
                    moves=2,
                    limit=24,
                )
            else:
                own, sent = order.call(
                    functools.partial(add_split, (slots_dp[level],), axis),
                    [own, got],
                    [raw(*shape)] * 2,
                    [room(*before)],
                    moves=2,
                    limit=16,
                )
            got = send(sent, "dp", bits)
            yield
        (own,) = order.call(add_last, [own, got], [(tuple(shape), BF16)], limit=16)
        got = send(own, "dp", dp_bits[-1])
        yield
        for level in reversed(range(len(dp_bits))):
            axis = axes[level]
            shape[axis] *= 2
            if level > 0:
                (own,) = order.call(
                    functools.partial(join, (slots_dp[level],), axis),
                    [Raw(own), Raw(got)],
                    [raw(*shape)],
                    moves=2,
                    limit=16,
                )
                got = send(own, "dp", dp_bits[level - 1])
                yield
        own_a, own_b = order.call(
            functools.partial(join_part, slots_dp[0], axes[0]),
            [Raw(own), Raw(got)],
            [raw(width // 4, columns)] * 2,
            [room(*shape)],
            moves=4,
            limit=16,
        )
        got_a, got_b = send(own_a, "section", 2), send(own_b, "section", 1)
        yield
        own_a, own_b = order.call(
            functools.partial(join, (slot_y, slot_x), 0),
            [Raw(own_a), Raw(got_a), Raw(own_b), Raw(got_b)],
            [raw(width // 2, columns)] * 2,
            moves=4,
            limit=16,
        )
        got_a, got_b = send(own_a, "section", 1), send(own_b, "section", 2)
        yield
        parts = len(products[0])
        family, layer = group % 2, 1 - group // 2
        result = ((2, width, columns // parts), F32, "raw")
        before = outputs.get(family)
        done = order.call(
            functools.partial(finish, layer, parts, (slot_x, slot_y), 2 * parts),
            [own_a, got_a, own_b, got_b] + [Raw(one) for one in before or ()],
            [result] * (2 * parts),
            [pltpu.VMEM((width // 2, columns // parts), F32)] * (4 * parts),
            moves=4 * parts,
            limit=40,
            update={at: 4 + at for at in range(2 * parts)} if before else None,
        )
        outputs[family] = done

    def small_stages():
        (packed,) = order.call(
            pack_small,
            [small_entry(step) for step in range(passes)] + [small_middle(step) for step in range(passes)],
            [((-(-(8 + passes) // 8) * 8, width), F32)], limit=8
        )
        hops = [("section", 1), ("section", 2)] + [("dp", bits) for bits in dp_bits]
        for axis, bits in hops[:-1]:
            got = lax.ppermute(packed, axis, xor_pairs(axis, bits))
            yield
            (packed,) = order.call(add_small, [packed, got], [(packed.shape, F32)], limit=8)
        axis, bits = hops[-1]
        got = lax.ppermute(packed, axis, xor_pairs(axis, bits))
        yield
        outputs["small"] = order.call(
            part_small,
            [packed, got],
            [((2, width), F32)] * 4 + [((passes, width), F32)],
            limit=8,
        )

    def input_stages(entered_t):
        pieces = entered_t.reshape(section_count, slice_width, half_rows)
        got = exchange([pick(pieces, section ^ bits) for bits in range(section_count)])
        yield
        (grad_t,) = order.call(
            place_items,
            [Raw(one) for one in got],
            [((batches, slice_width, half_rows), F32, "raw")],
            [pltpu.VMEM((section_count, slice_width, half_rows), F32)],
            moves=section_count + 1,
            limit=8,
        )
        outputs["inputs"] = jnp.swapaxes(grad_t, 1, 2)

    running = {}

    def advance(name):
        if name not in running:
            running[name] = stages(name)
        next(running[name], None)

    for step in reversed(range(1, passes)):
        fed = feed_step(step)
        if step == passes - 1:
            passes_got = exchange([pick(results, section ^ bits) for bits in range(section_count)])
        if step == 1:
            advance(0)
        state = attention_step(step, fed)
        if step == passes - 1:
            (passes_out,) = order.call(
                place_passes,
                [Scalars(counts)] + [Raw(one) for one in passes_got],
                [((batches, half_rows, width), F32)],
                [pltpu.VMEM((section_count, half_rows, width), F32)],
                moves=section_count,
                limit=16,
            )
    fed = feed_step(0)
    state = attention_step(0, fed)
    near_dr, part, other = state
    (entered_t,) = order.call(
        entry_backward,
        [Near(part), Near(other), Near(near_dr), entered(0), gain_one],
        [((width, half_rows), F32), small_entry(0)],
        [entry_v],
    )
    running["small"] = small_stages()
    running["inputs"] = input_stages(entered_t)
    for name in schedule(len(dp_bits)):
        advance(name)
    for name in running:
        for _ in running[name]:
            pass
    up, down = outputs[0]
    query, key, out, value = outputs[1]
    return (
        passes_out[None],
        outputs["inputs"],
        query,
        key,
        value,
        out,
        up,
        down,
        *outputs["small"],
    )


def solution(mesh):
    weight = P(None, None, "tensor")
    return jax.shard_map(
        shards,
        mesh=mesh,
        in_specs=(
            P("dp", "tensor", "section"),
            P("dp"),
            weight,
            weight,
            weight,
            weight,
            weight,
            weight,
            P(),
            P(),
            P(),
            P(),
            P(),
            P("section", "dp", "tensor", None),
        ),
        out_specs=(
            P("section", "dp", "tensor", None),
            P("dp", "tensor", "section"),
            weight,
            weight,
            weight,
            weight,
            weight,
            weight,
            P(),
            P(),
            P(),
            P(),
            P(),
        ),
        check_vma=False,
    )
```

time: 677 us -> 499 us (0.74)
  starting transfers between devices: 217 us -> 93.3 us
  Pallas kernels: 83.9 us -> 191 us
  local copies, waits for them, and re-layouts: 101 us -> 4.85 us
  other arithmetic: 82.6 us -> 1.21 us
  waiting for transfers between devices: 160 us -> 197 us
  matrix products: 13 us -> 0 us
    ppermute x100 -> x52, starting transfers between devices: 199 us -> 75.5 us  [the longest x48 69.6 us: stages(): lax.ppermute(value, axis, xor_pairs(axis, bits))]
    pallas_call x17 -> x62, Pallas kernels: 83.9 us -> 191 us  [call(): pl.pallas_call(kernel, out_shape=tuple(shapes), in_specs=[anywhere] * len...]
    unnamed x415 -> x40, local copies, waits for them, and re-layouts: 66.2 us -> 3.64 us
    concatenate x19 -> x0, other arithmetic: 40.3 us -> none  [the longest x12 31.6 us: widen(): ring = jnp.concatenate([other, buffer, other], axis=0)]
    convert_element_type x39 -> x0, other arithmetic: 33.1 us -> none  [the longest x28 18.4 us: add_low(): return (left.astype(F32) + right.astype(F32)).astype(BF16)]
    ppermute x12, waiting for transfers between devices: 17.8 us -> 38.4 us  [exchange(): lax.ppermute(pieces[bits], 'section', xor_pairs('section', bits))]
    dot_general x12 -> x0, matrix products: 13 us -> none  [dot(): return lax.dot_general(left, right, dims, preferred_element_type=F32)]
    dynamic_slice x25 -> x0, local copies, waits for them, and re-layouts: 12 us -> none  [the longest x9 6.49 us: pick(): return lax.dynamic_index_in_dim(stacked, index, 0, keepdims=False)]
  transfers between devices with their start and end apart: 130 -> 82, of which waited for: 40 -> 48; matrix products, arithmetic and copies ran while one was open for 17% -> 0% of each run, Pallas kernels for 8% -> 24%
where the time goes in v2:
time: 499 us; the launch traced here: 490 us
  waiting for transfers between devices  197 us (39%)
  Pallas kernels  191 us (38%)
  starting transfers between devices  93.3 us (19%)
    pallas_call x62, Pallas kernels, call(): pl.pallas_call(kernel, out_shape=tuple(shapes), in_specs=[anywhere] * len...  191 us
    ppermute x48, waiting for transfers between devices, stages(): lax.ppermute(value, axis, xor_pairs(axis, bits))  122 us
    ppermute x48, starting transfers between devices, stages(): lax.ppermute(value, axis, xor_pairs(axis, bits))  69.6 us
    ppermute x12, waiting for transfers between devices, exchange(): lax.ppermute(pieces[bits], 'section', xor_pairs('section', bits))  38.4 us
    ppermute x4, waiting for transfers between devices, small_stages(): got = lax.ppermute(packed, axis, xor_pairs(axis, bits))  18.7 us
    ppermute x18, waiting for transfers between devices, swap(): return lax.ppermute(value, 'tensor', [(0, 1), (1, 0)])  17.9 us
    ppermute x12, starting transfers between devices, exchange(): lax.ppermute(pieces[bits], 'section', xor_pairs('section', bits))  14.8 us
  transfers between devices with their start and end apart: 82, of which 48 were waited for; matrix products, arithmetic and copies ran while one was open for 0% of the time, Pallas kernels for 24%

profile of v2, /device:TPU:0, one launch (start us, length us, event | category | flops | bytes accessed | tf_op | source)
XLA Modules:
  0.0 489.9 jit_solution(17948900007302250245)
XLA Ops:
  1.8 4.0 collective-permute-start.2
  6.4 2.9 collective-permute-done.2.refs_3_
  15.4 5.5 %shard_map.238 = (f32[2,4,256,384]{3,2,1,0:T(8,128)}, f32[4,536,768]{2,1,0:T(8,128)}, bf16[4,4,256,768]{3,2,1,0:T(8,128)(2,1)}, bf16[4,7,256,384]{3,2,1,0:T(8,12...) custom-call(f32[2,4,256,384]{3,2,1,0:T(8,128)} %get-tuple-element.27, ...), custom_call_target="tpu_custom_call", output_to_operand_aliasing={{0}: (0, {})} | custom-call | flops 1000 | bytes 1000 | tf_op jit(solution)/shard_map/pallas_call | solution.py:217
  22.7 4.9 shard_map.239
  29.4 6.0 %shard_map.240 = (f32[2,4,256,384]{3,2,1,0:T(8,128)}, bf16[4,7,256,384]{3,2,1,0:T(8,128)(2,1)}, bf16[4,4,384,256]{3,2,1,0:T(8,128)(2,1)}, f32[4,536,768]{2,1,0:T...) custom-call(f32[2,4,256,384]{3,2,1,0:T(8,128)} %get-tuple-element.28, ...), custom_call_target="tpu_custom_call", output_to_operand_aliasing={{0}: (0, {}), {1}: (1, {}), {2}: (2, {}), {3}: (3, {}), {4}... | custom-call | flops 1000 | bytes 1000 | tf_op jit(solution)/shard_map/pallas_call | solution.py:217
  37.2 4.7 shard_map.241
  45.9 6.7 %shard_map.242 = (f32[2,4,256,384]{3,2,1,0:T(8,128)}, bf16[4,7,256,384]{3,2,1,0:T(8,128)(2,1)}, bf16[4,4,384,256]{3,2,1,0:T(8,128)(2,1)}, f32[4,536,768]{2,1,0:T...) custom-call(f32[2,4,256,384]{3,2,1,0:T(8,128)} %get-tuple-element.29, ...), custom_call_target="tpu_custom_call", output_to_operand_aliasing={{0}: (0, {}), {1}: (1, {}), {2}: (2, {}), {3}: (3, {}), {4}... | custom-call | flops 1000 | bytes 1000 | tf_op jit(solution)/shard_map/pallas_call | solution.py:217
  52.7 2.6 collective-permute-done.10.refs_4_
  55.3 7.8 %collective-permute-done.8.refs_2_ = f32[128,768]{1,0:T(8,128)S(1)} collective-permute-done((f32[128,768]{1,0:T(8,128)S(1)}, f32[128,768]{1,0:T(8,128)S(1)}, u32[]{:S(2)}, u32[]{:S(2)}) %collective-permute-start.8) | collective-permute-done | bytes 393248 | tf_op jit(solution)/shard_map/ppermute | solution.py:746
  64.0 5.1 %shard_map.244 = (f32[2,4,256,384]{3,2,1,0:T(8,128)}, f32[4,536,768]{2,1,0:T(8,128)}, bf16[4,4,256,768]{3,2,1,0:T(8,128)(2,1)}, f32[4,256,1536]{2,1,0:T(8,128)},...) custom-call(f32[2,4,256,384]{3,2,1,0:T(8,128)} %get-tuple-element.30, ...), custom_call_target="tpu_custom_call", output_to_operand_aliasing={{0}: (0, {}), {1}: (1, {}), {2}: (2, {}), {3}: (3, {}), {4}... | custom-call | flops 1000 | bytes 1000 | tf_op jit(solution)/shard_map/pallas_call | solution.py:217
  70.9 7.4 %shard_map.245 = (f32[2,4,256,384]{3,2,1,0:T(8,128)}, bf16[4,7,256,384]{3,2,1,0:T(8,128)(2,1)}, bf16[4,4,384,256]{3,2,1,0:T(8,128)(2,1)}, f32[4,536,768]{2,1,0:T...) custom-call(f32[2,4,256,384]{3,2,1,0:T(8,128)} %get-tuple-element.31, ...), custom_call_target="tpu_custom_call", output_to_operand_aliasing={{0}: (0, {}), {1}: (1, {}), {2}: (2, {}), {3}: (3, {}), {4}... | custom-call | flops 1000 | bytes 1000 | tf_op jit(solution)/shard_map/pallas_call | solution.py:217
  80.1 16.0 %shard_map.246 = (f32[2,4,256,384]{3,2,1,0:T(8,128)}, f32[4,536,768]{2,1,0:T(8,128)}, bf16[4,4,256,768]{3,2,1,0:T(8,128)(2,1)}, f32[4,256,1536]{2,1,0:T(8,128)},...) custom-call(f32[2,4,256,384]{3,2,1,0:T(8,128)} %get-tuple-element.32, ...), custom_call_target="tpu_custom_call", output_to_operand_aliasing={{0}: (0, {}), {1}: (1, {}), {2}: (2, {}), {3}: (3, {}), {4}... | custom-call | flops 1000 | bytes 1000 | tf_op jit(solution)/shard_map/pallas_call | solution.py:217
  97.9 6.1 %shard_map.247 = (f32[2,4,256,384]{3,2,1,0:T(8,128)}, f32[4,256,1536]{2,1,0:T(8,128)}, bf16[4,4,256,768]{3,2,1,0:T(8,128)(2,1)}, bf16[4,2,256,1536]{3,2,1,0:T(8,...) custom-call(f32[2,4,256,384]{3,2,1,0:T(8,128)} %get-tuple-element.32, ...), custom_call_target="tpu_custom_call", output_to_operand_aliasing={{0}: (0, {}), {1}: (1, {}), {2}: (2, {}), {3}: (3, {}), {6}... | custom-call | flops 1000 | bytes 1000 | tf_op jit(solution)/shard_map/pallas_call | solution.py:217
  108.8 13.3 %shard_map.248 = (f32[2,4,256,384]{3,2,1,0:T(8,128)}, f32[4,536,768]{2,1,0:T(8,128)}, bf16[4,7,256,384]{3,2,1,0:T(8,128)(2,1)}, bf16[4,4,384,256]{3,2,1,0:T(8,12...) custom-call(f32[2,4,256,384]{3,2,1,0:T(8,128)} %get-tuple-element.33, ...), custom_call_target="tpu_custom_call", output_to_operand_aliasing={{0}: (0, {}), {1}: (1, {}), {2}: (2, {}), {3}: (3, {}), {4}... | custom-call | flops 1000 | bytes 1000 | tf_op jit(solution)/shard_map/pallas_call | solution.py:217
  122.2 3.8 collective-permute-done.18.refs_4_
  126.0 2.4 shard_map.249
  128.5 7.4 %shard_map.250 = (f32[2,4,256,384]{3,2,1,0:T(8,128)}, f32[4,256,1536]{2,1,0:T(8,128)}, f32[4,536,768]{2,1,0:T(8,128)}, bf16[4,4,256,768]{3,2,1,0:T(8,128)(2,1)},...) custom-call(f32[2,4,256,384]{3,2,1,0:T(8,128)} %get-tuple-element.34, ...), custom_call_target="tpu_custom_call", output_to_operand_aliasing={{0}: (0, {}), {1}: (1, {}), {2}: (2, {}), {3}: (3, {}), {4}... | custom-call | flops 1000 | bytes 1000 | tf_op jit(solution)/shard_map/pallas_call | solution.py:217
  137.7 10.7 %shard_map.251 = (f32[2,4,256,384]{3,2,1,0:T(8,128)}, f32[4,536,768]{2,1,0:T(8,128)}, bf16[4,7,256,384]{3,2,1,0:T(8,128)(2,1)}, bf16[4,4,384,256]{3,2,1,0:T(8,12...) custom-call(f32[2,4,256,384]{3,2,1,0:T(8,128)} %get-tuple-element.35, ...), custom_call_target="tpu_custom_call", output_to_operand_aliasing={{0}: (0, {}), {1}: (1, {}), {2}: (2, {}), {3}: (3, {}), {4}... | custom-call | flops 1000 | bytes 1000 | tf_op jit(solution)/shard_map/pallas_call | solution.py:217
  150.2 7.4 %shard_map.252 = (f32[2,4,256,384]{3,2,1,0:T(8,128)}, f32[4,256,1536]{2,1,0:T(8,128)}, f32[4,536,768]{2,1,0:T(8,128)}, bf16[4,4,256,768]{3,2,1,0:T(8,128)(2,1)},...) custom-call(f32[2,4,256,384]{3,2,1,0:T(8,128)} %get-tuple-element.35, ...), custom_call_target="tpu_custom_call", output_to_operand_aliasing={{0}: (0, {}), {1}: (1, {}), {2}: (2, {}), {3}: (3, {}), {4}... | custom-call | flops 1000 | bytes 1000 | tf_op jit(solution)/shard_map/pallas_call | solution.py:217
  157.8 7.6 %shard_map.253 = (f32[2,4,256,384]{3,2,1,0:T(8,128)}, bf16[4,4,256,768]{3,2,1,0:T(8,128)(2,1)}, bf16[4,2,256,1536]{3,2,1,0:T(8,128)(2,1)}, bf16[384,1536]{1,0:T(...) custom-call(f32[2,4,256,384]{3,2,1,0:T(8,128)} %get-tuple-element.36, ...), custom_call_target="tpu_custom_call", output_to_operand_aliasing={{0}: (0, {}), {1}: (1, {}), {2}: (2, {})} | custom-call | flops 1000 | bytes 1000 | tf_op jit(solution)/shard_map/pallas_call | solution.py:217
  165.4 8.9 %shard_map.254 = (f32[2,4,256,384]{3,2,1,0:T(8,128)}, f32[4,536,768]{2,1,0:T(8,128)}, bf16[4,7,256,384]{3,2,1,0:T(8,128)(2,1)}, bf16[4,4,384,256]{3,2,1,0:T(8,12...) custom-call(f32[2,4,256,384]{3,2,1,0:T(8,128)} %get-tuple-element.36, ...), custom_call_target="tpu_custom_call", output_to_operand_aliasing={{0}: (0, {}), {1}: (1, {}), {2}: (2, {}), {3}: (3, {}), {4}... | custom-call | flops 1000 | bytes 1000 | tf_op jit(solution)/shard_map/pallas_call | solution.py:217
  177.1 7.4 %shard_map.255 = (f32[2,4,256,384]{3,2,1,0:T(8,128)}, f32[4,256,1536]{2,1,0:T(8,128)}, f32[4,536,768]{2,1,0:T(8,128)}, bf16[4,4,256,768]{3,2,1,0:T(8,128)(2,1)},...) custom-call(f32[2,4,256,384]{3,2,1,0:T(8,128)} %get-tuple-element.37, ...), custom_call_target="tpu_custom_call", output_to_operand_aliasing={{0}: (0, {}), {1}: (1, {}), {2}: (2, {}), {3}: (3, {}), {4}... | custom-call | flops 1000 | bytes 1000 | tf_op jit(solution)/shard_map/pallas_call | solution.py:217
  186.3 6.9 %shard_map.256 = (f32[2,4,256,384]{3,2,1,0:T(8,128)}, f32[4,536,768]{2,1,0:T(8,128)}, bf16[4,7,256,384]{3,2,1,0:T(8,128)(2,1)}, bf16[4,4,384,256]{3,2,1,0:T(8,12...) custom-call(f32[2,4,256,384]{3,2,1,0:T(8,128)} %get-tuple-element.38, ...), custom_call_target="tpu_custom_call", output_to_operand_aliasing={{0}: (0, {}), {1}: (1, {}), {2}: (2, {}), {3}: (3, {}), {4}... | custom-call | flops 1000 | bytes 1000 | tf_op jit(solution)/shard_map/pallas_call | solution.py:217
  195.0 2.8 shard_map.257
  199.0 3.8 collective-permute-done.27.refs_2_
  204.1 2.6 shard_map.259
  209.6 13.2 %collective-permute-done.29.refs_2_ = f32[16,768]{1,0:T(8,128)S(1)} collective-permute-done((f32[16,768]{1,0:T(8,128)S(1)}, f32[16,768]{1,0:T(8,128)S(1)}, u32[]{:S(2)}, u32[]{:S(2)}) %collective-permute-start.29) | collective-permute-done | bytes 49184 | tf_op jit(solution)/shard_map/ppermute | solution.py:1040
  223.6 6.4 %shard_map.261 = (f32[2,4,256,384]{3,2,1,0:T(8,128)}, bf16[4,4,256,768]{3,2,1,0:T(8,128)(2,1)}, bf16[4,7,256,384]{3,2,1,0:T(8,128)(2,1)}, bf16[384,768]{1,0:T(8,...) custom-call(f32[2,4,256,384]{3,2,1,0:T(8,128)} %get-tuple-element.40, ...), custom_call_target="tpu_custom_call", output_to_operand_aliasing={{0}: (0, {}), {1}: (1, {}), {2}: (2, {})} | custom-call | flops 1000 | bytes 1000 | tf_op jit(solution)/shard_map/pallas_call | solution.py:217
  234.7 11.7 %collective-permute-done.32.refs_4_ = f32[192,128]{1,0:T(8,128)S(1)} collective-permute-done((f32[192,128]{1,0:T(8,128)S(1)}, f32[192,128]{1,0:T(8,128)S(1)}, u32[]{:S(2)}, u32[]{:S(2)}) %collective-permute-start.32) | collective-permute-done | bytes 98336 | tf_op jit(solution)/shard_map/ppermute | solution.py:746
  247.0 4.0 collective-permute-done.31.refs_3_
  251.8 3.8 collective-permute-done.30.refs_2_
  257.5 2.4 collective-permute-done.33.refs_2_
  264.5 2.7 collective-permute-start.37
  271.5 4.2 shard_map.268
  281.4 9.2 %collective-permute-done.40.refs_2_ = bf16[96,3072]{1,0:T(8,128)(2,1)S(1)} collective-permute-done((bf16[96,3072]{1,0:T(8,128)(2,1)S(1)}, bf16[96,3072]{1,0:T(8,128)(2,1)S(1)}, u32[]{:S(2)}, u32[]{:S(2)}) %collective-permute-start.40) | collective-permute-done | bytes 589856 | tf_op jit(solution)/shard_map/ppermute | solution.py:934
  291.2 2.7 collective-permute-start.43
  293.9 8.8 %collective-permute-done.41.refs_2_ = bf16[192,768]{1,0:T(8,128)(2,1)S(1)} collective-permute-done((bf16[192,768]{1,0:T(8,128)(2,1)S(1)}, bf16[192,768]{1,0:T(8,128)(2,1)S(1)}, u32[]{:S(2)}, u32[]{:S(2)}) %collective-permute-start.41) | collective-permute-done | bytes 294944 | tf_op jit(solution)/shard_map/ppermute | solution.py:934
  308.2 3.3 collective-permute-done.44.refs_2_
  316.8 3.3 shard_map.274
  320.5 4.0 collective-permute-start.48
  325.2 4.3 collective-permute-done.48.refs_2_
  335.6 3.7 collective-permute-start.54
  339.3 3.5 collective-permute-done.52.refs_2_
  344.9 9.0 %collective-permute-done.55.refs_2_ = bf16[192,1536]{1,0:T(8,128)(2,1)S(1)} collective-permute-done((bf16[192,1536]{1,0:T(8,128)(2,1)S(1)}, bf16[192,1536]{1,0:T(8,128)(2,1)S(1)}, u32[]{:S(2)}, u32[]{:S(2)}) %collective-permute-start.55) | collective-permute-done | bytes 589856 | tf_op jit(solution)/shard_map/ppermute | solution.py:934
  358.6 2.8 collective-permute-start.60
  361.9 19.8 %collective-permute-done.58.refs_2_ = bf16[192,768]{1,0:T(8,128)(2,1)S(1)} collective-permute-done((bf16[192,768]{1,0:T(8,128)(2,1)S(1)}, bf16[192,768]{1,0:T(8,128)(2,1)S(1)}, u32[]{:S(2)}, u32[]{:S(2)}) %collective-permute-start.58) | collective-permute-done | bytes 294944 | tf_op jit(solution)/shard_map/ppermute | solution.py:934
  381.7 3.3 collective-permute-start.61
  385.6 3.5 collective-permute-start.62
  390.4 8.8 %collective-permute-done.61.refs_2_ = bf16[48,3072]{1,0:T(8,128)(2,1)S(1)} collective-permute-done((bf16[48,3072]{1,0:T(8,128)(2,1)S(1)}, bf16[48,3072]{1,0:T(8,128)(2,1)S(1)}, u32[]{:S(2)}, u32[]{:S(2)}) %collective-permute-start.61) | collective-permute-done | bytes 294944 | tf_op jit(solution)/shard_map/ppermute | solution.py:934
  400.9 4.9 shard_map.287
  408.9 2.5 collective-permute-done.67.refs_2_
  411.7 2.9 collective-permute-start.68
  414.6 7.0 %collective-permute-done.68.refs_2_ = bf16[48,1536]{1,0:T(8,128)(2,1)S(1)} collective-permute-done((bf16[48,1536]{1,0:T(8,128)(2,1)S(1)}, bf16[48,1536]{1,0:T(8,128)(2,1)S(1)}, u32[]{:S(2)}, u32[]{:S(2)}) %collective-permute-start.68) | collective-permute-done | bytes 147488 | tf_op jit(solution)/shard_map/ppermute | solution.py:934
  422.2 2.8 shard_map.291
  425.5 2.4 collective-permute-start.73
  429.5 3.4 collective-permute-start.72
  432.9 3.1 collective-permute-done.72.refs_2_
  436.4 5.6 %collective-permute-done.73.refs_2_ = bf16[192,1536]{1,0:T(8,128)(2,1)S(1)} collective-permute-done((bf16[192,1536]{1,0:T(8,128)(2,1)S(1)}, bf16[192,1536]{1,0:T(8,128)(2,1)S(1)}, u32[]{:S(2)}, u32[]{:S(2)}) %collective-permute-start.73) | collective-permute-done | bytes 589856 | tf_op jit(solution)/shard_map/ppermute | solution.py:934
  446.9 3.9 collective-permute-start.75
  450.8 4.7 collective-permute-done.75.refs_2_
  457.3 12.5 %collective-permute-done.76.refs_2_ = bf16[384,1536]{1,0:T(8,128)(2,1)S(1)} collective-permute-done((bf16[384,1536]{1,0:T(8,128)(2,1)S(1)}, bf16[384,1536]{1,0:T(8,128)(2,1)S(1)}, u32[]{:S(2)}, u32[]{:S(2)}) %collective-permute-start.76) | collective-permute-done | bytes 1179680 | tf_op jit(solution)/shard_map/ppermute | solution.py:934
  469.8 4.9 shard_map.296
  477.1 7.9 %collective-permute-done.80.refs_2_ = bf16[384,768]{1,0:T(8,128)(2,1)S(1)} collective-permute-done((bf16[384,768]{1,0:T(8,128)(2,1)S(1)}, bf16[384,768]{1,0:T(8,128)(2,1)S(1)}, u32[]{:S(2)}, u32[]{:S(2)}) %collective-permute-start.80) | collective-permute-done | bytes 589856 | tf_op jit(solution)/shard_map/ppermute | solution.py:934
  486.7 2.8 shard_map.298
  (206 shorter events, 113.6 us)
Async XLA Ops:
  1.8 7.5 %collective-permute-start.2 = (f32[192,128]{1,0:T(8,128)S(1)}, f32[192,128]{1,0:T(8,128)S(1)}, u32[]{:S(2)}, u32[]{:S(2)}) collective-permute-start(f32[192,128]{1,0:T(8,128)S(1)} %get-tuple-element.549), channel_id=1, source_target_pairs={{0,6},{2,4},{4,2},{6,0},{1,7},{3,5},{5,3},{7,1},{8,14},{10,12},{12... | collective-permute-start | bytes 294920 | tf_op jit(solution)/shard_map/ppermute | solution.py:746
  5.7 5.2 %collective-permute-start = (f32[192,128]{1,0:T(8,128)S(1)}, f32[192,128]{1,0:T(8,128)S(1)}, u32[]{:S(2)}, u32[]{:S(2)}) collective-permute-start(f32[192,128]{1,0:T(8,128)S(1)} %get-tuple-element.550), channel_id=1, source_target_pairs={{0,2},{2,0},{4,6},{6,4},{1,3},{3,1},{5,7},{7,5},{8,10},{10,8},{12,... | collective-permute-start | bytes 294920 | tf_op jit(solution)/shard_map/ppermute | solution.py:746
  6.3 4.7 collective-permute-start.1
  42.3 13.0 %collective-permute-start.10 = (f32[128,768]{1,0:T(8,128)S(1)}, f32[128,768]{1,0:T(8,128)S(1)}, u32[]{:S(2)}, u32[]{:S(2)}) collective-permute-start(f32[128,768]{1,0:T(8,128)S(1)} %get-tuple-element.541), channel_id=1, source_target_pairs={{0,6},{2,4},{4,2},{6,0},{1,7},{3,5},{5,3},{7,1},{8,14},{10,12},{12... | collective-permute-start | bytes 1179656 | tf_op jit(solution)/shard_map/ppermute | solution.py:746
  44.7 18.4 %collective-permute-start.8 = (f32[128,768]{1,0:T(8,128)S(1)}, f32[128,768]{1,0:T(8,128)S(1)}, u32[]{:S(2)}, u32[]{:S(2)}) collective-permute-start(f32[128,768]{1,0:T(8,128)S(1)} %get-tuple-element.542), channel_id=1, source_target_pairs={{0,2},{2,0},{4,6},{6,4},{1,3},{3,1},{5,7},{7,5},{8,10},{10,8},{12,... | collective-permute-start | bytes 1179656 | tf_op jit(solution)/shard_map/ppermute | solution.py:746
  45.2 17.9 %collective-permute-start.9 = (f32[128,768]{1,0:T(8,128)S(1)}, f32[128,768]{1,0:T(8,128)S(1)}, u32[]{:S(2)}, u32[]{:S(2)}) collective-permute-start(f32[128,768]{1,0:T(8,128)S(1)} %get-tuple-element.544), channel_id=1, source_target_pairs={{0,4},{2,6},{4,0},{6,2},{1,5},{3,7},{5,1},{7,3},{8,12},{10,14},{12... | collective-permute-start | bytes 1179656 | tf_op jit(solution)/shard_map/ppermute | solution.py:746
  52.6 11.4 %collective-permute-start.11 = (bf16[256,768]{1,0:T(8,128)(2,1)S(1)}, bf16[256,768]{1,0:T(8,128)(2,1)S(1)}, u32[]{:S(2)}, u32[]{:S(2)}) collective-permute-start(bf16[256,768]{1,0:T(8,128)(2,1)S(1)} %get-tuple-element.310.refs_5_), channel_id=1, source_target_pairs={{0,1},{1,0},{2,3},{3,2},{4,5},{5,4},{6,7},{7,6},{8,9},{9,8},{10,11... | collective-permute-start | bytes 1179656 | tf_op jit(solution)/shard_map/ppermute | solution.py:643
  63.9 34.0 %collective-permute-start.14 = (f32[4,128,768]{2,1,0:T(8,128)S(1)}, f32[4,128,768]{2,1,0:T(8,128)S(1)}, u32[]{:S(2)}, u32[]{:S(2)}) collective-permute-start(f32[4,128,768]{2,1,0:T(8,128)S(1)} %bitcast.44), channel_id=1, source_target_pairs={{0,1},{1,0},{2,3},{3,2},{4,5},{5,4},{6,7},{7,6},{8,9},{9,8},{10,11... | collective-permute-start | bytes 4718600 | tf_op jit(solution)/shard_map/ppermute | solution.py:643
  105.3 17.0 %collective-permute-start.19 = (f32[128,768]{1,0:T(8,128)S(1)}, f32[128,768]{1,0:T(8,128)S(1)}, u32[]{:S(2)}, u32[]{:S(2)}) collective-permute-start(f32[128,768]{1,0:T(8,128)S(1)} %get-tuple-element.537), channel_id=1, source_target_pairs={{0,6},{2,4},{4,2},{6,0},{1,7},{3,5},{5,3},{7,1},{8,14},{10,12},{12... | collective-permute-start | bytes 1179656 | tf_op jit(solution)/shard_map/ppermute | solution.py:746
  107.6 18.4 %collective-permute-start.18 = (f32[128,768]{1,0:T(8,128)S(1)}, f32[128,768]{1,0:T(8,128)S(1)}, u32[]{:S(2)}, u32[]{:S(2)}) collective-permute-start(f32[128,768]{1,0:T(8,128)S(1)} %get-tuple-element.538), channel_id=1, source_target_pairs={{0,4},{2,6},{4,0},{6,2},{1,5},{3,7},{5,1},{7,3},{8,12},{10,14},{12... | collective-permute-start | bytes 1179656 | tf_op jit(solution)/shard_map/ppermute | solution.py:746
  108.4 17.6 %collective-permute-start.17 = (f32[128,768]{1,0:T(8,128)S(1)}, f32[128,768]{1,0:T(8,128)S(1)}, u32[]{:S(2)}, u32[]{:S(2)}) collective-permute-start(f32[128,768]{1,0:T(8,128)S(1)} %get-tuple-element.539), channel_id=1, source_target_pairs={{0,2},{2,0},{4,6},{6,4},{1,3},{3,1},{5,7},{7,5},{8,10},{10,8},{12,... | collective-permute-start | bytes 1179656 | tf_op jit(solution)/shard_map/ppermute | solution.py:746
  122.1 6.4 %collective-permute-start.20 = (bf16[256,768]{1,0:T(8,128)(2,1)S(1)}, bf16[256,768]{1,0:T(8,128)(2,1)S(1)}, u32[]{:S(2)}, u32[]{:S(2)}) collective-permute-start(bf16[256,768]{1,0:T(8,128)(2,1)S(1)} %get-tuple-element.350.refs_10_), channel_id=1, source_target_pairs={{0,1},{1,0},{2,3},{3,2},{4,5},{5,4},{6,7},{7,6},{8,9},{9,8},{10,11... | collective-permute-start | bytes 1179656 | tf_op jit(solution)/shard_map/ppermute | solution.py:643
  157.6 7.8 %collective-permute-start.23 = (bf16[256,768]{1,0:T(8,128)(2,1)S(1)}, bf16[256,768]{1,0:T(8,128)(2,1)S(1)}, u32[]{:S(2)}, u32[]{:S(2)}) collective-permute-start(bf16[256,768]{1,0:T(8,128)(2,1)S(1)} %get-tuple-element.374.refs_5_), channel_id=1, source_target_pairs={{0,1},{1,0},{2,3},{3,2},{4,5},{5,4},{6,7},{7,6},{8,9},{9,8},{10,11... | collective-permute-start | bytes 1179656 | tf_op jit(solution)/shard_map/ppermute | solution.py:643
  174.8 28.0 %collective-permute-start.27 = (bf16[384,1536]{1,0:T(8,128)(2,1)S(1)}, bf16[384,1536]{1,0:T(8,128)(2,1)S(1)}, u32[]{:S(2)}, u32[]{:S(2)}) collective-permute-start(bf16[384,1536]{1,0:T(8,128)(2,1)S(1)} %get-tuple-element.398), channel_id=1, source_target_pairs={{0,2},{2,0},{4,6},{6,4},{1,3},{3,1},{5,7},{7,5},{8,10},{10,8},{12,... | collective-permute-start | bytes 3538952 | tf_op jit(solution)/shard_map/ppermute | solution.py:934
  176.4 27.7 %collective-permute-start.28 = (bf16[384,1536]{1,0:T(8,128)(2,1)S(1)}, bf16[384,1536]{1,0:T(8,128)(2,1)S(1)}, u32[]{:S(2)}, u32[]{:S(2)}) collective-permute-start(bf16[384,1536]{1,0:T(8,128)(2,1)S(1)} %get-tuple-element.400), channel_id=1, source_target_pairs={{0,4},{2,6},{4,0},{6,2},{1,5},{3,7},{5,1},{7,3},{8,12},{10,14},{12... | collective-permute-start | bytes 3538952 | tf_op jit(solution)/shard_map/ppermute | solution.py:934
  206.8 55.0 %collective-permute-start.34 = (bf16[192,1536]{1,0:T(8,128)(2,1)}, bf16[192,1536]{1,0:T(8,128)(2,1)}, u32[]{:S(2)}, u32[]{:S(2)}) collective-permute-start(bf16[192,1536]{1,0:T(8,128)(2,1)} %get-tuple-element.413), channel_id=1, source_target_pairs={{0,4},{2,6},{4,0},{6,2},{1,5},{3,7},{5,1},{7,3},{8,12},{10,14},{12... | collective-permute-start | bytes 1769480 | tf_op jit(solution)/shard_map/ppermute | solution.py:934
  207.5 54.2 %collective-permute-start.35 = (bf16[192,1536]{1,0:T(8,128)(2,1)}, bf16[192,1536]{1,0:T(8,128)(2,1)}, u32[]{:S(2)}, u32[]{:S(2)}) collective-permute-start(bf16[192,1536]{1,0:T(8,128)(2,1)} %get-tuple-element.415), channel_id=1, source_target_pairs={{0,2},{2,0},{4,6},{6,4},{1,3},{3,1},{5,7},{7,5},{8,10},{10,8},{12,... | collective-permute-start | bytes 1769480 | tf_op jit(solution)/shard_map/ppermute | solution.py:934
  208.6 14.1 %collective-permute-start.29 = (f32[16,768]{1,0:T(8,128)S(1)}, f32[16,768]{1,0:T(8,128)S(1)}, u32[]{:S(2)}, u32[]{:S(2)}) collective-permute-start(f32[16,768]{1,0:T(8,128)S(1)} %get-tuple-element.402.refs_1_), channel_id=1, source_target_pairs={{0,2},{2,0},{4,6},{6,4},{1,3},{3,1},{5,7},{7,5},{8,10},{10,8},{12,... | collective-permute-start | bytes 147464 | tf_op jit(solution)/shard_map/ppermute | solution.py:1040
  230.0 40.4 %collective-permute-start.38 = (bf16[384,768]{1,0:T(8,128)(2,1)}, bf16[384,768]{1,0:T(8,128)(2,1)S(1)}, u32[]{:S(2)}, u32[]{:S(2)}) collective-permute-start(bf16[384,768]{1,0:T(8,128)(2,1)} %get-tuple-element.422), channel_id=1, source_target_pairs={{0,2},{2,0},{4,6},{6,4},{1,3},{3,1},{5,7},{7,5},{8,10},{10,8},{12,... | collective-permute-start | bytes 1769480 | tf_op jit(solution)/shard_map/ppermute | solution.py:934
  231.1 39.2 %collective-permute-start.39 = (bf16[384,768]{1,0:T(8,128)(2,1)}, bf16[384,768]{1,0:T(8,128)(2,1)S(1)}, u32[]{:S(2)}, u32[]{:S(2)}) collective-permute-start(bf16[384,768]{1,0:T(8,128)(2,1)} %get-tuple-element.424), channel_id=1, source_target_pairs={{0,4},{2,6},{4,0},{6,2},{1,5},{3,7},{5,1},{7,3},{8,12},{10,14},{12... | collective-permute-start | bytes 1769480 | tf_op jit(solution)/shard_map/ppermute | solution.py:934
  233.1 13.3 %collective-permute-start.32 = (f32[192,128]{1,0:T(8,128)S(1)}, f32[192,128]{1,0:T(8,128)S(1)}, u32[]{:S(2)}, u32[]{:S(2)}) collective-permute-start(f32[192,128]{1,0:T(8,128)S(1)} %get-tuple-element.545), channel_id=1, source_target_pairs={{0,6},{2,4},{4,2},{6,0},{1,7},{3,5},{5,3},{7,1},{8,14},{10,12},{12... | collective-permute-start | bytes 294920 | tf_op jit(solution)/shard_map/ppermute | solution.py:746
  264.5 5.1 %collective-permute-start.37 = (f32[16,768]{1,0:T(8,128)S(1)}, f32[16,768]{1,0:T(8,128)S(1)}, u32[]{:S(2)}, u32[]{:S(2)}) collective-permute-start(f32[16,768]{1,0:T(8,128)S(1)} %get-tuple-element.419.refs_1_), channel_id=1, source_target_pairs={{0,16},{8,24},{16,0},{24,8},{1,17},{9,25},{17,1},{25,9},{2,18},{10... | collective-permute-start | bytes 147464 | tf_op jit(solution)/shard_map/ppermute | solution.py:1044
  275.7 36.4 %collective-permute-start.45 = (bf16[384,1536]{1,0:T(8,128)(2,1)S(1)}, bf16[384,1536]{1,0:T(8,128)(2,1)S(1)}, u32[]{:S(2)}, u32[]{:S(2)}) collective-permute-start(bf16[384,1536]{1,0:T(8,128)(2,1)S(1)} %get-tuple-element.444), channel_id=1, source_target_pairs={{0,2},{2,0},{4,6},{6,4},{1,3},{3,1},{5,7},{7,5},{8,10},{10,8},{12,... | collective-permute-start | bytes 3538952 | tf_op jit(solution)/shard_map/ppermute | solution.py:934
  276.6 35.6 %collective-permute-start.46 = (bf16[384,1536]{1,0:T(8,128)(2,1)S(1)}, bf16[384,1536]{1,0:T(8,128)(2,1)S(1)}, u32[]{:S(2)}, u32[]{:S(2)}) collective-permute-start(bf16[384,1536]{1,0:T(8,128)(2,1)S(1)} %get-tuple-element.446), channel_id=1, source_target_pairs={{0,4},{2,6},{4,0},{6,2},{1,5},{3,7},{5,1},{7,3},{8,12},{10,14},{12... | collective-permute-start | bytes 3538952 | tf_op jit(solution)/shard_map/ppermute | solution.py:934
  277.6 13.0 %collective-permute-start.40 = (bf16[96,3072]{1,0:T(8,128)(2,1)S(1)}, bf16[96,3072]{1,0:T(8,128)(2,1)S(1)}, u32[]{:S(2)}, u32[]{:S(2)}) collective-permute-start(bf16[96,3072]{1,0:T(8,128)(2,1)S(1)} %get-tuple-element.430), channel_id=1, source_target_pairs={{0,8},{8,0},{16,24},{24,16},{1,9},{9,1},{17,25},{25,17},{2,10},{10... | collective-permute-start | bytes 1769480 | tf_op jit(solution)/shard_map/ppermute | solution.py:934
  279.2 23.5 %collective-permute-start.41 = (bf16[192,768]{1,0:T(8,128)(2,1)S(1)}, bf16[192,768]{1,0:T(8,128)(2,1)S(1)}, u32[]{:S(2)}, u32[]{:S(2)}) collective-permute-start(bf16[192,768]{1,0:T(8,128)(2,1)S(1)} %get-tuple-element.433), channel_id=1, source_target_pairs={{0,4},{2,6},{4,0},{6,2},{1,5},{3,7},{5,1},{7,3},{8,12},{10,14},{12... | collective-permute-start | bytes 884744 | tf_op jit(solution)/shard_map/ppermute | solution.py:934
  280.1 22.6 %collective-permute-start.42 = (bf16[192,768]{1,0:T(8,128)(2,1)S(1)}, bf16[192,768]{1,0:T(8,128)(2,1)S(1)}, u32[]{:S(2)}, u32[]{:S(2)}) collective-permute-start(bf16[192,768]{1,0:T(8,128)(2,1)S(1)} %get-tuple-element.435), channel_id=1, source_target_pairs={{0,2},{2,0},{4,6},{6,4},{1,3},{3,1},{5,7},{7,5},{8,10},{10,8},{12,... | collective-permute-start | bytes 884744 | tf_op jit(solution)/shard_map/ppermute | solution.py:934
  291.2 15.7 %collective-permute-start.43 = (bf16[48,3072]{1,0:T(8,128)(2,1)S(1)}, bf16[48,3072]{1,0:T(8,128)(2,1)S(1)}, u32[]{:S(2)}, u32[]{:S(2)}) collective-permute-start(bf16[48,3072]{1,0:T(8,128)(2,1)S(1)} %get-tuple-element.438), channel_id=1, source_target_pairs={{0,16},{8,24},{16,0},{24,8},{1,17},{9,25},{17,1},{25,9},{2,18},{10... | collective-permute-start | bytes 884744 | tf_op jit(solution)/shard_map/ppermute | solution.py:934
  303.3 8.2 %collective-permute-start.44 = (bf16[96,1536]{1,0:T(8,128)(2,1)S(1)}, bf16[96,1536]{1,0:T(8,128)(2,1)S(1)}, u32[]{:S(2)}, u32[]{:S(2)}) collective-permute-start(bf16[96,1536]{1,0:T(8,128)(2,1)S(1)} %get-tuple-element.441), channel_id=1, source_target_pairs={{0,8},{8,0},{16,24},{24,16},{1,9},{9,1},{17,25},{25,17},{2,10},{10... | collective-permute-start | bytes 884744 | tf_op jit(solution)/shard_map/ppermute | solution.py:934
  307.2 12.9 %collective-permute-start.47 = (bf16[48,3072]{1,0:T(8,128)(2,1)S(1)}, bf16[48,3072]{1,0:T(8,128)(2,1)S(1)}, u32[]{:S(2)}, u32[]{:S(2)}) collective-permute-start(bf16[48,3072]{1,0:T(8,128)(2,1)S(1)} %get-tuple-element.451.refs_1_), channel_id=1, source_target_pairs={{0,16},{8,24},{16,0},{24,8},{1,17},{9,25},{17,1},{25,9},{2,18},{10... | collective-permute-start | bytes 884744 | tf_op jit(solution)/shard_map/ppermute | solution.py:934
  314.4 16.4 %collective-permute-start.49 = (bf16[192,1536]{1,0:T(8,128)(2,1)S(1)}, bf16[192,1536]{1,0:T(8,128)(2,1)S(1)}, u32[]{:S(2)}, u32[]{:S(2)}) collective-permute-start(bf16[192,1536]{1,0:T(8,128)(2,1)S(1)} %get-tuple-element.457), channel_id=1, source_target_pairs={{0,4},{2,6},{4,0},{6,2},{1,5},{3,7},{5,1},{7,3},{8,12},{10,14},{12... | collective-permute-start | bytes 1769480 | tf_op jit(solution)/shard_map/ppermute | solution.py:934
  315.6 16.3 %collective-permute-start.50 = (bf16[192,1536]{1,0:T(8,128)(2,1)S(1)}, bf16[192,1536]{1,0:T(8,128)(2,1)S(1)}, u32[]{:S(2)}, u32[]{:S(2)}) collective-permute-start(bf16[192,1536]{1,0:T(8,128)(2,1)S(1)} %get-tuple-element.459), channel_id=1, source_target_pairs={{0,2},{2,0},{4,6},{6,4},{1,3},{3,1},{5,7},{7,5},{8,10},{10,8},{12,... | collective-permute-start | bytes 1769480 | tf_op jit(solution)/shard_map/ppermute | solution.py:934
  320.3 13.0 %collective-permute-start.51 = (bf16[96,3072]{1,0:T(8,128)(2,1)S(1)}, bf16[96,3072]{1,0:T(8,128)(2,1)S(1)}, u32[]{:S(2)}, u32[]{:S(2)}) collective-permute-start(bf16[96,3072]{1,0:T(8,128)(2,1)S(1)} %get-tuple-element.461.refs_1_), channel_id=1, source_target_pairs={{0,8},{8,0},{16,24},{24,16},{1,9},{9,1},{17,25},{25,17},{2,10},{10... | collective-permute-start | bytes 1769480 | tf_op jit(solution)/shard_map/ppermute | solution.py:934
  320.5 9.0 %collective-permute-start.48 = (bf16[48,1536]{1,0:T(8,128)(2,1)S(1)}, bf16[48,1536]{1,0:T(8,128)(2,1)S(1)}, u32[]{:S(2)}, u32[]{:S(2)}) collective-permute-start(bf16[48,1536]{1,0:T(8,128)(2,1)S(1)} %get-tuple-element.454), channel_id=1, source_target_pairs={{0,16},{8,24},{16,0},{24,8},{1,17},{9,25},{17,1},{25,9},{2,18},{10... | collective-permute-start | bytes 442376 | tf_op jit(solution)/shard_map/ppermute | solution.py:934
  324.4 18.4 %collective-permute-start.52 = (bf16[384,768]{1,0:T(8,128)(2,1)S(1)}, bf16[384,768]{1,0:T(8,128)(2,1)S(1)}, u32[]{:S(2)}, u32[]{:S(2)}) collective-permute-start(bf16[384,768]{1,0:T(8,128)(2,1)S(1)} %get-tuple-element.464), channel_id=1, source_target_pairs={{0,2},{2,0},{4,6},{6,4},{1,3},{3,1},{5,7},{7,5},{8,10},{10,8},{12,... | collective-permute-start | bytes 1769480 | tf_op jit(solution)/shard_map/ppermute | solution.py:934
  329.5 13.8 %collective-permute-start.53 = (bf16[384,768]{1,0:T(8,128)(2,1)S(1)}, bf16[384,768]{1,0:T(8,128)(2,1)S(1)}, u32[]{:S(2)}, u32[]{:S(2)}) collective-permute-start(bf16[384,768]{1,0:T(8,128)(2,1)S(1)} %get-tuple-element.466), channel_id=1, source_target_pairs={{0,4},{2,6},{4,0},{6,2},{1,5},{3,7},{5,1},{7,3},{8,12},{10,14},{12... | collective-permute-start | bytes 1769480 | tf_op jit(solution)/shard_map/ppermute | solution.py:934
  333.6 20.3 %collective-permute-start.55 = (bf16[192,1536]{1,0:T(8,128)(2,1)S(1)}, bf16[192,1536]{1,0:T(8,128)(2,1)S(1)}, u32[]{:S(2)}, u32[]{:S(2)}) collective-permute-start(bf16[192,1536]{1,0:T(8,128)(2,1)S(1)} %get-tuple-element.470.refs_1_), channel_id=1, source_target_pairs={{0,4},{2,6},{4,0},{6,2},{1,5},{3,7},{5,1},{7,3},{8,12},{10,14},{12... | collective-permute-start | bytes 1769480 | tf_op jit(solution)/shard_map/ppermute | solution.py:934
  334.4 19.5 %collective-permute-start.56 = (bf16[192,1536]{1,0:T(8,128)(2,1)S(1)}, bf16[192,1536]{1,0:T(8,128)(2,1)S(1)}, u32[]{:S(2)}, u32[]{:S(2)}) collective-permute-start(bf16[192,1536]{1,0:T(8,128)(2,1)S(1)} %get-tuple-element.471.refs_3_), channel_id=1, source_target_pairs={{0,2},{2,0},{4,6},{6,4},{1,3},{3,1},{5,7},{7,5},{8,10},{10,8},{12,... | collective-permute-start | bytes 1769480 | tf_op jit(solution)/shard_map/ppermute | solution.py:934
  335.6 8.8 %collective-permute-start.54 = (bf16[48,1536]{1,0:T(8,128)(2,1)S(1)}, bf16[48,1536]{1,0:T(8,128)(2,1)S(1)}, u32[]{:S(2)}, u32[]{:S(2)}) collective-permute-start(bf16[48,1536]{1,0:T(8,128)(2,1)S(1)} %get-tuple-element.468.refs_1_), channel_id=1, source_target_pairs={{0,16},{8,24},{16,0},{24,8},{1,17},{9,25},{17,1},{25,9},{2,18},{10... | collective-permute-start | bytes 442376 | tf_op jit(solution)/shard_map/ppermute | solution.py:934
  342.8 15.7 %collective-permute-start.57 = (bf16[96,3072]{1,0:T(8,128)(2,1)S(1)}, bf16[96,3072]{1,0:T(8,128)(2,1)S(1)}, u32[]{:S(2)}, u32[]{:S(2)}) collective-permute-start(bf16[96,3072]{1,0:T(8,128)(2,1)S(1)} %get-tuple-element.474), channel_id=1, source_target_pairs={{0,8},{8,0},{16,24},{24,16},{1,9},{9,1},{17,25},{25,17},{2,10},{10... | collective-permute-start | bytes 1769480 | tf_op jit(solution)/shard_map/ppermute | solution.py:934
  354.4 46.5 %collective-permute-start.63 = (bf16[384,1536]{1,0:T(8,128)(2,1)S(1)}, bf16[384,1536]{1,0:T(8,128)(2,1)S(1)}, u32[]{:S(2)}, u32[]{:S(2)}) collective-permute-start(bf16[384,1536]{1,0:T(8,128)(2,1)S(1)} %get-tuple-element.489.refs_1_), channel_id=1, source_target_pairs={{0,2},{2,0},{4,6},{6,4},{1,3},{3,1},{5,7},{7,5},{8,10},{10,8},{12,... | collective-permute-start | bytes 3538952 | tf_op jit(solution)/shard_map/ppermute | solution.py:934
  355.5 45.4 %collective-permute-start.64 = (bf16[384,1536]{1,0:T(8,128)(2,1)S(1)}, bf16[384,1536]{1,0:T(8,128)(2,1)S(1)}, u32[]{:S(2)}, u32[]{:S(2)}) collective-permute-start(bf16[384,1536]{1,0:T(8,128)(2,1)S(1)} %get-tuple-element.490.refs_3_), channel_id=1, source_target_pairs={{0,4},{2,6},{4,0},{6,2},{1,5},{3,7},{5,1},{7,3},{8,12},{10,14},{12... | collective-permute-start | bytes 3538952 | tf_op jit(solution)/shard_map/ppermute | solution.py:934
  357.0 24.7 %collective-permute-start.58 = (bf16[192,768]{1,0:T(8,128)(2,1)S(1)}, bf16[192,768]{1,0:T(8,128)(2,1)S(1)}, u32[]{:S(2)}, u32[]{:S(2)}) collective-permute-start(bf16[192,768]{1,0:T(8,128)(2,1)S(1)} %get-tuple-element.477), channel_id=1, source_target_pairs={{0,4},{2,6},{4,0},{6,2},{1,5},{3,7},{5,1},{7,3},{8,12},{10,14},{12... | collective-permute-start | bytes 884744 | tf_op jit(solution)/shard_map/ppermute | solution.py:934
  357.6 27.5 %collective-permute-start.59 = (bf16[192,768]{1,0:T(8,128)(2,1)S(1)}, bf16[192,768]{1,0:T(8,128)(2,1)S(1)}, u32[]{:S(2)}, u32[]{:S(2)}) collective-permute-start(bf16[192,768]{1,0:T(8,128)(2,1)S(1)} %get-tuple-element.479), channel_id=1, source_target_pairs={{0,2},{2,0},{4,6},{6,4},{1,3},{3,1},{5,7},{7,5},{8,10},{10,8},{12,... | collective-permute-start | bytes 884744 | tf_op jit(solution)/shard_map/ppermute | solution.py:934
  358.6 30.6 %collective-permute-start.60 = (bf16[96,1536]{1,0:T(8,128)(2,1)S(1)}, bf16[96,1536]{1,0:T(8,128)(2,1)S(1)}, u32[]{:S(2)}, u32[]{:S(2)}) collective-permute-start(bf16[96,1536]{1,0:T(8,128)(2,1)S(1)} %get-tuple-element.481.refs_1_), channel_id=1, source_target_pairs={{0,8},{8,0},{16,24},{24,16},{1,9},{9,1},{17,25},{25,17},{2,10},{10... | collective-permute-start | bytes 884744 | tf_op jit(solution)/shard_map/ppermute | solution.py:934
  381.7 17.5 %collective-permute-start.61 = (bf16[48,3072]{1,0:T(8,128)(2,1)S(1)}, bf16[48,3072]{1,0:T(8,128)(2,1)S(1)}, u32[]{:S(2)}, u32[]{:S(2)}) collective-permute-start(bf16[48,3072]{1,0:T(8,128)(2,1)S(1)} %get-tuple-element.484), channel_id=1, source_target_pairs={{0,16},{8,24},{16,0},{24,8},{1,17},{9,25},{17,1},{25,9},{2,18},{10... | collective-permute-start | bytes 884744 | tf_op jit(solution)/shard_map/ppermute | solution.py:934
  385.6 14.6 %collective-permute-start.62 = (bf16[96,1536]{1,0:T(8,128)(2,1)S(1)}, bf16[96,1536]{1,0:T(8,128)(2,1)S(1)}, u32[]{:S(2)}, u32[]{:S(2)}) collective-permute-start(bf16[96,1536]{1,0:T(8,128)(2,1)S(1)} %get-tuple-element.487), channel_id=1, source_target_pairs={{0,8},{8,0},{16,24},{24,16},{1,9},{9,1},{17,25},{25,17},{2,10},{10... | collective-permute-start | bytes 884744 | tf_op jit(solution)/shard_map/ppermute | solution.py:934
  389.4 16.5 %collective-permute-start.65 = (bf16[192,768]{1,0:T(8,128)(2,1)S(1)}, bf16[192,768]{1,0:T(8,128)(2,1)S(1)}, u32[]{:S(2)}, u32[]{:S(2)}) collective-permute-start(bf16[192,768]{1,0:T(8,128)(2,1)S(1)} %get-tuple-element.492.refs_1_), channel_id=1, source_target_pairs={{0,4},{2,6},{4,0},{6,2},{1,5},{3,7},{5,1},{7,3},{8,12},{10,14},{12... | collective-permute-start | bytes 884744 | tf_op jit(solution)/shard_map/ppermute | solution.py:934
  399.2 6.7 %collective-permute-start.66 = (bf16[192,768]{1,0:T(8,128)(2,1)S(1)}, bf16[192,768]{1,0:T(8,128)(2,1)S(1)}, u32[]{:S(2)}, u32[]{:S(2)}) collective-permute-start(bf16[192,768]{1,0:T(8,128)(2,1)S(1)} %get-tuple-element.493.refs_3_), channel_id=1, source_target_pairs={{0,2},{2,0},{4,6},{6,4},{1,3},{3,1},{5,7},{7,5},{8,10},{10,8},{12,... | collective-permute-start | bytes 884744 | tf_op jit(solution)/shard_map/ppermute | solution.py:934
  400.2 11.2 %collective-permute-start.67 = (bf16[48,3072]{1,0:T(8,128)(2,1)S(1)}, bf16[48,3072]{1,0:T(8,128)(2,1)S(1)}, u32[]{:S(2)}, u32[]{:S(2)}) collective-permute-start(bf16[48,3072]{1,0:T(8,128)(2,1)S(1)} %get-tuple-element.495.refs_1_), channel_id=1, source_target_pairs={{0,16},{8,24},{16,0},{24,8},{1,17},{9,25},{17,1},{25,9},{2,18},{10... | collective-permute-start | bytes 884744 | tf_op jit(solution)/shard_map/ppermute | solution.py:934
  406.2 16.0 %collective-permute-start.69 = (bf16[384,768]{1,0:T(8,128)(2,1)S(1)}, bf16[384,768]{1,0:T(8,128)(2,1)S(1)}, u32[]{:S(2)}, u32[]{:S(2)}) collective-permute-start(bf16[384,768]{1,0:T(8,128)(2,1)S(1)} %get-tuple-element.500.refs_1_), channel_id=1, source_target_pairs={{0,2},{2,0},{4,6},{6,4},{1,3},{3,1},{5,7},{7,5},{8,10},{10,8},{12,... | collective-permute-start | bytes 1769480 | tf_op jit(solution)/shard_map/ppermute | solution.py:934
  407.8 14.4 %collective-permute-start.70 = (bf16[384,768]{1,0:T(8,128)(2,1)S(1)}, bf16[384,768]{1,0:T(8,128)(2,1)S(1)}, u32[]{:S(2)}, u32[]{:S(2)}) collective-permute-start(bf16[384,768]{1,0:T(8,128)(2,1)S(1)} %get-tuple-element.501.refs_3_), channel_id=1, source_target_pairs={{0,4},{2,6},{4,0},{6,2},{1,5},{3,7},{5,1},{7,3},{8,12},{10,14},{12... | collective-permute-start | bytes 1769480 | tf_op jit(solution)/shard_map/ppermute | solution.py:934
  411.6 13.5 %collective-permute-start.71 = (bf16[96,3072]{1,0:T(8,128)(2,1)S(1)}, bf16[96,3072]{1,0:T(8,128)(2,1)S(1)}, u32[]{:S(2)}, u32[]{:S(2)}) collective-permute-start(bf16[96,3072]{1,0:T(8,128)(2,1)S(1)} %get-tuple-element.503.refs_1_), channel_id=1, source_target_pairs={{0,8},{8,0},{16,24},{24,16},{1,9},{9,1},{17,25},{25,17},{2,10},{10... | collective-permute-start | bytes 1769480 | tf_op jit(solution)/shard_map/ppermute | solution.py:934
  411.7 9.9 %collective-permute-start.68 = (bf16[48,1536]{1,0:T(8,128)(2,1)S(1)}, bf16[48,1536]{1,0:T(8,128)(2,1)S(1)}, u32[]{:S(2)}, u32[]{:S(2)}) collective-permute-start(bf16[48,1536]{1,0:T(8,128)(2,1)S(1)} %get-tuple-element.498), channel_id=1, source_target_pairs={{0,16},{8,24},{16,0},{24,8},{1,17},{9,25},{17,1},{25,9},{2,18},{10... | collective-permute-start | bytes 442376 | tf_op jit(solution)/shard_map/ppermute | solution.py:934
  425.5 16.6 %collective-permute-start.73 = (bf16[192,1536]{1,0:T(8,128)(2,1)S(1)}, bf16[192,1536]{1,0:T(8,128)(2,1)S(1)}, u32[]{:S(2)}, u32[]{:S(2)}) collective-permute-start(bf16[192,1536]{1,0:T(8,128)(2,1)S(1)} %get-tuple-element.507.refs_1_), channel_id=1, source_target_pairs={{0,4},{2,6},{4,0},{6,2},{1,5},{3,7},{5,1},{7,3},{8,12},{10,14},{12... | collective-permute-start | bytes 1769480 | tf_op jit(solution)/shard_map/ppermute | solution.py:934
  427.9 16.3 %collective-permute-start.74 = (bf16[192,1536]{1,0:T(8,128)(2,1)S(1)}, bf16[192,1536]{1,0:T(8,128)(2,1)S(1)}, u32[]{:S(2)}, u32[]{:S(2)}) collective-permute-start(bf16[192,1536]{1,0:T(8,128)(2,1)S(1)} %get-tuple-element.508.refs_3_), channel_id=1, source_target_pairs={{0,2},{2,0},{4,6},{6,4},{1,3},{3,1},{5,7},{7,5},{8,10},{10,8},{12,... | collective-permute-start | bytes 1769480 | tf_op jit(solution)/shard_map/ppermute | solution.py:934
  429.5 6.6 %collective-permute-start.72 = (bf16[48,1536]{1,0:T(8,128)(2,1)S(1)}, bf16[48,1536]{1,0:T(8,128)(2,1)S(1)}, u32[]{:S(2)}, u32[]{:S(2)}) collective-permute-start(bf16[48,1536]{1,0:T(8,128)(2,1)S(1)} %get-tuple-element.505.refs_1_), channel_id=1, source_target_pairs={{0,16},{8,24},{16,0},{24,8},{1,17},{9,25},{17,1},{25,9},{2,18},{10... | collective-permute-start | bytes 442376 | tf_op jit(solution)/shard_map/ppermute | solution.py:934
  444.7 25.0 %collective-permute-start.76 = (bf16[384,1536]{1,0:T(8,128)(2,1)S(1)}, bf16[384,1536]{1,0:T(8,128)(2,1)S(1)}, u32[]{:S(2)}, u32[]{:S(2)}) collective-permute-start(bf16[384,1536]{1,0:T(8,128)(2,1)S(1)} %get-tuple-element.512.refs_1_), channel_id=1, source_target_pairs={{0,2},{2,0},{4,6},{6,4},{1,3},{3,1},{5,7},{7,5},{8,10},{10,8},{12,... | collective-permute-start | bytes 3538952 | tf_op jit(solution)/shard_map/ppermute | solution.py:934
  446.3 23.4 %collective-permute-start.77 = (bf16[384,1536]{1,0:T(8,128)(2,1)S(1)}, bf16[384,1536]{1,0:T(8,128)(2,1)S(1)}, u32[]{:S(2)}, u32[]{:S(2)}) collective-permute-start(bf16[384,1536]{1,0:T(8,128)(2,1)S(1)} %get-tuple-element.513.refs_3_), channel_id=1, source_target_pairs={{0,4},{2,6},{4,0},{6,2},{1,5},{3,7},{5,1},{7,3},{8,12},{10,14},{12... | collective-permute-start | bytes 3538952 | tf_op jit(solution)/shard_map/ppermute | solution.py:934
  446.9 8.6 %collective-permute-start.75 = (bf16[96,1536]{1,0:T(8,128)(2,1)S(1)}, bf16[96,1536]{1,0:T(8,128)(2,1)S(1)}, u32[]{:S(2)}, u32[]{:S(2)}) collective-permute-start(bf16[96,1536]{1,0:T(8,128)(2,1)S(1)} %get-tuple-element.510.refs_1_), channel_id=1, source_target_pairs={{0,8},{8,0},{16,24},{24,16},{1,9},{9,1},{17,25},{25,17},{2,10},{10... | collective-permute-start | bytes 884744 | tf_op jit(solution)/shard_map/ppermute | solution.py:934
  455.7 18.9 %collective-permute-start.78 = (bf16[192,768]{1,0:T(8,128)(2,1)S(1)}, bf16[192,768]{1,0:T(8,128)(2,1)S(1)}, u32[]{:S(2)}, u32[]{:S(2)}) collective-permute-start(bf16[192,768]{1,0:T(8,128)(2,1)S(1)} %get-tuple-element.517.refs_1_), channel_id=1, source_target_pairs={{0,4},{2,6},{4,0},{6,2},{1,5},{3,7},{5,1},{7,3},{8,12},{10,14},{12... | collective-permute-start | bytes 884744 | tf_op jit(solution)/shard_map/ppermute | solution.py:934
  457.2 17.4 %collective-permute-start.79 = (bf16[192,768]{1,0:T(8,128)(2,1)S(1)}, bf16[192,768]{1,0:T(8,128)(2,1)S(1)}, u32[]{:S(2)}, u32[]{:S(2)}) collective-permute-start(bf16[192,768]{1,0:T(8,128)(2,1)S(1)} %get-tuple-element.518.refs_3_), channel_id=1, source_target_pairs={{0,2},{2,0},{4,6},{6,4},{1,3},{3,1},{5,7},{7,5},{8,10},{10,8},{12,... | collective-permute-start | bytes 884744 | tf_op jit(solution)/shard_map/ppermute | solution.py:934
  475.0 9.9 %collective-permute-start.80 = (bf16[384,768]{1,0:T(8,128)(2,1)S(1)}, bf16[384,768]{1,0:T(8,128)(2,1)S(1)}, u32[]{:S(2)}, u32[]{:S(2)}) collective-permute-start(bf16[384,768]{1,0:T(8,128)(2,1)S(1)} %get-tuple-element.520.refs_1_), channel_id=1, source_target_pairs={{0,2},{2,0},{4,6},{6,4},{1,3},{3,1},{5,7},{7,5},{8,10},{10,8},{12,... | collective-permute-start | bytes 1769480 | tf_op jit(solution)/shard_map/ppermute | solution.py:934
  476.8 9.9 %collective-permute-start.81 = (bf16[384,768]{1,0:T(8,128)(2,1)S(1)}, bf16[384,768]{1,0:T(8,128)(2,1)S(1)}, u32[]{:S(2)}, u32[]{:S(2)}) collective-permute-start(bf16[384,768]{1,0:T(8,128)(2,1)S(1)} %get-tuple-element.521.refs_3_), channel_id=1, source_target_pairs={{0,4},{2,6},{4,0},{6,2},{1,5},{3,7},{5,1},{7,3},{8,12},{10,14},{12... | collective-permute-start | bytes 1769480 | tf_op jit(solution)/shard_map/ppermute | solution.py:934
  (38 other events, 212.0 us)
